TPU v7x, 32 devices: a whole 2x2x4 slice. The times are simulated.
32 devices in a mesh: expert: 4 (over z), context: 2 (over y), dp: 4 (over x, core).
Axes of the slice: x: 2, y: 2, z: 4, core: 2. Of those that a mesh axis runs over, the one named last changes fastest.
Arguments:
- prompt_in: bfloat16 [16, 128, 2048], P(('expert', 'dp'), 'context'), may hold values from -6 to 6
- cont_in: bfloat16 [16, 2, 128, 2048], P(('expert', 'dp'), 'context'), may hold values from -6 to 6
- prompt_cot: bfloat16 [16, 128, 2048], P(('expert', 'dp'), 'context'), may hold values from -6 to 6
- cont_cot: bfloat16 [16, 2, 128, 2048], P(('expert', 'dp'), 'context'), may hold values from -6 to 6
- prompt_routes: int32 [16, 128, 8], P(('expert', 'dp'), 'context'), may hold values from 0 to 15, all different within a row; in each aligned block of 64 rows (0 to 63, 64 to 127, ..., all dimensions but the last counted through in order) at most 36 rows name the same one
- cont_routes: int32 [16, 2, 128, 8], P(('expert', 'dp'), 'context'), may hold values from 0 to 15, all different within a row; in each aligned block of 128 rows (0 to 127, 128 to 255, ..., all dimensions but the last counted through in order) at most 72 rows name the same one
- prefix: int32 [16, 2], P(('expert', 'dp'), 'context'), may hold values from 1 to 128, as said below
- attn_gain: bfloat16 [2048], P('context'), may hold values from 0.099609375 to 1.8984375
- query_gain: bfloat16 [2048], P('context'), may hold values from 0.099609375 to 1.8984375
- key_gain: bfloat16 [2048], P('context'), may hold values from 0.099609375 to 1.8984375
- ffn_gain: bfloat16 [2048], P('context'), may hold values from 0.099609375 to 1.8984375
- w_query: bfloat16 [2048, 2048], P('context'), may hold values from -0.125 to 0.125
- w_key: bfloat16 [2048, 2048], P('context'), may hold values from -0.125 to 0.125
- w_value: bfloat16 [2048, 2048], P('context'), may hold values from -0.125 to 0.125
- w_output: bfloat16 [2048, 2048], P('context'), may hold values from -1 to 1
- w_router: bfloat16 [2048, 16], P('context'), may hold values from -0.0625 to 0.0625
- expert_gate: bfloat16 [16, 1024, 2048], P(('expert', 'dp')), may hold values from -0.125 to 0.125
- expert_up: bfloat16 [16, 1024, 2048], P(('expert', 'dp')), may hold values from -0.125 to 0.125
- expert_down: bfloat16 [16, 1024, 2048], P(('expert', 'dp')), may hold values from -0.375 to 0.375
Outputs:
- prompt_out: bfloat16 [16, 128, 2048], P(('expert', 'dp'), 'context')
- cont_out: bfloat16 [16, 2, 128, 2048], P(('expert', 'dp'), 'context')
- prompt_grad: float32 [16, 128, 2048], P(('expert', 'dp'), 'context')
- cont_grad: float32 [16, 2, 128, 2048], P(('expert', 'dp'), 'context')
- attn_gain_grad: float32 [2048], P(('expert', 'context', 'dp'))
- query_gain_grad: float32 [2048], P(('expert', 'context', 'dp'))
- key_gain_grad: float32 [2048], P(('expert', 'context', 'dp'))
- ffn_gain_grad: float32 [2048], P(('expert', 'context', 'dp'))
- query_grad: float32 [2048, 2048], P(('expert', 'context', 'dp'))
- key_grad: float32 [2048, 2048], P(('expert', 'context', 'dp'))
- value_grad: float32 [2048, 2048], P(('expert', 'context', 'dp'))
- output_grad: float32 [2048, 2048], P(('expert', 'context', 'dp'))
- router_grad: float32 [2048, 16], P(('expert', 'context', 'dp'))
- gate_grad: float32 [16, 1024, 2048], P(('expert', 'dp'), 'context')
- up_grad: float32 [16, 1024, 2048], P(('expert', 'dp'), 'context')
- down_grad: float32 [16, 1024, 2048], P(('expert', 'dp'), 'context')
Inputs may be any that keep to these rules, and one draw needn't show every extreme that they name: `prompt_routes`: each token names 8 different experts; among the prompt tokens of one device no expert is named more than 36 times, and some expert exactly that often. `cont_routes`: each token names 8 different experts; among the continuation tokens of one device no expert is named more than 72 times, and some expert exactly that often. `prefix`: in every group one continuation follows the whole prompt.
All inputs are finite; a program needn't handle non-finite values.
Results may differ from a plain program's by a relative error of at most 0.02.
Values may be sent and summed in bfloat16 or wider, within the bound.
No kernel may reach another device: no remote copies, remote signals or barrier semaphores. Data moves between devices by JAX's collectives and lax.ppermute only.
A program may use at most 320 MiB of HBM per device.

v0:
```python
import jax
import jax.numpy as jnp
from jax import lax
from jax.sharding import PartitionSpec as P

HEADS = 16


EPSILON = 1e-05
NEG_LARGE = -1e30


def rms_scale(values, gain_row):
    inverse = lax.rsqrt(jnp.mean(values * values, axis=-1, keepdims=True) + EPSILON)
    return values * inverse * gain_row


def angle_table(positions, head_dim):
    half_index = jnp.arange(head_dim // 2, dtype=jnp.float32)
    frequency = 10000.0 ** (-2.0 * half_index / head_dim)
    return positions.astype(jnp.float32)[:, None] * frequency[None, :]


def rotate(values, angles, head_count):
    row_count = values.shape[0]
    shaped = values.reshape(row_count, head_count, -1)
    half_size = shaped.shape[-1] // 2
    first_half = shaped[..., :half_size]
    second = shaped[..., half_size:]
    cosine = jnp.cos(angles)[:, None, :]
    sine_part = jnp.sin(angles)[:, None, :]
    turned = jnp.concatenate(
        [first_half * cosine - second * sine_part, second * cosine + first_half * sine_part],
        axis=-1,
    )
    return turned.reshape(row_count, -1)


def qk_post(raw_rows, gain_row, angles, head_count):
    return rotate(rms_scale(raw_rows, gain_row), angles, head_count)


def build_mask(prompt_pos, start_len, prompt_total, cont_len):
    key_prompt = jnp.arange(prompt_total, dtype=jnp.int32)[None, :]
    prompt_rows = jnp.concatenate(
        [
            key_prompt <= prompt_pos[:, None],
            jnp.zeros((prompt_pos.shape[0], cont_len), dtype=jnp.bool_),
        ],
        axis=1,
    )
    own_index = jnp.arange(cont_len, dtype=jnp.int32)
    cont_rows = jnp.concatenate(
        [
            jnp.broadcast_to(key_prompt < start_len, (cont_len, prompt_total)),
            own_index[None, :] <= own_index[:, None],
        ],
        axis=1,
    )
    return jnp.concatenate([prompt_rows, cont_rows], axis=0)


def head_scores(queries, key_set, read_mask, head_count):
    q_heads = queries.reshape(queries.shape[0], head_count, -1)
    k_heads = key_set.reshape(key_set.shape[0], head_count, -1)
    raw_scores = jnp.einsum("qhd,khd->hqk", q_heads, k_heads, preferred_element_type=jnp.float32)
    return jnp.where(read_mask[None], raw_scores * q_heads.shape[-1] ** (-0.5), NEG_LARGE)


def shards(
    prompt_in,
    cont_in,
    prompt_cot,
    cont_cot,
    prompt_routes,
    cont_routes,
    prefix,
    attn_gain,
    query_gain,
    key_gain,
    ffn_gain,
    w_query,
    w_key,
    w_value,
    w_output,
    w_router,
    expert_gate,
    expert_up,
    expert_down,
):
    prompt_dev = prompt_in.shape[1]
    cont_len = cont_in.shape[2]
    tok_dev = prompt_dev + cont_len
    model_width = prompt_in.shape[2]
    head_dim = model_width // HEADS
    top_count = prompt_routes.shape[2]
    expert_count = w_router.shape[1]
    context_size = lax.axis_size("context")
    context_index = lax.axis_index("context")
    prompt_total = prompt_dev * context_size
    most_prompt = 9 * prompt_dev * top_count // (8 * expert_count)
    most_cont = 9 * cont_len * top_count // (8 * expert_count)
    slot_count = most_prompt + most_cont
    gathered = (
        lax.all_gather(attn_gain, "context", axis=0, tiled=True),
        lax.all_gather(query_gain, "context", axis=0, tiled=True),
        lax.all_gather(key_gain, "context", axis=0, tiled=True),
        lax.all_gather(ffn_gain, "context", axis=0, tiled=True),
        lax.all_gather(w_query, "context", axis=0, tiled=True),
        lax.all_gather(w_key, "context", axis=0, tiled=True),
        lax.all_gather(w_value, "context", axis=0, tiled=True),
        lax.all_gather(w_output, "context", axis=0, tiled=True),
        lax.all_gather(w_router, "context", axis=0, tiled=True),
    )
    gain_attn = gathered[0].astype(jnp.float32)
    gain_query = gathered[1].astype(jnp.float32)
    gain_key = gathered[2].astype(jnp.float32)
    gain_ffn = gathered[3].astype(jnp.float32)
    full_query, full_key, full_value, full_output, full_router = (
        gathered[4],
        gathered[5],
        gathered[6],
        gathered[7],
        gathered[8],
    )
    x_rows = jnp.concatenate([prompt_in[0], cont_in[0, 0]], axis=0).astype(jnp.float32)
    d_out = jnp.concatenate([prompt_cot[0], cont_cot[0, 0]], axis=0).astype(jnp.float32)
    routes = jnp.concatenate([prompt_routes[0], cont_routes[0, 0]], axis=0)
    start_len = prefix[0, 0]
    prompt_pos = context_index * prompt_dev + jnp.arange(prompt_dev, dtype=jnp.int32)
    positions = jnp.concatenate([prompt_pos, start_len + jnp.arange(cont_len, dtype=jnp.int32)])
    angles = angle_table(positions, head_dim)
    normed_low = rms_scale(x_rows, gain_attn).astype(jnp.bfloat16)
    query_raw = jnp.dot(normed_low, full_query, preferred_element_type=jnp.float32)
    key_raw = jnp.dot(normed_low, full_key, preferred_element_type=jnp.float32)
    value_low = jnp.dot(normed_low, full_value, preferred_element_type=jnp.float32).astype(
        jnp.bfloat16
    )
    query_low = qk_post(query_raw, gain_query, angles, HEADS).astype(jnp.bfloat16)
    key_low = qk_post(key_raw, gain_key, angles, HEADS).astype(jnp.bfloat16)
    prompt_keys, prompt_values = (
        lax.all_gather(key_low[:prompt_dev], "context", axis=0, tiled=True),
        lax.all_gather(value_low[:prompt_dev], "context", axis=0, tiled=True),
    )
    key_set = jnp.concatenate([prompt_keys, key_low[prompt_dev:]], axis=0)
    value_set = jnp.concatenate([prompt_values, value_low[prompt_dev:]], axis=0)
    read_mask = build_mask(prompt_pos, start_len, prompt_total, cont_len)
    scores = head_scores(query_low, key_set, read_mask, HEADS)
    top_score = jnp.max(scores, axis=-1, keepdims=True)
    exponent = jnp.exp(scores - top_score)
    row_total = jnp.sum(exponent, axis=-1, keepdims=True)
    weights = (exponent / row_total).astype(jnp.bfloat16)
    value_heads = value_set.reshape(value_set.shape[0], HEADS, head_dim)
    attended = (
        jnp.einsum("hqk,khd->qhd", weights, value_heads, preferred_element_type=jnp.float32)
        .reshape(tok_dev, model_width)
        .astype(jnp.bfloat16)
    )
    mixed_rows = x_rows + jnp.dot(attended, full_output, preferred_element_type=jnp.float32)
    normed2_low = rms_scale(mixed_rows, gain_ffn).astype(jnp.bfloat16)
    logits = jnp.dot(normed2_low, full_router, preferred_element_type=jnp.float32)
    shifted = jnp.exp(logits - jnp.max(logits, axis=1, keepdims=True))
    router_probs = shifted / jnp.sum(shifted, axis=1, keepdims=True)
    expert_ids = jnp.arange(expert_count, dtype=jnp.int32)
    route_hits = (routes[:, :, None] == expert_ids[None, None, :]).astype(jnp.float32)
    member = jnp.sum(route_hits, axis=1)
    member_prompt = member[:prompt_dev]
    member_cont = member[prompt_dev:]
    slot_rank = jnp.concatenate(
        [
            jnp.cumsum(member_prompt, axis=0) - member_prompt,
            jnp.cumsum(member_cont, axis=0) - member_cont + most_prompt,
        ],
        axis=0,
    )
    slot_index = jnp.take_along_axis(slot_rank, routes, axis=1).astype(jnp.int32)
    flat_slot = routes * slot_count + slot_index
    token_ids = jnp.broadcast_to(jnp.arange(tok_dev, dtype=jnp.int32)[:, None], routes.shape)
    slot_owner = (
        jnp.full((expert_count * slot_count,), tok_dev, dtype=jnp.int32)
        .at[flat_slot.reshape(-1)]
        .set(token_ids.reshape(-1))
    )
    padded_in = jnp.concatenate([normed2_low, jnp.zeros((1, model_width), jnp.bfloat16)], axis=0)
    outgoing = padded_in[slot_owner].reshape(expert_count, slot_count, model_width)
    slot_items = lax.all_to_all(outgoing, ("expert", "dp"), split_axis=0, concat_axis=0, tiled=True)
    flat_in = slot_items.reshape(-1, model_width)
    gate_pre = jnp.einsum("rd,fd->rf", flat_in, expert_gate[0], preferred_element_type=jnp.float32)
    up_pre = jnp.einsum("rd,fd->rf", flat_in, expert_up[0], preferred_element_type=jnp.float32)
    expert_act_low = (gate_pre * jax.nn.sigmoid(gate_pre) * up_pre).astype(jnp.bfloat16)
    result = (
        jnp.dot(expert_act_low, expert_down[0], preferred_element_type=jnp.float32)
        .astype(jnp.bfloat16)
        .reshape(slot_items.shape)
    )
    sent_back = lax.all_to_all(result, ("expert", "dp"), split_axis=0, concat_axis=0, tiled=True)
    gate_kept = gate_pre.reshape(slot_items.shape[0], slot_items.shape[1], -1)
    up_kept = up_pre.reshape(slot_items.shape[0], slot_items.shape[1], -1)
    picked = sent_back.reshape(-1, model_width)[flat_slot].astype(jnp.float32)
    gate_values = jnp.take_along_axis(router_probs, routes, axis=1)
    out_rows = mixed_rows + jnp.sum(gate_values[:, :, None] * picked, axis=1)
    probs_padded = jnp.concatenate(
        [router_probs, jnp.zeros((1, expert_count), jnp.float32)], axis=0
    )
    slot_expert = jnp.arange(expert_count * slot_count, dtype=jnp.int32) // slot_count
    slot_gate = probs_padded[slot_owner, slot_expert]
    cot_padded = jnp.concatenate([d_out, jnp.zeros((1, model_width), jnp.float32)], axis=0)
    grad_outgoing = (
        (slot_gate[:, None] * cot_padded[slot_owner])
        .astype(jnp.bfloat16)
        .reshape(expert_count, slot_count, model_width)
    )
    grad_received = lax.all_to_all(
        grad_outgoing, ("expert", "dp"), split_axis=0, concat_axis=0, tiled=True
    )
    grad_flat = grad_received.reshape(-1, model_width)
    gate_flat = gate_kept.reshape(grad_flat.shape[0], -1)
    up_flat = up_kept.reshape(grad_flat.shape[0], -1)
    input_flat = slot_items.reshape(-1, model_width)
    sigmoid_gate = jax.nn.sigmoid(gate_flat)
    silu_gate = gate_flat * sigmoid_gate
    act_low = (silu_gate * up_flat).astype(jnp.bfloat16)
    d_act = jnp.einsum("rd,fd->rf", grad_flat, expert_down[0], preferred_element_type=jnp.float32)
    d_gate = (d_act * up_flat * (sigmoid_gate * (1.0 + gate_flat * (1.0 - sigmoid_gate)))).astype(
        jnp.bfloat16
    )
    d_up = (d_act * silu_gate).astype(jnp.bfloat16)
    d_input = (
        jnp.dot(d_gate, expert_gate[0], preferred_element_type=jnp.float32)
        + jnp.dot(d_up, expert_up[0], preferred_element_type=jnp.float32)
    ).astype(jnp.bfloat16)
    grad_returned = lax.all_to_all(
        d_input.reshape(grad_received.shape),
        ("expert", "dp"),
        split_axis=0,
        concat_axis=0,
        tiled=True,
    )
    expert_sums = lax.psum_scatter(
        jnp.concatenate(
            [
                jnp.einsum("rf,rd->fd", d_gate, input_flat, preferred_element_type=jnp.float32),
                jnp.einsum("rf,rd->fd", d_up, input_flat, preferred_element_type=jnp.float32),
                jnp.einsum("rf,rd->fd", act_low, grad_flat, preferred_element_type=jnp.float32),
            ],
            axis=1,
        ).astype(jnp.bfloat16),
        "context",
        scatter_dimension=0,
        tiled=True,
    ).astype(jnp.float32)
    dprob_routes = jnp.sum(d_out[:, None, :] * picked, axis=2)
    dprobs = jnp.sum(dprob_routes[:, :, None] * route_hits, axis=1)
    dlogit_low = (
        router_probs * (dprobs - jnp.sum(router_probs * dprobs, axis=1, keepdims=True))
    ).astype(jnp.bfloat16)
    router_grad = jnp.einsum(
        "td,te->de", normed2_low, dlogit_low, preferred_element_type=jnp.float32
    )
    d_normed2 = jnp.sum(
        grad_returned.reshape(-1, model_width)[flat_slot].astype(jnp.float32), axis=1
    ) + jnp.einsum("te,de->td", dlogit_low, full_router, preferred_element_type=jnp.float32)
    _, ffn_back = jax.vjp(rms_scale, mixed_rows, gain_ffn)
    d_mixed_norm, ffn_gain_grad = ffn_back(d_normed2)
    d_mixed = d_out + d_mixed_norm
    branch_low = d_mixed.astype(jnp.bfloat16)
    output_grad = jnp.einsum("tc,td->cd", attended, branch_low, preferred_element_type=jnp.float32)
    d_attended = jnp.einsum(
        "td,cd->tc", branch_low, full_output, preferred_element_type=jnp.float32
    ).astype(jnp.bfloat16)
    again_keys, again_values = (
        lax.all_gather(key_low[:prompt_dev], "context", axis=0, tiled=True),
        lax.all_gather(value_low[:prompt_dev], "context", axis=0, tiled=True),
    )
    key_back = jnp.concatenate([again_keys, key_low[prompt_dev:]], axis=0)
    value_back = jnp.concatenate([again_values, value_low[prompt_dev:]], axis=0)
    scores_back = head_scores(query_low, key_back, read_mask, HEADS)
    probs_back = jnp.exp(scores_back - top_score) / row_total
    weights_back = probs_back.astype(jnp.bfloat16)
    d_heads = d_attended.reshape(tok_dev, HEADS, head_dim)
    d_probs = jnp.einsum(
        "qhd,khd->hqk",
        d_heads,
        value_back.reshape(value_back.shape[0], HEADS, head_dim),
        preferred_element_type=jnp.float32,
    )
    d_scores = (
        probs_back
        * (d_probs - jnp.sum(probs_back * d_probs, axis=-1, keepdims=True))
        * head_dim ** (-0.5)
    ).astype(jnp.bfloat16)
    d_queries = jnp.einsum(
        "hqk,khd->qhd",
        d_scores,
        key_back.reshape(key_back.shape[0], HEADS, head_dim),
        preferred_element_type=jnp.float32,
    ).reshape(tok_dev, model_width)
    d_keys_all = jnp.einsum(
        "hqk,qhd->khd",
        d_scores,
        query_low.reshape(tok_dev, HEADS, head_dim),
        preferred_element_type=jnp.float32,
    ).reshape(-1, model_width)
    d_values_all = jnp.einsum(
        "hqk,qhd->khd", weights_back, d_heads, preferred_element_type=jnp.float32
    ).reshape(-1, model_width)
    d_prompt_keys, d_prompt_values = (
        lax.psum_scatter(
            d_keys_all[:prompt_total].astype(jnp.bfloat16),
            "context",
            scatter_dimension=0,
            tiled=True,
        ).astype(jnp.float32),
        lax.psum_scatter(
            d_values_all[:prompt_total].astype(jnp.bfloat16),
            "context",
            scatter_dimension=0,
            tiled=True,
        ).astype(jnp.float32),
    )
    d_keys = jnp.concatenate([d_prompt_keys, d_keys_all[prompt_total:]], axis=0)
    d_values = jnp.concatenate([d_prompt_values, d_values_all[prompt_total:]], axis=0)

    def query_side(raw_rows, gain_row):
        return qk_post(raw_rows, gain_row, angles, HEADS)

    _, query_back = jax.vjp(query_side, query_raw, gain_query)
    d_query_raw, query_gain_grad = query_back(d_queries)
    _, key_back_fn = jax.vjp(query_side, key_raw, gain_key)
    d_key_raw, key_gain_grad = key_back_fn(d_keys)
    d_query_low = d_query_raw.astype(jnp.bfloat16)
    d_key_low = d_key_raw.astype(jnp.bfloat16)
    d_value_low = d_values.astype(jnp.bfloat16)
    query_grad = jnp.einsum(
        "tc,td->cd", normed_low, d_query_low, preferred_element_type=jnp.float32
    )
    key_grad = jnp.einsum("tc,td->cd", normed_low, d_key_low, preferred_element_type=jnp.float32)
    value_grad = jnp.einsum(
        "tc,td->cd", normed_low, d_value_low, preferred_element_type=jnp.float32
    )
    d_normed = (
        jnp.einsum("td,cd->tc", d_query_low, full_query, preferred_element_type=jnp.float32)
        + jnp.einsum("td,cd->tc", d_key_low, full_key, preferred_element_type=jnp.float32)
        + jnp.einsum("td,cd->tc", d_value_low, full_value, preferred_element_type=jnp.float32)
    )
    _, attn_back = jax.vjp(rms_scale, x_rows, gain_attn)
    d_x_norm, attn_gain_grad = attn_back(d_normed)
    d_x = d_mixed + d_x_norm
    first_section = (
        lax.psum_scatter(
            attn_gain_grad.astype(jnp.bfloat16), "expert", scatter_dimension=0, tiled=True
        ).astype(jnp.float32),
        lax.psum_scatter(
            query_gain_grad.astype(jnp.bfloat16), "expert", scatter_dimension=0, tiled=True
        ).astype(jnp.float32),
        lax.psum_scatter(
            key_gain_grad.astype(jnp.bfloat16), "expert", scatter_dimension=0, tiled=True
        ).astype(jnp.float32),
        lax.psum_scatter(
            ffn_gain_grad.astype(jnp.bfloat16), "expert", scatter_dimension=0, tiled=True
        ).astype(jnp.float32),
        lax.psum_scatter(
            query_grad.astype(jnp.bfloat16), "expert", scatter_dimension=0, tiled=True
        ).astype(jnp.float32),
        lax.psum_scatter(
            key_grad.astype(jnp.bfloat16), "expert", scatter_dimension=0, tiled=True
        ).astype(jnp.float32),
        lax.psum_scatter(
            value_grad.astype(jnp.bfloat16), "expert", scatter_dimension=0, tiled=True
        ).astype(jnp.float32),
        lax.psum_scatter(
            output_grad.astype(jnp.bfloat16), "expert", scatter_dimension=0, tiled=True
        ).astype(jnp.float32),
        lax.psum_scatter(
            router_grad.astype(jnp.bfloat16), "expert", scatter_dimension=0, tiled=True
        ).astype(jnp.float32),
    )
    reduced = (
        lax.psum_scatter(
            first_section[0].astype(jnp.bfloat16),
            ("context", "dp"),
            scatter_dimension=0,
            tiled=True,
        ).astype(jnp.float32),
        lax.psum_scatter(
            first_section[1].astype(jnp.bfloat16),
            ("context", "dp"),
            scatter_dimension=0,
            tiled=True,
        ).astype(jnp.float32),
        lax.psum_scatter(
            first_section[2].astype(jnp.bfloat16),
            ("context", "dp"),
            scatter_dimension=0,
            tiled=True,
        ).astype(jnp.float32),
        lax.psum_scatter(
            first_section[3].astype(jnp.bfloat16),
            ("context", "dp"),
            scatter_dimension=0,
            tiled=True,
        ).astype(jnp.float32),
        lax.psum_scatter(
            first_section[4].astype(jnp.bfloat16),
            ("context", "dp"),
            scatter_dimension=0,
            tiled=True,
        ).astype(jnp.float32),
        lax.psum_scatter(
            first_section[5].astype(jnp.bfloat16),
            ("context", "dp"),
            scatter_dimension=0,
            tiled=True,
        ).astype(jnp.float32),
        lax.psum_scatter(
            first_section[6].astype(jnp.bfloat16),
            ("context", "dp"),
            scatter_dimension=0,
            tiled=True,
        ).astype(jnp.float32),
        lax.psum_scatter(
            first_section[7].astype(jnp.bfloat16),
            ("context", "dp"),
            scatter_dimension=0,
            tiled=True,
        ).astype(jnp.float32),
        lax.psum_scatter(
            first_section[8].astype(jnp.bfloat16),
            ("context", "dp"),
            scatter_dimension=0,
            tiled=True,
        ).astype(jnp.float32),
    )
    gate_grad = expert_sums[:, :model_width][None]
    up_grad = expert_sums[:, model_width : 2 * model_width][None]
    down_grad = expert_sums[:, 2 * model_width :][None]
    return (
        out_rows[:prompt_dev].astype(jnp.bfloat16)[None],
        out_rows[prompt_dev:].astype(jnp.bfloat16)[None, None],
        d_x[:prompt_dev][None],
        d_x[prompt_dev:][None, None],
        reduced[0],
        reduced[1],
        reduced[2],
        reduced[3],
        reduced[4],
        reduced[5],
        reduced[6],
        reduced[7],
        reduced[8],
        gate_grad,
        up_grad,
        down_grad,
    )


def solution(mesh):
    in_specs = (
        P(("expert", "dp"), "context", None),
        P(("expert", "dp"), "context", None, None),
        P(("expert", "dp"), "context", None),
        P(("expert", "dp"), "context", None, None),
        P(("expert", "dp"), "context", None),
        P(("expert", "dp"), "context", None, None),
        P(("expert", "dp"), "context"),
        P("context"),
        P("context"),
        P("context"),
        P("context"),
        P("context", None),
        P("context", None),
        P("context", None),
        P("context", None),
        P("context", None),
        P(("expert", "dp"), None, None),
        P(("expert", "dp"), None, None),
        P(("expert", "dp"), None, None),
    )
    out_specs = (
        P(("expert", "dp"), "context", None),
        P(("expert", "dp"), "context", None, None),
        P(("expert", "dp"), "context", None),
        P(("expert", "dp"), "context", None, None),
        P(("expert", "context", "dp")),
        P(("expert", "context", "dp")),
        P(("expert", "context", "dp")),
        P(("expert", "context", "dp")),
        P(("expert", "context", "dp"), None),
        P(("expert", "context", "dp"), None),
        P(("expert", "context", "dp"), None),
        P(("expert", "context", "dp"), None),
        P(("expert", "context", "dp"), None),
        P(("expert", "dp"), "context", None),
        P(("expert", "dp"), "context", None),
        P(("expert", "dp"), "context", None),
    )
    return jax.shard_map(shards, mesh=mesh, in_specs=in_specs, out_specs=out_specs, check_vma=False)
```

profile of v0, /device:TPU:0, one launch (start us, length us, event | category | flops | bytes accessed | tf_op | source)
XLA Modules:
  0.0 2249.7 jit_solution(3720993805051845149)
XLA Ops:
  52.0 64.3 %all-gather.5.cloned.1.call-done = bf16[2048,2048]{1,0:T(8,128)(2,1)} async-done(((bf16[1024,2048]{1,0:T(8,128)(2,1)}), bf16[2048,2048]{1,0:T(8,128)(2,1)}) %all-gather.5.cloned.1.call-update) | async-done | bytes 8388624 | tf_op jit(solution)/shard_map/all_gather | solution.py:111
  122.3 99.6 %all-gather.9.cloned.1.call-done = bf16[2048,2048]{1,0:T(8,128)(2,1)} async-done(((bf16[1024,2048]{1,0:T(8,128)(2,1)}), bf16[2048,2048]{1,0:T(8,128)(2,1)}) %all-gather.9.cloned.1.call-update) | async-done | bytes 8388624 | tf_op jit(solution)/shard_map/all_gather | solution.py:110
  228.7 98.8 %all-gather.7.cloned.1.call-done = bf16[2048,2048]{1,0:T(8,128)(2,1)} async-done(((bf16[1024,2048]{1,0:T(8,128)(2,1)}), bf16[2048,2048]{1,0:T(8,128)(2,1)}) %all-gather.7.cloned.1.call-update) | async-done | bytes 8388624 | tf_op jit(solution)/shard_map/all_gather | solution.py:109
  342.5 15.2 all_gather.42
  359.1 15.1 all_gather.37
  381.8 62.4 %all-gather.11.cloned.1.call-done = bf16[2048,2048]{1,0:T(8,128)(2,1)} async-done(((bf16[1024,2048]{1,0:T(8,128)(2,1)}), bf16[2048,2048]{1,0:T(8,128)(2,1)}) %all-gather.11.cloned.1.call-update) | async-done | bytes 8388624 | tf_op jit(solution)/shard_map/all_gather | solution.py:112
  502.6 13.6 gather_fusion.2
  525.3 80.5 %all-to-all-done = bf16[16,108,2048]{2,1,0:T(8,128)(2,1)} async-done(((bf16[16,108,2048]{2,1,0:T(8,128)(2,1)}), bf16[16,108,2048]{2,1,0:T(8,128)(2,1)}, u32[]{:S(2)}, u32[]{:S(2)}) %all-to-all-start) | async-done | bytes 7077920 | tf_op jit(solution)/shard_map/all_to_all | solution.py:186
  605.8 32.8 %all-to-all-start.2 = ((bf16[16,108,2048]{2,1,0:T(8,128)(2,1)}), bf16[16,108,2048]{2,1,0:T(8,128)(2,1)}, u32[]{:S(2)}, u32[]{:S(2)}) async-start(bf16[16,108,2048]{2,1,0:T(8,128)(2,1)} %multiply_convert_fusion), calls=%async_computation.2 | async-start | bytes 14680064 | tf_op jit(solution)/shard_map/all_to_all | solution.py:213
  647.3 13.0 fusion.13
  670.2 100.9 %all-to-all-done.2 = bf16[16,108,2048]{2,1,0:T(8,128)(2,1)} async-done(((bf16[16,108,2048]{2,1,0:T(8,128)(2,1)}), bf16[16,108,2048]{2,1,0:T(8,128)(2,1)}, u32[]{:S(2)}, u32[]{:S(2)}) %all-to-all-start.2) | async-done | bytes 7077920 | tf_op jit(solution)/shard_map/all_to_all | solution.py:213
  779.8 19.1 multiply_convert_fusion.1
  818.6 32.3 %all-to-all-start.1 = ((bf16[16,108,2048]{2,1,0:T(8,128)(2,1)}), bf16[16,108,2048]{2,1,0:T(8,128)(2,1)}, u32[]{:S(2)}, u32[]{:S(2)}) async-start(bf16[16,108,2048]{2,1,0:T(8,128)(2,1)} %reshape.384), calls=%async_computation.1 | async-start | bytes 14680064 | tf_op jit(solution)/shard_map/all_to_all | solution.py:196
  884.4 99.0 %all-to-all-done.1 = bf16[16,108,2048]{2,1,0:T(8,128)(2,1)} async-done(((bf16[16,108,2048]{2,1,0:T(8,128)(2,1)}), bf16[16,108,2048]{2,1,0:T(8,128)(2,1)}, u32[]{:S(2)}, u32[]{:S(2)}) %all-to-all-start.1) | async-done | bytes 7077920 | tf_op jit(solution)/shard_map/all_to_all | solution.py:196
  983.4 32.3 %all-to-all-start.3 = ((bf16[16,108,2048]{2,1,0:T(8,128)(2,1)}), bf16[16,108,2048]{2,1,0:T(8,128)(2,1)}, u32[]{:S(2)}, u32[]{:S(2)}) async-start(bf16[16,108,2048]{2,1,0:T(8,128)(2,1)} %reshape.387), calls=%async_computation.3 | async-start | bytes 14680064 | tf_op jit(solution)/shard_map/all_to_all | solution.py:232
  1016.3 12.7 gather_fusion.5
  1038.1 16.8 gather_fusion.1
  1061.6 86.6 %all-to-all-done.3 = bf16[16,108,2048]{2,1,0:T(8,128)(2,1)} async-done(((bf16[16,108,2048]{2,1,0:T(8,128)(2,1)}), bf16[16,108,2048]{2,1,0:T(8,128)(2,1)}, u32[]{:S(2)}, u32[]{:S(2)}) %all-to-all-start.3) | async-done | bytes 7077920 | tf_op jit(solution)/shard_map/all_to_all | solution.py:232
  1156.8 17.0 gather_fusion.4
  1195.5 24.8 %fusion.27 = f32[256,16,128]{2,0,1:T(8,128)} fusion(f32[16,192,256]{2,1,0:T(8,128)} %fusion.51, bf16[192,16,64]{2,0,1:T(8,128)(2,1)} %get-tuple-element.44, bf16[192,16,64]{2,0,1:T(8,128)(2,1)} %get-tuple-element.43, f32[16,192,256]{2,1,0:T(8,128)} %get-tuple-element.72, f32[16,192]{1,0:T(8,128)S(1)} %copy-done.101), kind=kOutput, calls=%fused_computation.69 | convolution fusion | flops 208407808 | bytes 9187328 | tf_op jit(solution)/shard_map/hqk,qhd->khd/dot_general | solution.py:298
  1242.2 20.8 fusion.45
  1344.3 91.0 %reduce-scatter.32.cloned.1.call-done = bf16[512,2048]{1,0:T(8,128)(2,1)} async-done(((bf16[2048,2048]{1,0:T(8,128)(2,1)}), bf16[512,2048]{1,0:T(8,128)(2,1)}) %reduce-scatter.32.cloned.1.call-update) | async-done | bytes 2097168 | tf_op jit(solution)/shard_map/reduce_scatter | solution.py:371
  1435.3 147.6 %reduce-scatter.28.cloned.1.call-done = bf16[512,2048]{1,0:T(8,128)(2,1)} async-done(((bf16[2048,2048]{1,0:T(8,128)(2,1)}), bf16[512,2048]{1,0:T(8,128)(2,1)}) %reduce-scatter.28.cloned.1.call-update) | async-done | bytes 2097168 | tf_op jit(solution)/shard_map/reduce_scatter | solution.py:368
  1583.0 147.4 %reduce-scatter.24.cloned.1.call-done = bf16[512,2048]{1,0:T(8,128)(2,1)} async-done(((bf16[2048,2048]{1,0:T(8,128)(2,1)}), bf16[512,2048]{1,0:T(8,128)(2,1)}) %reduce-scatter.24.cloned.1.call-update) | async-done | bytes 2097168 | tf_op jit(solution)/shard_map/reduce_scatter | solution.py:365
  1734.6 33.9 %reduce-scatter.44.cloned.1.call-done = bf16[64,16]{1,0:T(8,128)(2,1)} async-done(((bf16[512,16]{1,0:T(8,128)(2,1)}), bf16[64,16]{1,0:T(8,128)(2,1)}) %reduce-scatter.44.cloned.1.call-update) | async-done | bytes 2064
  1784.2 131.0 %reduce-scatter.20.cloned.1.call-done = bf16[512,2048]{1,0:T(8,128)(2,1)} async-done(((bf16[2048,2048]{1,0:T(8,128)(2,1)}), bf16[512,2048]{1,0:T(8,128)(2,1)}) %reduce-scatter.20.cloned.1.call-update) | async-done | bytes 2097168 | tf_op jit(solution)/shard_map/reduce_scatter | solution.py:362
  1923.2 18.1 all-reduce.17
  1960.1 102.8 %reduce-scatter.38.cloned.1.call-done = bf16[512,6144]{1,0:T(8,128)(2,1)} async-done(((bf16[1024,6144]{1,0:T(8,128)(2,1)}), bf16[512,6144]{1,0:T(8,128)(2,1)}) %reduce-scatter.38.cloned.1.call-update) | async-done | bytes 6291472 | tf_op jit(solution)/shard_map/reduce_scatter | solution.py:239
  2082.4 24.9 %reduce-scatter.34.cloned.1.call-done = bf16[64,2048]{1,0:T(8,128)(2,1)} async-done(((bf16[512,2048]{1,0:T(8,128)(2,1)}), bf16[64,2048]{1,0:T(8,128)(2,1)}) %reduce-scatter.34.cloned.1.call-update) | async-done | bytes 262160 | tf_op jit(solution)/shard_map/reduce_scatter | solution.py:421
  2109.1 43.0 %reduce-scatter.30.cloned.1.call-done = bf16[64,2048]{1,0:T(8,128)(2,1)} async-done(((bf16[512,2048]{1,0:T(8,128)(2,1)}), bf16[64,2048]{1,0:T(8,128)(2,1)}) %reduce-scatter.30.cloned.1.call-update) | async-done | bytes 262160 | tf_op jit(solution)/shard_map/reduce_scatter | solution.py:415
  2153.8 42.6 %reduce-scatter.26.cloned.1.call-done = bf16[64,2048]{1,0:T(8,128)(2,1)} async-done(((bf16[512,2048]{1,0:T(8,128)(2,1)}), bf16[64,2048]{1,0:T(8,128)(2,1)}) %reduce-scatter.26.cloned.1.call-update) | async-done | bytes 262160 | tf_op jit(solution)/shard_map/reduce_scatter | solution.py:409
  2198.2 43.0 %reduce-scatter.22.cloned.1.call-done = bf16[64,2048]{1,0:T(8,128)(2,1)} async-done(((bf16[512,2048]{1,0:T(8,128)(2,1)}), bf16[64,2048]{1,0:T(8,128)(2,1)}) %reduce-scatter.22.cloned.1.call-update) | async-done | bytes 262160 | tf_op jit(solution)/shard_map/reduce_scatter | solution.py:403
  (422 shorter events, 449.0 us)
Async XLA Ops:
  7.2 109.2 %all-gather.5.cloned.1.call-start = ((), (), s32[]{:S(2)}) async-start(), calls=%async_computation.17 | async-start | bytes 12582912 | tf_op jit(solution)/shard_map/all_gather | solution.py:111
  7.9 214.0 %all-gather.9.cloned.1.call-start = ((), (), s32[]{:S(2)}) async-start(), calls=%async_computation.19 | async-start | bytes 12582912 | tf_op jit(solution)/shard_map/all_gather | solution.py:110
  8.7 318.9 %all-gather.7.cloned.1.call-start = ((), (), s32[]{:S(2)}) async-start(), calls=%async_computation.18 | async-start | bytes 12582912 | tf_op jit(solution)/shard_map/all_gather | solution.py:109
  9.5 434.7 %all-gather.11.cloned.1.call-start = ((), (), s32[]{:S(2)}) async-start(), calls=%async_computation.20 | async-start | bytes 12582912 | tf_op jit(solution)/shard_map/all_gather | solution.py:112
  15.5 312.0 %copy-start.41 = (f32[2048]{0:T(1024)}, f32[2048]{0:T(1024)S(1)}, u32[]{:S(2)}) copy-start(f32[2048]{0:T(1024)S(1)} %convert_element_type.195) | copy-start | bytes 24580
  19.9 207.4 %copy-start.53 = (f32[2048]{0:T(1024)}, f32[2048]{0:T(1024)S(1)}, u32[]{:S(2)}) copy-start(f32[2048]{0:T(1024)S(1)} %convert_element_type.200) | copy-start | bytes 24580
  24.3 308.6 %copy-start.51 = (f32[2048]{0:T(1024)}, f32[2048]{0:T(1024)S(1)}, u32[]{:S(2)}) copy-start(f32[2048]{0:T(1024)S(1)} %convert_element_type.198) | copy-start | bytes 24580
  29.3 420.3 %copy-start.55 = (f32[2048]{0:T(1024)}, f32[2048]{0:T(1024)S(1)}, u32[]{:S(2)}) copy-start(f32[2048]{0:T(1024)S(1)} %convert_element_type.205) | copy-start | bytes 24580
  51.6 275.9 %copy-start.59 = (f32[192]{0:T(256)}, f32[192]{0:T(256)S(1)}, u32[]{:S(2)}) copy-start(f32[192]{0:T(256)S(1)} %fusion.80) | copy-start | bytes 2308
  52.0 283.6 %copy-start.43 = (f32[192,64]{1,0:T(8,128)}, f32[192,64]{1,0:T(8,128)S(1)}, u32[]{:S(2)}) copy-start(f32[192,64]{1,0:T(8,128)S(1)} %get-tuple-element.65) | copy-start | bytes 147460
  52.0 283.6 %copy-start.45 = (f32[192,64]{1,0:T(8,128)}, f32[192,64]{1,0:T(8,128)S(1)}, u32[]{:S(2)}) copy-start(f32[192,64]{1,0:T(8,128)S(1)} %get-tuple-element.66) | copy-start | bytes 147460
  122.3 256.9 %copy-start.26 = (bf16[128,2048]{1,0:T(8,128)(2,1)}, bf16[128,2048]{1,0:T(8,128)(2,1)S(1)}, u32[]{:S(2)}) copy-start(bf16[128,2048]{1,0:T(8,128)(2,1)S(1)} %slice.127) | copy-start | bytes 1572868
  467.6 138.3 %all-to-all-start = ((bf16[16,108,2048]{2,1,0:T(8,128)(2,1)}), bf16[16,108,2048]{2,1,0:T(8,128)(2,1)}, u32[]{:S(2)}, u32[]{:S(2)}) async-start(bf16[16,108,2048]{2,1,0:T(8,128)(2,1)} %reshape.382), calls=%async_computation | async-start | bytes 14680064 | tf_op jit(solution)/shard_map/all_to_all | solution.py:186
  605.8 165.2 %all-to-all-start.2 = ((bf16[16,108,2048]{2,1,0:T(8,128)(2,1)}), bf16[16,108,2048]{2,1,0:T(8,128)(2,1)}, u32[]{:S(2)}, u32[]{:S(2)}) async-start(bf16[16,108,2048]{2,1,0:T(8,128)(2,1)} %multiply_convert_fusion), calls=%async_computation.2 | async-start | bytes 14680064 | tf_op jit(solution)/shard_map/all_to_all | solution.py:213
  818.6 164.8 %all-to-all-start.1 = ((bf16[16,108,2048]{2,1,0:T(8,128)(2,1)}), bf16[16,108,2048]{2,1,0:T(8,128)(2,1)}, u32[]{:S(2)}, u32[]{:S(2)}) async-start(bf16[16,108,2048]{2,1,0:T(8,128)(2,1)} %reshape.384), calls=%async_computation.1 | async-start | bytes 14680064 | tf_op jit(solution)/shard_map/all_to_all | solution.py:196
  983.4 164.8 %all-to-all-start.3 = ((bf16[16,108,2048]{2,1,0:T(8,128)(2,1)}), bf16[16,108,2048]{2,1,0:T(8,128)(2,1)}, u32[]{:S(2)}, u32[]{:S(2)}) async-start(bf16[16,108,2048]{2,1,0:T(8,128)(2,1)} %reshape.387), calls=%async_computation.3 | async-start | bytes 14680064 | tf_op jit(solution)/shard_map/all_to_all | solution.py:232
  1015.7 218.7 %reduce-scatter.42.cloned.1.call-start = ((), (), s32[]{:S(2)}) async-start(), calls=%async_computation.32 | async-start | bytes 786432
  1191.9 76.2 %reduce-scatter.40.cloned.1.call-start = ((), (), s32[]{:S(2)}) async-start(), calls=%async_computation.31 | async-start | bytes 786432 | tf_op jit(solution)/shard_map/reduce_scatter | solution.py:308
  1226.5 63.4 %reduce-scatter.36.cloned.1.call-start = ((), (), s32[]{:S(2)}) async-start(), calls=%async_computation.29 | async-start | bytes 81920 | tf_op jit(solution)/shard_map/reduce_scatter | solution.py:374
  1227.5 207.7 %reduce-scatter.32.cloned.1.call-start = ((), (), s32[]{:S(2)}) async-start(), calls=%async_computation.27 | async-start | bytes 10485760 | tf_op jit(solution)/shard_map/reduce_scatter | solution.py:371
  1234.3 348.6 %reduce-scatter.28.cloned.1.call-start = ((), (), s32[]{:S(2)}) async-start(), calls=%async_computation.25 | async-start | bytes 10485760 | tf_op jit(solution)/shard_map/reduce_scatter | solution.py:368
  1241.9 488.6 %reduce-scatter.24.cloned.1.call-start = ((), (), s32[]{:S(2)}) async-start(), calls=%async_computation.23 | async-start | bytes 10485760 | tf_op jit(solution)/shard_map/reduce_scatter | solution.py:365
  1281.7 486.8 %reduce-scatter.44.cloned.1.call-start = ((), (), s32[]{:S(2)}) async-start(), calls=%async_computation.33 | async-start | bytes 147456
  1291.4 623.8 %reduce-scatter.20.cloned.1.call-start = ((), (), s32[]{:S(2)}) async-start(), calls=%async_computation.21 | async-start | bytes 10485760 | tf_op jit(solution)/shard_map/reduce_scatter | solution.py:362
  1301.8 761.2 %reduce-scatter.38.cloned.1.call-start = ((), (), s32[]{:S(2)}) async-start(), calls=%async_computation.30 | async-start | bytes 18874368 | tf_op jit(solution)/shard_map/reduce_scatter | solution.py:239
  1344.2 763.1 %reduce-scatter.34.cloned.1.call-start = ((), (), s32[]{:S(2)}) async-start(), calls=%async_computation.28 | async-start | bytes 2359296 | tf_op jit(solution)/shard_map/reduce_scatter | solution.py:421
  1435.2 716.8 %reduce-scatter.30.cloned.1.call-start = ((), (), s32[]{:S(2)}) async-start(), calls=%async_computation.26 | async-start | bytes 2359296 | tf_op jit(solution)/shard_map/reduce_scatter | solution.py:415
  1583.0 147.6 %copy-start.93 = (u32[32]{0:T(128)S(1)}, u32[32]{0:T(128)}, u32[]{:S(2)}) copy-start(u32[32]{0:T(128)} %constant.167) | copy-start | bytes 388
  1583.0 148.2 %copy-start.92 = (u32[32]{0:T(128)S(1)}, u32[32]{0:T(128)}, u32[]{:S(2)}) copy-start(u32[32]{0:T(128)} %constant.171) | copy-start | bytes 388
  1583.0 150.1 %copy-start.25 = (bf16[192,2048]{1,0:T(8,128)(2,1)S(1)}, bf16[192,2048]{1,0:T(8,128)(2,1)}, u32[]{:S(2)}) copy-start(bf16[192,2048]{1,0:T(8,128)(2,1)} %get-tuple-element.52) | copy-start | bytes 2359300
  1583.0 613.5 %reduce-scatter.26.cloned.1.call-start = ((), (), s32[]{:S(2)}) async-start(), calls=%async_computation.24 | async-start | bytes 2359296 | tf_op jit(solution)/shard_map/reduce_scatter | solution.py:409
  1730.5 510.7 %reduce-scatter.22.cloned.1.call-start = ((), (), s32[]{:S(2)}) async-start(), calls=%async_computation.22 | async-start | bytes 2359296 | tf_op jit(solution)/shard_map/reduce_scatter | solution.py:403
  (96 other events, 1533.9 us)
Sparse Core Ops, SparseCore 0:
  9.6 106.7 all-gather.4
  117.9 104.0 all-gather.8
  223.5 103.9 all-gather.6
  328.9 115.2 all-gather.10
  1192.0 41.1 reduce-scatter.41
  1236.0 32.0 reduce-scatter.39
  1270.9 18.9 reduce-scatter.35
  1292.4 142.7 reduce-scatter.31
  1437.7 145.1 reduce-scatter.27
  1585.2 145.1 reduce-scatter.23
  1734.3 34.0 reduce-scatter.43
  1770.7 144.4 reduce-scatter.19
  1917.5 145.3 reduce-scatter.37
  2066.1 41.1 reduce-scatter.33
  2110.8 41.2 reduce-scatter.29
  2155.2 41.2 reduce-scatter.25
  2199.9 41.2 reduce-scatter.21
where the time goes:
time: 2260 us; the launch traced here: 2250 us
  waiting for transfers between devices  1520 us (67%)
  matrix products  236 us (10%)
  local copies, waits for them, and re-layouts  216 us (10%)
  starting transfers between devices  105 us (5%)
  blocking collectives  83.7 us (4%)
  other arithmetic  75.5 us (3%)
    reduce_scatter x1, waiting for transfers between devices, shards(): lax.psum_scatter(value_grad.astype(jnp.bfloat16), 'expert', scatter_dimen...  148 us
    reduce_scatter x1, waiting for transfers between devices, shards(): lax.psum_scatter(key_grad.astype(jnp.bfloat16), 'expert', scatter_dimensi...  147 us
    reduce_scatter x1, waiting for transfers between devices, shards(): lax.psum_scatter(query_grad.astype(jnp.bfloat16), 'expert', scatter_dimen...  131 us
    reduce_scatter x1, waiting for transfers between devices, shards(): lax.psum_scatter(jnp.concatenate([jnp.einsum('rf,rd->fd', d_gate, input_f...  103 us
    all_to_all x1, waiting for transfers between devices, shards(): lax.all_to_all(grad_outgoing, ('expert', 'dp'), split_axis=0, concat_axis...  101 us
    all_gather x1, waiting for transfers between devices, shards(): lax.all_gather(w_key, 'context', axis=0, tiled=True)  99.6 us
    all_to_all x1, waiting for transfers between devices, shards(): lax.all_to_all(result, ('expert', 'dp'), split_axis=0, concat_axis=0, til...  99 us
    all_gather x1, waiting for transfers between devices, shards(): lax.all_gather(w_query, 'context', axis=0, tiled=True)  98.8 us
  transfers between devices with their start and end apart: 21, of which 20 were waited for; matrix products, arithmetic and copies ran while one was open for 18% of the time, Pallas kernels for 0%

commit v1 on v0

v1 whole, which is shorter than its diff:
```python
import functools

import jax
import jax.numpy as jnp
from jax import lax
from jax.experimental import pallas as pl
from jax.experimental.pallas import tpu as pltpu
from jax.sharding import PartitionSpec as P

HEADS = 16
EPSILON = 1e-05
NEG_LARGE = -1e30
F32 = jnp.float32
BF16 = jnp.bfloat16
PLANE = ("expert", "dp")
VMEM_LIMIT = 48 * 1024 * 1024


def dot(left, right, dims=((1,), (0,)), out=F32):
    return lax.dot_general(left, right, (dims, ((), ())), preferred_element_type=out)


NT = ((1,), (1,))
TN = ((0,), (0,))


def post_kernel(count, *refs):
    parts, (gain_ref, cos_ref, sin_ref, raw_ref, low_ref) = refs[:count], refs[count:]
    raw = parts[0][...]
    for part in parts[1:]:
        raw = raw + part[...].astype(F32)
    raw_ref[...] = raw
    inverse = lax.rsqrt(jnp.mean(raw * raw, axis=-1, keepdims=True) + EPSILON)
    scaled = raw * inverse * gain_ref[...]
    cosine, sine = cos_ref[...], sin_ref[...]
    head = cosine.shape[1]
    for h in range(raw.shape[1] // head):
        piece = scaled[:, h * head : (h + 1) * head]
        turned = piece * cosine + pltpu.roll(piece, head // 2, 1) * sine
        low_ref[:, h * head : (h + 1) * head] = turned.astype(BF16)


def qk_post(parts, gain, cosine, sine):
    rows, width = parts[0].shape
    head = cosine.shape[1]
    step = 64
    row = lambda w: pl.BlockSpec((step, w), lambda i: (i, 0))
    return pl.pallas_call(
        functools.partial(post_kernel, len(parts)),
        grid=(rows // step,),
        in_specs=[row(width)] * len(parts)
        + [pl.BlockSpec((1, width), lambda i: (0, 0)), row(head), row(head)],
        out_specs=[row(width), row(width)],
        out_shape=[
            jax.ShapeDtypeStruct((rows, width), F32),
            jax.ShapeDtypeStruct((rows, width), BF16),
        ],
        compiler_params=pltpu.CompilerParams(vmem_limit_bytes=VMEM_LIMIT),
        name="qk_post",
    )(*parts, gain, cosine, sine)


def post_back_kernel(grad_ref, raw_ref, gain_ref, cos_ref, sin_ref, low_ref, gain_grad_ref):
    raw = raw_ref[...]
    inverse = lax.rsqrt(jnp.mean(raw * raw, axis=-1, keepdims=True) + EPSILON)
    cosine, sine = cos_ref[...], sin_ref[...]
    head = cosine.shape[1]
    pieces = []
    for h in range(raw.shape[1] // head):
        piece = grad_ref[:, h * head : (h + 1) * head]
        pieces.append(piece * cosine - pltpu.roll(piece, head // 2, 1) * sine)
    grad = jnp.concatenate(pieces, axis=1)
    scaled = grad * gain_ref[...]
    centre = jnp.mean(scaled * raw, axis=-1, keepdims=True)
    low_ref[...] = (inverse * scaled - raw * (inverse * inverse * inverse * centre)).astype(BF16)
    total = jnp.sum(grad * raw * inverse, axis=0, keepdims=True)

    @pl.when(pl.program_id(0) == 0)
    def _():
        gain_grad_ref[...] = total

    @pl.when(pl.program_id(0) > 0)
    def _():
        gain_grad_ref[...] += total


def qk_post_back(grad, raw, gain, cosine, sine):
    rows, width = raw.shape
    head = cosine.shape[1]
    step = 64
    row = lambda w: pl.BlockSpec((step, w), lambda i: (i, 0))
    whole = pl.BlockSpec((1, width), lambda i: (0, 0))
    return pl.pallas_call(
        post_back_kernel,
        grid=(rows // step,),
        in_specs=[row(width), row(width), whole, row(head), row(head)],
        out_specs=[row(width), whole],
        out_shape=[
            jax.ShapeDtypeStruct((rows, width), BF16),
            jax.ShapeDtypeStruct((1, width), F32),
        ],
        compiler_params=pltpu.CompilerParams(vmem_limit_bytes=VMEM_LIMIT),
        name="qk_post_back",
    )(grad, raw, gain, cosine, sine)


def read_mask(meta_ref, rows, keys, prompt_dev, prompt_total):
    row = lax.broadcasted_iota(jnp.int32, (rows, keys), 0)
    key = lax.broadcasted_iota(jnp.int32, (rows, keys), 1)
    is_prompt_row = row < prompt_dev
    is_prompt_key = key < prompt_total
    prompt_limit = jnp.where(is_prompt_row, meta_ref[0] + row + 1, meta_ref[1])
    own_limit = jnp.where(is_prompt_row, 0, row - prompt_dev + 1)
    limit = jnp.where(is_prompt_key, prompt_limit, own_limit + prompt_total)
    return key < limit


def head_probs(query, key, mask):
    scores = jnp.where(mask, dot(query, key, NT) * (query.shape[1] ** -0.5), NEG_LARGE)
    exponent = jnp.exp(scores - jnp.max(scores, axis=-1, keepdims=True))
    return exponent / jnp.sum(exponent, axis=-1, keepdims=True)


def attend_kernel(heads, prompt_dev, prompt_total, meta_ref, q_ref, k_ref, v_ref, out_ref):
    mask = read_mask(meta_ref, q_ref.shape[0], k_ref.shape[0], prompt_dev, prompt_total)
    head = q_ref.shape[1] // heads
    for h in range(heads):
        at = slice(h * head, (h + 1) * head)
        weights = head_probs(q_ref[:, at], k_ref[:, at], mask).astype(BF16)
        out_ref[:, at] = dot(weights, v_ref[:, at]).astype(BF16)


def attend_back_kernel(
    heads, prompt_dev, prompt_total, meta_ref, q_ref, k_ref, v_ref, d_ref, dq_ref, dk_ref, dv_ref
):
    mask = read_mask(meta_ref, q_ref.shape[0], k_ref.shape[0], prompt_dev, prompt_total)
    head = q_ref.shape[1] // heads
    for h in range(heads):
        at = slice(h * head, (h + 1) * head)
        query, key, grad = q_ref[:, at], k_ref[:, at], d_ref[:, at]
        probs = head_probs(query, key, mask)
        d_probs = dot(grad, v_ref[:, at], NT)
        centre = jnp.sum(probs * d_probs, axis=-1, keepdims=True)
        d_scores = (probs * (d_probs - centre) * head**-0.5).astype(BF16)
        dq_ref[:, at] = dot(d_scores, key)
        dk_ref[:, at] = dot(d_scores, query, TN)
        dv_ref[:, at] = dot(probs.astype(BF16), grad, TN)


def attention_call(kernel, name, arrays, outs, meta, prompt_dev, prompt_total):
    width = arrays[0].shape[1]
    heads = 4
    spec = lambda a: pl.BlockSpec((a.shape[0], width * heads // HEADS), lambda i, m: (0, i))
    return pl.pallas_call(
        functools.partial(kernel, heads, prompt_dev, prompt_total),
        grid_spec=pltpu.PrefetchScalarGridSpec(
            num_scalar_prefetch=1,
            grid=(HEADS // heads,),
            in_specs=[spec(a) for a in arrays],
            out_specs=[spec(a) for a in outs],
        ),
        out_shape=outs,
        compiler_params=pltpu.CompilerParams(vmem_limit_bytes=VMEM_LIMIT),
        name=name,
    )(meta, *arrays)


def shards(
    prompt_in,
    cont_in,
    prompt_cot,
    cont_cot,
    prompt_routes,
    cont_routes,
    prefix,
    attn_gain,
    query_gain,
    key_gain,
    ffn_gain,
    w_query,
    w_key,
    w_value,
    w_output,
    w_router,
    expert_gate,
    expert_up,
    expert_down,
):
    prompt_dev, width = prompt_in.shape[1:]
    cont_len = cont_in.shape[2]
    tokens = prompt_dev + cont_len
    head_dim = width // HEADS
    top_count = prompt_routes.shape[2]
    expert_count = w_router.shape[1]
    hidden = expert_gate.shape[1]
    planes = lax.axis_size("context")
    me = lax.axis_index("context")
    rows_e, rows_d = lax.axis_size("expert"), lax.axis_size("dp")
    owners = rows_e * rows_d
    my_expert = lax.axis_index("expert") * rows_d + lax.axis_index("dp")
    prompt_total = prompt_dev * planes
    most_prompt = 9 * prompt_dev * top_count // (8 * expert_count)
    most_cont = 9 * cont_len * top_count // (8 * expert_count)
    slots = (most_prompt + most_cont + 15) // 16 * 16
    part = width // planes
    out_group = width // (rows_e * planes)

    def shift(value, r):
        return lax.ppermute(value, "context", [(i, (i + r) % planes) for i in range(planes)])

    def block(value, r):
        return lax.dynamic_slice_in_dim(value, ((me + r) % planes) * part, part, axis=1)

    def out_part(value, r):
        at = ((me + r) % planes) * out_group
        return jnp.concatenate(
            [
                lax.dynamic_slice_in_dim(value, e * planes * out_group + at, out_group, axis=1)
                for e in range(rows_e)
            ],
            axis=1,
        )

    def placed(blocks):
        full = jnp.zeros((tokens, width), blocks[0].dtype)
        for r, piece in enumerate(blocks):
            full = lax.dynamic_update_slice_in_dim(full, piece, ((me + r) % planes) * part, axis=1)
        return full

    others = range(1, planes)

    x_low = jnp.concatenate([prompt_in[0], cont_in[0, 0]], axis=0)
    x_rows = x_low.astype(F32)
    inverse = lax.rsqrt(jnp.mean(x_rows * x_rows, axis=-1) + EPSILON)
    x_blocks = [block(x_low, 0)] + [shift(block(x_low, r), r) for r in others]
    inverses = [inverse] + [shift(inverse, r) for r in others]
    gain_part = attn_gain.astype(F32)
    normed_blocks = [
        (piece.astype(F32) * inv[:, None] * gain_part).astype(BF16)
        for piece, inv in zip(x_blocks, inverses)
    ]

    small = jnp.concatenate(
        [jnp.stack([attn_gain, query_gain, key_gain, ffn_gain], axis=1), w_router], axis=1
    )
    small = lax.all_gather(small, "context", axis=0, tiled=True)
    gains = small[:, :4].T.astype(F32)
    gain_attn, gain_query, gain_key, gain_ffn = [gains[i : i + 1] for i in range(4)]
    full_router = small[:, 4:]

    d_out_low = jnp.concatenate([prompt_cot[0], cont_cot[0, 0]], axis=0)
    routes = jnp.concatenate([prompt_routes[0], cont_routes[0, 0]], axis=0)
    all_routes = lax.all_gather(routes, PLANE, axis=0, tiled=True)
    all_cot = lax.all_gather(d_out_low, PLANE, axis=0, tiled=True)

    start_len = prefix[0, 0]
    prompt_pos = me * prompt_dev + jnp.arange(prompt_dev, dtype=jnp.int32)
    positions = jnp.concatenate([prompt_pos, start_len + jnp.arange(cont_len, dtype=jnp.int32)])
    half_index = jnp.arange(head_dim // 2, dtype=F32)
    angles = positions.astype(F32)[:, None] * (10000.0 ** (-2.0 * half_index / head_dim))[None, :]
    cosine = jnp.cos(angles)
    sine = jnp.sin(angles)
    cosine = jnp.concatenate([cosine, cosine], axis=1)
    sine = jnp.concatenate([-sine, sine], axis=1)
    meta = jnp.stack([me * prompt_dev, start_len]).astype(jnp.int32)

    def project(pieces, weight):
        sent = [shift(dot(pieces[r], weight).astype(BF16), planes - r) for r in others]
        return [dot(pieces[0], weight)] + sent

    key_parts = project(normed_blocks, w_key)
    value_parts = project(normed_blocks, w_value)
    query_parts = project(normed_blocks, w_query)
    key_raw, key_low = qk_post(key_parts, gain_key, cosine, sine)
    value_low = sum(p.astype(F32) for p in value_parts).astype(BF16)
    query_raw, query_low = qk_post(query_parts, gain_query, cosine, sine)

    def with_prompt(rows):
        full = jnp.zeros((prompt_total + cont_len, width), BF16)
        full = lax.dynamic_update_slice_in_dim(full, rows[prompt_dev:], prompt_total, axis=0)
        for r in range(planes):
            piece = rows[:prompt_dev]
            if r:
                piece = shift(piece, planes - r)
            full = lax.dynamic_update_slice_in_dim(
                full, piece, ((me + r) % planes) * prompt_dev, axis=0
            )
        return full

    key_set = with_prompt(key_low)
    value_set = with_prompt(value_low)
    (attended,) = attention_call(
        attend_kernel,
        "attend",
        [query_low, key_set, value_set],
        [jax.ShapeDtypeStruct((tokens, width), BF16)],
        meta,
        prompt_dev,
        prompt_total,
    )

    attended_blocks = [block(attended, 0)] + [shift(block(attended, r), r) for r in others]
    mixed_rows = x_rows + sum(p.astype(F32) for p in project(attended_blocks, w_output))
    inverse2 = lax.rsqrt(jnp.mean(mixed_rows * mixed_rows, axis=-1, keepdims=True) + EPSILON)
    normed2_low = (mixed_rows * inverse2 * gain_ffn).astype(BF16)

    all_normed2 = lax.all_gather(normed2_low, PLANE, axis=0, tiled=True)

    normed_low = (x_rows * inverse[:, None] * gain_attn).astype(BF16)
    normed_out = jnp.concatenate(
        [out_part(normed_low, 0)] + [shift(out_part(normed_low, r), r) for r in others], axis=0
    )
    attended_out = jnp.concatenate(
        [out_part(attended, 0)] + [shift(out_part(attended, r), r) for r in others], axis=0
    )

    logits = dot(normed2_low, full_router)
    shifted = jnp.exp(logits - jnp.max(logits, axis=1, keepdims=True))
    router_probs = shifted / jnp.sum(shifted, axis=1, keepdims=True)

    member = jnp.sum((all_routes == my_expert).astype(F32), axis=1).reshape(owners, tokens)

    def ranks(m):
        count = m.shape[1]
        before = jnp.triu(jnp.ones((count, count), BF16), 1)
        return dot(m.astype(BF16), before)

    slot_of = jnp.concatenate(
        [ranks(member[:, :prompt_dev]), ranks(member[:, prompt_dev:]) + most_prompt], axis=1
    )
    slot_of = jnp.where(member > 0, slot_of, -1.0)
    pick = (
        slot_of[:, None, :] == jnp.arange(slots, dtype=F32)[None, :, None]
    ).astype(BF16)

    def gather_rows(values):
        picked = jnp.einsum(
            "sjt,std->sjd",
            pick,
            values.reshape(owners, tokens, width),
            preferred_element_type=BF16,
        )
        return picked.reshape(owners * slots, width)

    def spread_rows(values):
        return jnp.einsum(
            "sjt,sjd->std",
            pick,
            values.reshape(owners, slots, width),
            preferred_element_type=BF16,
        ).reshape(owners * tokens, width)

    gate_w, up_w, down_w = expert_gate[0], expert_up[0], expert_down[0]
    slot_cot = gather_rows(all_cot)
    d_act_plain = dot(slot_cot, down_w, NT)

    slot_in = gather_rows(all_normed2)
    slot_logits = dot(slot_in, full_router)
    slot_exp = jnp.exp(slot_logits - jnp.max(slot_logits, axis=1, keepdims=True))
    is_mine = jnp.arange(expert_count, dtype=jnp.int32) == my_expert
    slot_gate = jnp.sum(jnp.where(is_mine, slot_exp, 0.0), axis=1, keepdims=True) / jnp.sum(
        slot_exp, axis=1, keepdims=True
    )
    gate_pre = dot(slot_in, gate_w, NT)
    up_pre = dot(slot_in, up_w, NT)
    sigmoid = jax.nn.sigmoid(gate_pre)
    silu = gate_pre * sigmoid
    act_low = (silu * up_pre).astype(BF16)
    d_act = slot_gate * d_act_plain
    d_gate = (d_act * up_pre * (sigmoid * (1.0 + gate_pre * (1.0 - sigmoid)))).astype(BF16)
    d_up = (d_act * silu).astype(BF16)
    slot_dprob = jnp.sum(act_low.astype(F32) * d_act_plain, axis=1).reshape(owners, slots)
    token_dprob = jnp.sum(pick.astype(F32) * slot_dprob[:, :, None], axis=1)
    dprobs = lax.all_to_all(token_dprob, PLANE, split_axis=0, concat_axis=0, tiled=True).T
    d_input = (dot(d_gate, gate_w) + dot(d_up, up_w)).astype(BF16)
    d_normed2_moe = lax.psum_scatter(
        spread_rows(d_input), PLANE, scatter_dimension=0, tiled=True
    ).astype(F32)

    slot_dy = (slot_gate * slot_cot.astype(F32)).astype(BF16)
    piece = hidden // planes

    def expert_grad(left, right):
        def rows(r):
            cols = lax.dynamic_slice_in_dim(left, ((me + r) % planes) * piece, piece, axis=1)
            return dot(cols, right, TN)

        sent = [shift(rows(r).astype(BF16), r) for r in others]
        return rows(0) + sum(s.astype(F32) for s in sent)

    gate_grad = expert_grad(d_gate, slot_in)
    up_grad = expert_grad(d_up, slot_in)
    down_grad = expert_grad(act_low, slot_dy)

    slot_out = (slot_gate * dot(act_low, down_w)).astype(BF16)
    moe_out = lax.psum_scatter(
        spread_rows(slot_out), PLANE, scatter_dimension=0, tiled=True
    ).astype(F32)
    out_rows = mixed_rows + moe_out

    d_out = d_out_low.astype(F32)
    dlogit_low = (
        router_probs * (dprobs - jnp.sum(router_probs * dprobs, axis=1, keepdims=True))
    ).astype(BF16)
    router_grad = dot(normed2_low, dlogit_low, TN)
    d_normed2 = d_normed2_moe + dot(dlogit_low, full_router, NT)
    scaled2 = gain_ffn * d_normed2
    centre2 = jnp.mean(scaled2 * mixed_rows, axis=-1, keepdims=True)
    d_mixed = d_out + inverse2 * scaled2 - mixed_rows * (inverse2**3 * centre2)
    ffn_gain_grad = jnp.sum(d_normed2 * mixed_rows * inverse2, axis=0)

    branch_low = d_mixed.astype(BF16)
    branches = [branch_low] + [shift(branch_low, r) for r in others]

    def back_blocks(pairs_of):
        sent = [shift(pairs_of(r).astype(BF16), planes - r) for r in others]
        return [pairs_of(0)] + sent

    d_attended = placed(
        [p.astype(BF16) for p in back_blocks(lambda r: dot(branches[r], w_output, NT))]
    )
    output_grad = dot(attended_out, jnp.concatenate(branches, axis=0), TN).astype(BF16)

    key_total = prompt_total + cont_len
    d_queries, d_keys_all, d_values_all = attention_call(
        attend_back_kernel,
        "attend_back",
        [query_low, key_set, value_set, d_attended],
        [
            jax.ShapeDtypeStruct((tokens, width), F32),
            jax.ShapeDtypeStruct((key_total, width), F32),
            jax.ShapeDtypeStruct((key_total, width), F32),
        ],
        meta,
        prompt_dev,
        prompt_total,
    )

    def own_keys(rows):
        def prompt_rows(r):
            return lax.dynamic_slice_in_dim(
                rows, ((me + r) % planes) * prompt_dev, prompt_dev, axis=0
            )

        total = prompt_rows(0)
        for r in others:
            total = total + shift(prompt_rows(r).astype(BF16), r).astype(F32)
        return jnp.concatenate([total, rows[prompt_total:]], axis=0)

    d_value_low = own_keys(d_values_all).astype(BF16)
    d_query_low, query_gain_grad = qk_post_back(d_queries, query_raw, gain_query, cosine, sine)
    d_key_low, key_gain_grad = qk_post_back(
        own_keys(d_keys_all), key_raw, gain_key, cosine, sine
    )

    def spread(low):
        return [low] + [shift(low, r) for r in others]

    d_values, d_query_rows, d_key_rows = spread(d_value_low), spread(d_query_low), spread(d_key_low)
    d_normed = placed(
        [
            p.astype(F32)
            for p in back_blocks(
                lambda r: dot(d_values[r], w_value, NT)
                + dot(d_query_rows[r], w_query, NT)
                + dot(d_key_rows[r], w_key, NT)
            )
        ]
    )
    value_grad = dot(normed_out, jnp.concatenate(d_values, axis=0), TN).astype(BF16)
    query_grad = dot(normed_out, jnp.concatenate(d_query_rows, axis=0), TN).astype(BF16)
    key_grad = dot(normed_out, jnp.concatenate(d_key_rows, axis=0), TN).astype(BF16)

    scaled = gain_attn * d_normed
    centre = jnp.mean(scaled * x_rows, axis=-1, keepdims=True)
    inv = inverse[:, None]
    d_x = d_mixed + inv * scaled - x_rows * (inv**3 * centre)
    attn_gain_grad = jnp.sum(d_normed * x_rows * inv, axis=0)

    def scatter(value):
        return lax.psum_scatter(value, PLANE, scatter_dimension=0, tiled=True).astype(F32)

    everywhere = ("expert", "context", "dp")
    small_grads = jnp.concatenate(
        [
            jnp.stack([attn_gain_grad, query_gain_grad[0], key_gain_grad[0], ffn_gain_grad], axis=1),
            router_grad,
        ],
        axis=1,
    )
    small_grads = lax.psum_scatter(small_grads, everywhere, scatter_dimension=0, tiled=True)
    return (
        out_rows[:prompt_dev].astype(BF16)[None],
        out_rows[prompt_dev:].astype(BF16)[None, None],
        d_x[:prompt_dev][None],
        d_x[prompt_dev:][None, None],
        small_grads[:, 0],
        small_grads[:, 1],
        small_grads[:, 2],
        small_grads[:, 3],
        scatter(query_grad),
        scatter(key_grad),
        scatter(value_grad),
        scatter(output_grad),
        small_grads[:, 4:],
        gate_grad[None],
        up_grad[None],
        down_grad[None],
    )


def solution(mesh):
    rows = P(("expert", "dp"), "context", None)
    conts = P(("expert", "dp"), "context", None, None)
    experts = P(("expert", "dp"), None, None)
    everywhere = ("expert", "context", "dp")
    in_specs = (
        (rows, conts, rows, conts, rows, conts, P(("expert", "dp"), "context"))
        + (P("context"),) * 4
        + (P("context", None),) * 5
        + (experts,) * 3
    )
    out_specs = (
        (rows, conts, rows, conts)
        + (P(everywhere),) * 4
        + (P(everywhere, None),) * 5
        + (rows,) * 3
    )
    return jax.shard_map(shards, mesh=mesh, in_specs=in_specs, out_specs=out_specs, check_vma=False)
```

time: 2260 us -> 1050 us (0.46)
  waiting for transfers between devices: 1520 us -> 642 us
  local copies, waits for them, and re-layouts: 216 us -> 34.3 us
  starting transfers between devices: 105 us -> 31.3 us
  other arithmetic: 75.5 us -> 28.8 us
  blocking collectives: 83.7 us -> 43.1 us
  Pallas kernels: 0 us -> 22.7 us
    reduce_scatter x11 -> x6, waiting for transfers between devices: 787 us -> 344 us  [the longest x4 245 us: scatter(): lax.psum_scatter(value, PLANE, scatter_dimension=0, tiled=True).astype(F32)]
    all_to_all x4 -> x1, waiting for transfers between devices: 367 us -> 5.69 us  [shards(): lax.all_to_all(token_dprob, PLANE, split_axis=0, concat_axis=0, tiled=True)]
    all_gather x4 -> x2, waiting for transfers between devices: 325 us -> 56.3 us  [the longest x1 56.3 us: shards(): all_normed2 = lax.all_gather(normed2_low, PLANE, axis=0, tiled=True)]
    ppermute x0 -> x22, waiting for transfers between devices: none -> 235 us  [shift(): lax.ppermute(value, 'context', [(i, (i + r) % planes) for i in range(plan...]
    gather x14 -> x0, local copies, waits for them, and re-layouts: 103 us -> none  [the longest x2 21.9 us: shards(): cot_padded[slot_owner]]
    all_to_all x4 -> x1, starting transfers between devices: 103 us -> 3.49 us  [shards(): lax.all_to_all(token_dprob, PLANE, split_axis=0, concat_axis=0, tiled=True)]
    reshape x9 -> x0, local copies, waits for them, and re-layouts: 60.9 us -> none  [the longest x1 8.71 us: shards(): flat_in = slot_items.reshape(-1, model_width)]
    unnamed x19 -> x10, waiting for transfers between devices: 36.7 us -> 0.15 us
  transfers between devices with their start and end apart: 21 -> 32, of which waited for: 20 -> 24; matrix products, arithmetic and copies ran while one was open for 18% -> 18% of each run, Pallas kernels for 0% -> 2%
where the time goes in v1:
time: 1050 us; the launch traced here: 1040 us
  waiting for transfers between devices  642 us (61%)
  matrix products  223 us (21%)
  blocking collectives  43.1 us (4%)
  local copies, waits for them, and re-layouts  34.3 us (3%)
  starting transfers between devices  31.3 us (3%)
  other arithmetic  28.8 us (3%)
  Pallas kernels  22.7 us (2%)
  between operations  16 us (2%)
    reduce_scatter x4, waiting for transfers between devices, scatter(): lax.psum_scatter(value, PLANE, scatter_dimension=0, tiled=True).astype(F32)  245 us
    ppermute x22, waiting for transfers between devices, shift(): lax.ppermute(value, 'context', [(i, (i + r) % planes) for i in range(plan...  235 us
    dot_general x38, matrix products, dot(): lax.dot_general(left, right, (dims, ((), ())), preferred_element_type=out)  191 us
    reduce_scatter x1, waiting for transfers between devices, shards(): lax.psum_scatter(spread_rows(d_input), PLANE, scatter_dimension=0, tiled=...  98.9 us
    all_gather x1, waiting for transfers between devices, shards(): all_normed2 = lax.all_gather(normed2_low, PLANE, axis=0, tiled=True)  56.3 us
    all_gather x1, blocking collectives, shards(): all_routes = lax.all_gather(routes, PLANE, axis=0, tiled=True)  34.3 us
    ppermute x22, starting transfers between devices, shift(): lax.ppermute(value, 'context', [(i, (i + r) % planes) for i in range(plan...  27 us
  transfers between devices with their start and end apart: 32, of which 24 were waited for; matrix products, arithmetic and copies ran while one was open for 18% of the time, Pallas kernels for 2%

profile of v1, /device:TPU:0, one launch (start us, length us, event | category | flops | bytes accessed | tf_op | source)
XLA Modules:
  0.0 1040.6 jit_solution(14488655813387010981)
XLA Ops:
  14.9 8.8 all_gather.12
  47.5 10.2 collective-permute-done.5
  60.5 14.0 %collective-permute-done.3.refs_1_ = bf16[192,2048]{1,0:T(8,128)(2,1)S(1)} collective-permute-done((bf16[192,2048]{1,0:T(8,128)(2,1)S(1)}, bf16[192,2048]{1,0:T(8,128)(2,1)S(1)}, u32[]{:S(2)}, u32[]{:S(2)}) %collective-permute-start.3) | collective-permute-done | bytes 786464 | tf_op jit(solution)/shard_map/ppermute | solution.py:209
  78.6 12.9 %collective-permute-done.2.refs_1_ = bf16[192,2048]{1,0:T(8,128)(2,1)} collective-permute-done((bf16[192,2048]{1,0:T(8,128)(2,1)}, bf16[192,2048]{1,0:T(8,128)(2,1)}, u32[]{:S(2)}, u32[]{:S(2)}) %collective-permute-start.2) | collective-permute-done | bytes 786464 | tf_op jit(solution)/shard_map/ppermute | solution.py:209
  107.4 8.2 collective-permute-done.7
  117.8 16.0 %collective-permute-done.8 = bf16[192,2048]{1,0:T(8,128)(2,1)S(1)} collective-permute-done((bf16[192,2048]{1,0:T(8,128)(2,1)S(1)}, bf16[192,2048]{1,0:T(8,128)(2,1)S(1)}, u32[]{:S(2)}, u32[]{:S(2)}) %collective-permute-start.8) | collective-permute-done | bytes 786464 | tf_op jit(solution)/shard_map/ppermute | solution.py:209
  138.9 34.3 %all-gather = s32[16,192,8]{1,2,0:T(8,128)S(1)} all-gather(s32[1,192,8]{1,2,0:T(8,128)S(1)} %add_bitcast_fusion.3), channel_id=1, replica_groups=mesh['expert'=4,'context'=2,'dp'=4] {'expert','dp'}, dimensions={0}, use_global_device_ids=true | all-gather | bytes 104448 | tf_op jit(solution)/shard_map/all_gather | solution.py:253
  173.6 10.8 %fusion.47 = bf16[16,112,2048]{2,1,0:T(8,128)(2,1)} fusion(bf16[16,192,2048]{2,1,0:T(8,128)(2,1)} %bitcast.132, f32[16,192]{1,0:T(8,128)S(1)} %maximum_select_fusion), kind=kOutput, calls=%fused_computation.82 | convolution fusion | flops 1409630208 | bytes 19935232 | tf_op jit(solution)/shard_map/sjt,std->sjd/dot_general | solution.py:337
  184.4 56.3 %all-gather.4.cloned.1.call-done = bf16[3072,2048]{1,0:T(8,128)(2,1)} async-done(((bf16[192,2048]{1,0:T(8,128)(2,1)}), bf16[3072,2048]{1,0:T(8,128)(2,1)}) %all-gather.4.cloned.1.call-update) | async-done | bytes 12582928 | tf_op jit(solution)/shard_map/all_gather | solution.py:307
  252.5 9.9 fusion.5
  262.4 9.8 fusion.9
  272.3 20.2 %multiply_reduce_fusion = (f32[1792]{0:T(1024)}, bf16[1792,1024]{0,1:T(8,128)(2,1)}, bf16[1792,1024]{0,1:T(8,128)(2,1)S(1)}, bf16[1792,1024]{0,1:T(8,128)(2,1)}) fusion(f32[1792,1024]{0,1:T(8,128)} %fusion.5, f32[1792,1024]{0,1:T(8,128)} %fusion.9, f32[1792]{0:T(1024)S(1)} %div.45, bf16[1792,2048]{1,0:T(8,128)(2,1)} %bitcast.142, ...), kind=kOutput, calls=%fused_computation.3 | convolution fusion | flops 7551055872 | bytes 37238784 | tf_op jit(solution)/shard_map/dot_general | solution.py:20
  292.6 11.3 %fusion.7 = f32[1792,2048]{1,0:T(8,128)} fusion(bf16[1792,1024]{0,1:T(8,128)(2,1)S(1)} %get-tuple-element.46, bf16[1,1024,2048]{2,1,0:T(8,128)(2,1)S(1)} %copy-done.80), kind=kOutput, calls=%fused_computation.15 | convolution fusion | flops 7516192768 | bytes 22544384 | tf_op jit(solution)/shard_map/dot_general | solution.py:20
  303.9 12.9 %add_convert_fusion = bf16[1792,2048]{1,0:T(8,128)(2,1)S(1)} fusion(f32[1792,2048]{1,0:T(8,128)} %fusion.7, bf16[1792,1024]{0,1:T(8,128)(2,1)} %get-tuple-element.47, bf16[1,1024,2048]{2,1,0:T(8,128)(2,1)} %param.36), kind=kOutput, calls=%fused_computation.1 | convolution fusion | flops 7523532800 | bytes 29884416 | tf_op jit(solution)/shard_map/dot_general | solution.py:20
  323.4 11.1 %multiply_convert_fusion.1 = bf16[1792,2048]{1,0:T(8,128)(2,1)S(1)} fusion(bf16[1792,1024]{0,1:T(8,128)(2,1)} %get-tuple-element.45, f32[1792]{0:T(1024)S(1)} %div.45, bf16[1,1024,2048]{2,1,0:T(8,128)(2,1)} %param.37), kind=kOutput, calls=%fused_computation.2 | convolution fusion | flops 7523532800 | bytes 15211520 | tf_op jit(solution)/shard_map/dot_general | solution.py:20
  334.4 7.8 fusion.48
  357.5 98.9 %reduce-scatter.12.cloned.1.call-done = bf16[192,2048]{1,0:T(8,128)(2,1)} async-done(((bf16[3072,2048]{1,0:T(8,128)(2,1)}), bf16[192,2048]{1,0:T(8,128)(2,1)}) %reduce-scatter.12.cloned.1.call-update) | async-done | bytes 786448 | tf_op jit(solution)/shard_map/reduce_scatter | solution.py:376
  465.5 16.5 %collective-permute-done.9 = bf16[192,2048]{1,0:T(8,128)(2,1)} collective-permute-done((bf16[192,2048]{1,0:T(8,128)(2,1)}, bf16[192,2048]{1,0:T(8,128)(2,1)}, u32[]{:S(2)}, u32[]{:S(2)}) %collective-permute-start.9) | collective-permute-done | bytes 786464 | tf_op jit(solution)/shard_map/ppermute | solution.py:209
  498.7 11.4 %attend_back.1 = (f32[192,2048]{1,0:T(8,128)S(1)}, f32[256,2048]{1,0:T(8,128)}, f32[256,2048]{1,0:T(8,128)}) custom-call(s32[2]{0:T(128)S(1)} %copy-done.18, bf16[192,2048]{1,0:T(8,128)(2,1)S(1)} %copy-done.4, bf16[256,2048]{1,0:T(8,128)(2,1)S(1)} %constant_dynamic-update-slice_fusion.3.k_ref, ...), custom_call_target="tpu_custom_call" | custom-call | tf_op jit(solution)/shard_map/attend_back/pallas_call | solution.py:154
  533.6 9.7 collective-permute-done.14
  546.0 27.2 %collective-permute-done.15 = bf16[192,2048]{1,0:T(8,128)(2,1)S(1)} collective-permute-done((bf16[192,2048]{1,0:T(8,128)(2,1)S(1)}, bf16[192,2048]{1,0:T(8,128)(2,1)S(1)}, u32[]{:S(2)}, u32[]{:S(2)}) %collective-permute-start.15) | collective-permute-done | bytes 786464 | tf_op jit(solution)/shard_map/ppermute | solution.py:209
  618.6 9.0 convolution_convert_fusion.5
  628.2 8.5 convolution_convert_fusion.6
  644.2 7.8 convolution_convert_fusion.4
  652.8 25.8 %collective-permute-done.20 = bf16[512,2048]{1,0:T(8,128)(2,1)} collective-permute-done((bf16[512,2048]{1,0:T(8,128)(2,1)}, bf16[512,2048]{1,0:T(8,128)(2,1)}, u32[]{:S(2)}, u32[]{:S(2)}) %collective-permute-start.20) | collective-permute-done | bytes 2097184 | tf_op jit(solution)/shard_map/ppermute | solution.py:209
  678.6 9.0 add_bitcast_fusion.1
  687.6 38.0 %collective-permute-done.19 = bf16[512,2048]{1,0:T(8,128)(2,1)} collective-permute-done((bf16[512,2048]{1,0:T(8,128)(2,1)}, bf16[512,2048]{1,0:T(8,128)(2,1)}, u32[]{:S(2)}, u32[]{:S(2)}) %collective-permute-start.19) | collective-permute-done | bytes 2097184 | tf_op jit(solution)/shard_map/ppermute | solution.py:209
  732.4 32.0 %collective-permute-done.21 = bf16[512,2048]{1,0:T(8,128)(2,1)S(1)} collective-permute-done((bf16[512,2048]{1,0:T(8,128)(2,1)S(1)}, bf16[512,2048]{1,0:T(8,128)(2,1)S(1)}, u32[]{:S(2)}, u32[]{:S(2)}) %collective-permute-start.21) | collective-permute-done | bytes 2097184 | tf_op jit(solution)/shard_map/ppermute | solution.py:209
  781.4 24.0 %reduce-scatter.20.cloned.1.call-done = bf16[64,2048]{1,0:T(8,128)(2,1)} async-done(((bf16[1024,2048]{1,0:T(8,128)(2,1)}), bf16[64,2048]{1,0:T(8,128)(2,1)}) %reduce-scatter.20.cloned.1.call-update) | async-done | bytes 262160 | tf_op jit(solution)/shard_map/reduce_scatter | solution.py:481
  807.2 73.6 %reduce-scatter.18.cloned.1.call-done = bf16[64,2048]{1,0:T(8,128)(2,1)} async-done(((bf16[1024,2048]{1,0:T(8,128)(2,1)}), bf16[64,2048]{1,0:T(8,128)(2,1)}) %reduce-scatter.18.cloned.1.call-update) | async-done | bytes 262160 | tf_op jit(solution)/shard_map/reduce_scatter | solution.py:481
  882.6 74.3 %reduce-scatter.16.cloned.1.call-done = bf16[64,2048]{1,0:T(8,128)(2,1)} async-done(((bf16[1024,2048]{1,0:T(8,128)(2,1)}), bf16[64,2048]{1,0:T(8,128)(2,1)}) %reduce-scatter.16.cloned.1.call-update) | async-done | bytes 262160 | tf_op jit(solution)/shard_map/reduce_scatter | solution.py:481
  958.7 73.4 %reduce-scatter.14.cloned.1.call-done = bf16[64,2048]{1,0:T(8,128)(2,1)} async-done(((bf16[1024,2048]{1,0:T(8,128)(2,1)}), bf16[64,2048]{1,0:T(8,128)(2,1)}) %reduce-scatter.14.cloned.1.call-update) | async-done | bytes 262160 | tf_op jit(solution)/shard_map/reduce_scatter | solution.py:481
  (360 shorter events, 230.7 us)
Async XLA Ops:
  7.3 166.4 %all-gather.6.cloned.1.call-start = ((), (), s32[]{:S(2)}) async-start(), calls=%async_computation.10 | async-start | bytes 13369344 | tf_op jit(solution)/shard_map/all_gather | solution.py:254
  9.4 231.3 %all-gather.4.cloned.1.call-start = ((), (), s32[]{:S(2)}) async-start(), calls=%async_computation.8 | async-start | bytes 13369344 | tf_op jit(solution)/shard_map/all_gather | solution.py:307
  10.5 23.4 %collective-permute-start = (bf16[192,1024]{1,0:T(8,128)(2,1)S(1)}, bf16[192,1024]{1,0:T(8,128)(2,1)}, u32[]{:S(2)}, u32[]{:S(2)}) collective-permute-start(bf16[192,1024]{1,0:T(8,128)(2,1)S(1)} %fusion.68), channel_id=1, source_target_pairs={{0,4},{4,0},{1,5},{5,1},{2,6},{6,2},{3,7},{7,3},{8,12},{12,8},{9,1... | collective-permute-start | bytes 1179656 | tf_op jit(solution)/shard_map/ppermute | solution.py:209
  13.8 20.1 %collective-permute-start.1 = (f32[192]{0:T(256)S(1)}, f32[192]{0:T(256)S(1)}, u32[]{:S(2)}, u32[]{:S(2)}) collective-permute-start(f32[192]{0:T(256)S(1)} %add_rsqrt_fusion.1), channel_id=1, source_target_pairs={{0,4},{4,0},{1,5},{5,1},{2,6},{6,2},{3,7},{7,3},{8,12},{12,8},{9,1... | collective-permute-start | bytes 2312 | tf_op jit(solution)/shard_map/ppermute | solution.py:209
  37.0 20.7 %collective-permute-start.5 = (bf16[192,2048]{1,0:T(8,128)(2,1)}, bf16[192,2048]{1,0:T(8,128)(2,1)S(1)}, u32[]{:S(2)}, u32[]{:S(2)}) collective-permute-start(bf16[192,2048]{1,0:T(8,128)(2,1)} %convolution_convert_fusion.8), channel_id=1, source_target_pairs={{0,4},{4,0},{1,5},{5,1},{2,6},{6,2},{3,7},{7,3},{8,12},{12,8},{9,1... | collective-permute-start | bytes 2359304 | tf_op jit(solution)/shard_map/ppermute | solution.py:209
  42.5 32.1 %collective-permute-start.3 = (bf16[192,2048]{1,0:T(8,128)(2,1)S(1)}, bf16[192,2048]{1,0:T(8,128)(2,1)S(1)}, u32[]{:S(2)}, u32[]{:S(2)}) collective-permute-start(bf16[192,2048]{1,0:T(8,128)(2,1)S(1)} %convolution_convert_fusion.9), channel_id=1, source_target_pairs={{0,4},{4,0},{1,5},{5,1},{2,6},{6,2},{3,7},{7,3},{8,12},{12,8},{9,1... | collective-permute-start | bytes 2359304 | tf_op jit(solution)/shard_map/ppermute | solution.py:209
  45.9 45.6 %collective-permute-start.2 = (bf16[192,2048]{1,0:T(8,128)(2,1)}, bf16[192,2048]{1,0:T(8,128)(2,1)}, u32[]{:S(2)}, u32[]{:S(2)}) collective-permute-start(bf16[192,2048]{1,0:T(8,128)(2,1)} %convolution_convert_fusion.10), channel_id=1, source_target_pairs={{0,4},{4,0},{1,5},{5,1},{2,6},{6,2},{3,7},{7,3},{8,12},{12,8},{9,1... | collective-permute-start | bytes 2359304 | tf_op jit(solution)/shard_map/ppermute | solution.py:209
  58.8 38.3 %collective-permute-start.6 = (bf16[64,2048]{1,0:T(8,128)(2,1)}, bf16[64,2048]{1,0:T(8,128)(2,1)}, u32[]{:S(2)}, u32[]{:S(2)}) collective-permute-start(bf16[64,2048]{1,0:T(8,128)(2,1)} %get-tuple-element.67), channel_id=1, source_target_pairs={{0,4},{4,0},{1,5},{5,1},{2,6},{6,2},{3,7},{7,3},{8,12},{12,8},{9,1... | collective-permute-start | bytes 786440 | tf_op jit(solution)/shard_map/ppermute | solution.py:209
  76.8 24.2 %collective-permute-start.4 = (bf16[64,2048]{1,0:T(8,128)(2,1)S(1)}, bf16[64,2048]{1,0:T(8,128)(2,1)S(1)}, u32[]{:S(2)}, u32[]{:S(2)}) collective-permute-start(bf16[64,2048]{1,0:T(8,128)(2,1)S(1)} %get-tuple-element.69), channel_id=1, source_target_pairs={{0,4},{4,0},{1,5},{5,1},{2,6},{6,2},{3,7},{7,3},{8,12},{12,8},{9,1... | collective-permute-start | bytes 786440 | tf_op jit(solution)/shard_map/ppermute | solution.py:209
  105.9 9.7 collective-permute-start.7
  116.6 17.2 %collective-permute-start.8 = (bf16[192,2048]{1,0:T(8,128)(2,1)S(1)}, bf16[192,2048]{1,0:T(8,128)(2,1)S(1)}, u32[]{:S(2)}, u32[]{:S(2)}) collective-permute-start(bf16[192,2048]{1,0:T(8,128)(2,1)S(1)} %convolution_convert_fusion.7), channel_id=1, source_target_pairs={{0,4},{4,0},{1,5},{5,1},{2,6},{6,2},{3,7},{7,3},{8,12},{12,8},{9,1... | collective-permute-start | bytes 2359304 | tf_op jit(solution)/shard_map/ppermute | solution.py:209
  138.7 317.7 %reduce-scatter.12.cloned.1.call-start = ((), (), s32[]{:S(2)}) async-start(), calls=%async_computation.11 | async-start | bytes 13369344 | tf_op jit(solution)/shard_map/reduce_scatter | solution.py:376
  323.3 446.8 %reduce-scatter.10.cloned.1.call-start = ((), (), s32[]{:S(2)}) async-start(), calls=%async_computation.9 | async-start | bytes 13369344 | tf_op jit(solution)/shard_map/reduce_scatter | solution.py:396
  346.8 10.0 all-to-all-start
  350.3 426.3 %reduce-scatter.22.cloned.1.call-start = ((), (), s32[]{:S(2)}) async-start(), calls=%async_computation.16 | async-start | bytes 1081344
  463.3 18.8 %collective-permute-start.9 = (bf16[192,2048]{1,0:T(8,128)(2,1)}, bf16[192,2048]{1,0:T(8,128)(2,1)}, u32[]{:S(2)}, u32[]{:S(2)}) collective-permute-start(bf16[192,2048]{1,0:T(8,128)(2,1)} %fusion.111), channel_id=1, source_target_pairs={{0,4},{4,0},{1,5},{5,1},{2,6},{6,2},{3,7},{7,3},{8,12},{12,8},{9,1... | collective-permute-start | bytes 2359304 | tf_op jit(solution)/shard_map/ppermute | solution.py:209
  486.5 12.1 %collective-permute-start.10 = (bf16[192,1024]{1,0:T(8,128)(2,1)S(1)}, bf16[192,1024]{1,0:T(8,128)(2,1)S(1)}, u32[]{:S(2)}, u32[]{:S(2)}) collective-permute-start(bf16[192,1024]{1,0:T(8,128)(2,1)S(1)} %convolution_convert_fusion.11), channel_id=1, source_target_pairs={{0,4},{4,0},{1,5},{5,1},{2,6},{6,2},{3,7},{7,3},{8,12},{12,8},{9,1... | collective-permute-start | bytes 1179656 | tf_op jit(solution)/shard_map/ppermute | solution.py:209
  488.9 101.2 %collective-permute-start.18 = (bf16[192,1024]{1,0:T(8,128)(2,1)}, bf16[192,1024]{1,0:T(8,128)(2,1)}, u32[]{:S(2)}, u32[]{:S(2)}) collective-permute-start(bf16[192,1024]{1,0:T(8,128)(2,1)} %pad_maximum_fusion.6), channel_id=1, source_target_pairs={{0,4},{4,0},{1,5},{5,1},{2,6},{6,2},{3,7},{7,3},{8,12},{12,8},{9,1... | collective-permute-start | bytes 1179656 | tf_op jit(solution)/shard_map/ppermute | solution.py:209
  511.3 9.3 collective-permute-start.11
  517.0 9.3 collective-permute-start.12
  518.9 24.4 %collective-permute-start.14 = (bf16[192,2048]{1,0:T(8,128)(2,1)S(1)}, bf16[192,2048]{1,0:T(8,128)(2,1)}, u32[]{:S(2)}, u32[]{:S(2)}) collective-permute-start(bf16[192,2048]{1,0:T(8,128)(2,1)S(1)} %get-tuple-element.32), channel_id=1, source_target_pairs={{0,4},{4,0},{1,5},{5,1},{2,6},{6,2},{3,7},{7,3},{8,12},{12,8},{9,1... | collective-permute-start | bytes 2359304 | tf_op jit(solution)/shard_map/ppermute | solution.py:209
  522.6 52.2 %collective-permute-start.13 = (bf16[192,2048]{1,0:T(8,128)(2,1)}, bf16[192,2048]{1,0:T(8,128)(2,1)}, u32[]{:S(2)}, u32[]{:S(2)}) collective-permute-start(bf16[192,2048]{1,0:T(8,128)(2,1)} %pad_maximum_fusion.3), channel_id=1, source_target_pairs={{0,4},{4,0},{1,5},{5,1},{2,6},{6,2},{3,7},{7,3},{8,12},{12,8},{9,1... | collective-permute-start | bytes 2359304 | tf_op jit(solution)/shard_map/ppermute | solution.py:209
  529.0 44.2 %collective-permute-start.15 = (bf16[192,2048]{1,0:T(8,128)(2,1)S(1)}, bf16[192,2048]{1,0:T(8,128)(2,1)S(1)}, u32[]{:S(2)}, u32[]{:S(2)}) collective-permute-start(bf16[192,2048]{1,0:T(8,128)(2,1)S(1)} %get-tuple-element.35), channel_id=1, source_target_pairs={{0,4},{4,0},{1,5},{5,1},{2,6},{6,2},{3,7},{7,3},{8,12},{12,8},{9,1... | collective-permute-start | bytes 2359304 | tf_op jit(solution)/shard_map/ppermute | solution.py:209
  577.5 7.8 collective-permute-start.16
  589.7 215.7 %reduce-scatter.20.cloned.1.call-start = ((), (), s32[]{:S(2)}) async-start(), calls=%async_computation.15 | async-start | bytes 4456448 | tf_op jit(solution)/shard_map/reduce_scatter | solution.py:481
  596.1 284.7 %reduce-scatter.18.cloned.1.call-start = ((), (), s32[]{:S(2)}) async-start(), calls=%async_computation.14 | async-start | bytes 4456448 | tf_op jit(solution)/shard_map/reduce_scatter | solution.py:481
  597.6 7.8 collective-permute-start.17
  611.8 345.1 %reduce-scatter.16.cloned.1.call-start = ((), (), s32[]{:S(2)}) async-start(), calls=%async_computation.13 | async-start | bytes 4456448 | tf_op jit(solution)/shard_map/reduce_scatter | solution.py:481
  618.5 413.6 %reduce-scatter.14.cloned.1.call-start = ((), (), s32[]{:S(2)}) async-start(), calls=%async_computation.12 | async-start | bytes 4456448 | tf_op jit(solution)/shard_map/reduce_scatter | solution.py:481
  627.6 51.0 %collective-permute-start.20 = (bf16[512,2048]{1,0:T(8,128)(2,1)}, bf16[512,2048]{1,0:T(8,128)(2,1)}, u32[]{:S(2)}, u32[]{:S(2)}) collective-permute-start(bf16[512,2048]{1,0:T(8,128)(2,1)} %convolution_convert_fusion.5), channel_id=1, source_target_pairs={{0,4},{4,0},{1,5},{5,1},{2,6},{6,2},{3,7},{7,3},{8,12},{12,8},{9,1... | collective-permute-start | bytes 6291464 | tf_op jit(solution)/shard_map/ppermute | solution.py:209
  636.7 88.9 %collective-permute-start.19 = (bf16[512,2048]{1,0:T(8,128)(2,1)}, bf16[512,2048]{1,0:T(8,128)(2,1)}, u32[]{:S(2)}, u32[]{:S(2)}) collective-permute-start(bf16[512,2048]{1,0:T(8,128)(2,1)} %convolution_convert_fusion.6), channel_id=1, source_target_pairs={{0,4},{4,0},{1,5},{5,1},{2,6},{6,2},{3,7},{7,3},{8,12},{12,8},{9,1... | collective-permute-start | bytes 6291464 | tf_op jit(solution)/shard_map/ppermute | solution.py:209
  652.1 112.3 %collective-permute-start.21 = (bf16[512,2048]{1,0:T(8,128)(2,1)S(1)}, bf16[512,2048]{1,0:T(8,128)(2,1)S(1)}, u32[]{:S(2)}, u32[]{:S(2)}) collective-permute-start(bf16[512,2048]{1,0:T(8,128)(2,1)S(1)} %convolution_convert_fusion.4), channel_id=1, source_target_pairs={{0,4},{4,0},{1,5},{5,1},{2,6},{6,2},{3,7},{7,3},{8,12},{12,8},{9,1... | collective-permute-start | bytes 6291464 | tf_op jit(solution)/shard_map/ppermute | solution.py:209
  (93 other events, 2442.7 us)
Sparse Core Ops, SparseCore 0:
  10.4 103.4 all-gather.5
  138.8 101.8 all-gather.3
  323.4 132.9 reduce-scatter.11
  460.3 133.8 reduce-scatter.9
  596.3 136.3 reduce-scatter.21
  737.0 68.4 reduce-scatter.19
  809.3 71.5 reduce-scatter.17
  885.2 71.7 reduce-scatter.15
  960.8 71.2 reduce-scatter.13

commit v2 on v1

--- a/solution.py
+++ b/solution.py
@@ -163,6 +163,197 @@
         compiler_params=pltpu.CompilerParams(vmem_limit_bytes=VMEM_LIMIT),
         name=name,
     )(meta, *arrays)
+
+
+def expert_kernel(*refs):
+    refs = refs[:10] + refs[-10:]
+    (
+        x0_ref, x1_ref, x2_ref, x3_ref, pick_ref, plain_ref, gate_w_ref, up_w_ref, router_ref, mine_ref,
+        in_ref, act_ref, dg_ref, du_ref, prob_ref,
+        keep_ref, send_ref, dprob_ref,
+        total_ref, dp_ref,
+    ) = refs
+    step = pl.program_id(0)
+    slots = pick_ref.shape[1]
+
+    @pl.when(step == 0)
+    def _():
+        for s, x_ref in enumerate((x0_ref, x1_ref, x2_ref, x3_ref)):
+            in_ref[s * slots : (s + 1) * slots, :] = dot(pick_ref[s], x_ref[...]).astype(BF16)
+        logits = dot(in_ref[...], router_ref[...])
+        exponent = jnp.exp(logits - jnp.max(logits, axis=1, keepdims=True))
+        total = jnp.sum(exponent, axis=1, keepdims=True)
+        prob_ref[...] = jnp.sum(exponent * mine_ref[...], axis=1, keepdims=True) / total
+
+    rows = in_ref[...]
+    gate_w, up_w = gate_w_ref[...], up_w_ref[...]
+    gate_pre = dot(rows, gate_w, NT)
+    up_pre = dot(rows, up_w, NT)
+    plain = plain_ref[...]
+    sigmoid = 1.0 / (1.0 + jnp.exp(-gate_pre))
+    silu = gate_pre * sigmoid
+    act = (silu * up_pre).astype(BF16)
+    act_ref[...] = act
+    d_act = prob_ref[...] * plain
+    d_gate = (d_act * up_pre * (sigmoid * (1.0 + gate_pre * (1.0 - sigmoid)))).astype(BF16)
+    d_up = (d_act * silu).astype(BF16)
+    dg_ref[...] = d_gate
+    du_ref[...] = d_up
+    d_prob = jnp.sum(act.astype(F32) * plain, axis=1, keepdims=True)
+    d_in = dot(d_gate, gate_w) + dot(d_up, up_w)
+
+    @pl.when(step == 0)
+    def _():
+        dp_ref[...] = d_prob
+        total_ref[...] = d_in
+
+    @pl.when(step > 0)
+    def _():
+        dp_ref[...] += d_prob
+        total_ref[...] += d_in
+
+    @pl.when(step == pl.num_programs(0) - 1)
+    def _():
+        values = total_ref[...].astype(BF16)
+        for s in range(4):
+            at = slice(s * slots, (s + 1) * slots)
+            (keep_ref, send_ref)[s % 2][s // 2] = dot(pick_ref[s], values[at, :], TN).astype(BF16)
+            dprob_ref[s : s + 1, :] = jnp.sum(
+                pick_ref[s].astype(F32) * dp_ref[at, :], axis=0, keepdims=True
+            )
+
+
+def expert_quarter(quarter, blocks, pick, plain, gate_w, up_w, router, mine, kept):
+    tokens, width = blocks[0].shape
+    hidden = gate_w.shape[0]
+    tile = 256
+    slots = pick.shape[1]
+    rows = 4 * slots
+    whole = lambda *shape: pl.BlockSpec(shape, lambda f: (0,) * len(shape))
+    any_spec = pl.BlockSpec(memory_space=pl.ANY)
+    pair = jax.ShapeDtypeStruct((2, tokens, width), BF16)
+    tiled = pl.BlockSpec((rows, tile), lambda f: (quarter, f))
+    every = pick.shape[0] * slots
+    return pl.pallas_call(
+        expert_kernel,
+        grid=(hidden // tile,),
+        in_specs=[whole(tokens, width)] * 4
+        + [
+            pl.BlockSpec((4, slots, tokens), lambda f: (quarter, 0, 0)),
+            tiled,
+            pl.BlockSpec((tile, width), lambda f: (f, 0)),
+            pl.BlockSpec((tile, width), lambda f: (f, 0)),
+            whole(*router.shape),
+            whole(*mine.shape),
+        ]
+        + [any_spec] * len(kept),
+        out_specs=[
+            pl.BlockSpec((rows, width), lambda f: (quarter, 0)),
+            tiled,
+            tiled,
+            tiled,
+            pl.BlockSpec((rows, 1), lambda f: (quarter, 0)),
+        ]
+        + [whole(2, tokens, width)] * 2
+        + [whole(4, tokens)],
+        out_shape=[
+            jax.ShapeDtypeStruct((every, width), BF16),
+            jax.ShapeDtypeStruct((every, hidden), BF16),
+            jax.ShapeDtypeStruct((every, hidden), BF16),
+            jax.ShapeDtypeStruct((every, hidden), BF16),
+            jax.ShapeDtypeStruct((every, 1), F32),
+            pair,
+            pair,
+            jax.ShapeDtypeStruct((4, tokens), F32),
+        ],
+        scratch_shapes=[pltpu.VMEM((rows, width), F32), pltpu.VMEM((rows, 1), F32)],
+        input_output_aliases={10 + k: k for k in range(len(kept))},
+        compiler_params=pltpu.CompilerParams(vmem_limit_bytes=VMEM_LIMIT),
+        name="expert",
+    )(*blocks, pick, plain, gate_w, up_w, router, mine, *kept)
+
+
+def expert_out_kernel(source_ref, pick_ref, act_ref, down_ref, prob_ref, out_ref, values_ref):
+    s = pl.program_id(1)
+
+    @pl.when(s == 0)
+    def _():
+        values = (prob_ref[...] * dot(act_ref[...], down_ref[...])).astype(BF16)
+        values_ref[...] = values.reshape(values_ref.shape)
+
+    out_ref[0] = dot(pick_ref[0], values_ref[s], TN).astype(BF16)
+
+
+def expert_out(source, pick, act, down_w, prob):
+    hidden, width = down_w.shape
+    owners, slots, tokens = pick.shape
+    rows = 4 * slots
+    return pl.pallas_call(
+        expert_out_kernel,
+        grid_spec=pltpu.PrefetchScalarGridSpec(
+            num_scalar_prefetch=1,
+            grid=(owners // 4, 4),
+            in_specs=[
+                pl.BlockSpec((1, slots, tokens), lambda q, s, m: (4 * q + s, 0, 0)),
+                pl.BlockSpec((rows, hidden), lambda q, s, m: (q, 0)),
+                pl.BlockSpec((hidden, width), lambda q, s, m: (0, 0)),
+                pl.BlockSpec((rows, 1), lambda q, s, m: (q, 0)),
+            ],
+            out_specs=pl.BlockSpec((1, tokens, width), lambda q, s, m: (m[4 * q + s], 0, 0)),
+            scratch_shapes=[pltpu.VMEM((4, slots, width), BF16)],
+        ),
+        out_shape=jax.ShapeDtypeStruct((owners, tokens, width), BF16),
+        compiler_params=pltpu.CompilerParams(vmem_limit_bytes=VMEM_LIMIT),
+        name="expert_out",
+    )(source, pick, act, down_w, prob)
+
+
+def swap(value, axis, bit):
+    return lax.ppermute(value, axis, [(i, i ^ bit) for i in range(lax.axis_size(axis))])
+
+
+def plus(*values):
+    return sum(v.astype(F32) for v in values).astype(values[0].dtype)
+
+
+ORDER = [
+    (i, j) for x in (0, 2) for z in (0, 2) for i in (z, z + 1) for j in (x, x + 1)
+]
+
+
+def fence(*values):
+    return lax.optimization_barrier(values)
+
+
+def split(value, axis_name, bit, at):
+    mine = (lax.axis_index(axis_name) // bit) % 2
+    shape = value.shape
+    pairs = value.reshape(shape[:at] + (shape[at] // 2, 2) + shape[at + 1 :])
+    keep = lax.dynamic_index_in_dim(pairs, mine, at + 1, keepdims=False)
+    send = lax.dynamic_index_in_dim(pairs, 1 - mine, at + 1, keepdims=False)
+    return keep, send
+
+
+STAGES = (("dp", 1, 1), ("dp", 2, 1), ("expert", 1, 0), ("expert", 2, 0))
+
+
+class RowScatter:
+    def __init__(self, value):
+        rows_e, rows_d = lax.axis_size("expert"), lax.axis_size("dp")
+        self.value = value.reshape((rows_e, rows_d, -1, value.shape[-1]))
+        self.stage = 0
+
+    def start(self):
+        axis, bit, at = STAGES[self.stage]
+        self.keep, send = split(self.value, axis, bit, at)
+        self.stage += 1
+        return swap(send, axis, bit)
+
+    def finish(self, received):
+        self.value = plus(self.keep, received)
+
+    def result(self):
+        return self.value.reshape(self.value.shape[-2:])
 
 
 def shards(
@@ -240,17 +431,27 @@
         for piece, inv in zip(x_blocks, inverses)
     ]
 
-    small = jnp.concatenate(
-        [jnp.stack([attn_gain, query_gain, key_gain, ffn_gain], axis=1), w_router], axis=1
-    )
-    small = lax.all_gather(small, "context", axis=0, tiled=True)
-    gains = small[:, :4].T.astype(F32)
+    def gathered(value, axis):
+        shape = list(value.shape)
+        shape[axis] = shape[axis] * planes
+        full = jnp.zeros(shape, value.dtype)
+        for r in range(planes):
+            piece = shift(value, r) if r else value
+            at = ((me - r) % planes) * value.shape[axis]
+            full = lax.dynamic_update_slice_in_dim(full, piece, at, axis=axis)
+        return full
+
+    gains = gathered(jnp.stack([attn_gain, query_gain, key_gain, ffn_gain]), 1).astype(F32)
     gain_attn, gain_query, gain_key, gain_ffn = [gains[i : i + 1] for i in range(4)]
-    full_router = small[:, 4:]
+    full_router = gathered(w_router, 0)
 
     d_out_low = jnp.concatenate([prompt_cot[0], cont_cot[0, 0]], axis=0)
     routes = jnp.concatenate([prompt_routes[0], cont_routes[0, 0]], axis=0)
-    all_routes = lax.all_gather(routes, PLANE, axis=0, tiled=True)
+    named = sum(
+        (routes[:, k : k + 1] == jnp.arange(expert_count, dtype=jnp.int32)[None, :]).astype(F32)
+        for k in range(top_count)
+    )
+    member = lax.all_to_all(named.T, PLANE, split_axis=0, concat_axis=0, tiled=True)
     all_cot = lax.all_gather(d_out_low, PLANE, axis=0, tiled=True)
 
     start_len = prefix[0, 0]
@@ -265,8 +466,10 @@
     meta = jnp.stack([me * prompt_dev, start_len]).astype(jnp.int32)
 
     def project(pieces, weight):
-        sent = [shift(dot(pieces[r], weight).astype(BF16), planes - r) for r in others]
-        return [dot(pieces[0], weight)] + sent
+        products = [dot(pieces[r], weight).astype(BF16) for r in others]
+        products = fence(pieces[0], *products)
+        sent = [shift(product, planes - r) for r, product in zip(others, products[1:])]
+        return [dot(products[0], weight)] + sent
 
     key_parts = project(normed_blocks, w_key)
     value_parts = project(normed_blocks, w_value)
@@ -304,21 +507,15 @@
     inverse2 = lax.rsqrt(jnp.mean(mixed_rows * mixed_rows, axis=-1, keepdims=True) + EPSILON)
     normed2_low = (mixed_rows * inverse2 * gain_ffn).astype(BF16)
 
-    all_normed2 = lax.all_gather(normed2_low, PLANE, axis=0, tiled=True)
-
     normed_low = (x_rows * inverse[:, None] * gain_attn).astype(BF16)
-    normed_out = jnp.concatenate(
-        [out_part(normed_low, 0)] + [shift(out_part(normed_low, r), r) for r in others], axis=0
-    )
-    attended_out = jnp.concatenate(
-        [out_part(attended, 0)] + [shift(out_part(attended, r), r) for r in others], axis=0
-    )
 
     logits = dot(normed2_low, full_router)
     shifted = jnp.exp(logits - jnp.max(logits, axis=1, keepdims=True))
     router_probs = shifted / jnp.sum(shifted, axis=1, keepdims=True)
 
-    member = jnp.sum((all_routes == my_expert).astype(F32), axis=1).reshape(owners, tokens)
+    my_e, my_d = lax.axis_index("expert"), lax.axis_index("dp")
+    source = jnp.stack([(my_e ^ i) * rows_d + (my_d ^ j) for i, j in ORDER]).astype(jnp.int32)
+    member = jnp.take(member, source, axis=0)
 
     def ranks(m):
         count = m.shape[1]
@@ -332,71 +529,100 @@
     pick = (
         slot_of[:, None, :] == jnp.arange(slots, dtype=F32)[None, :, None]
     ).astype(BF16)
-
-    def gather_rows(values):
-        picked = jnp.einsum(
-            "sjt,std->sjd",
-            pick,
-            values.reshape(owners, tokens, width),
-            preferred_element_type=BF16,
-        )
-        return picked.reshape(owners * slots, width)
-
-    def spread_rows(values):
-        return jnp.einsum(
-            "sjt,sjd->std",
-            pick,
-            values.reshape(owners, slots, width),
-            preferred_element_type=BF16,
-        ).reshape(owners * tokens, width)
-
     gate_w, up_w, down_w = expert_gate[0], expert_up[0], expert_down[0]
-    slot_cot = gather_rows(all_cot)
+    mine = (jnp.arange(expert_count, dtype=jnp.int32) == my_expert).astype(F32)[None, :]
+
+    def z1(v):
+        return swap(v, "expert", 1)
+
+    def z2(v):
+        return swap(v, "expert", 2)
+
+    def core(v):
+        return swap(v, "dp", 1)
+
+    def across(v):
+        return swap(v, "dp", 2)
+
+    b0, all_cot, normed_low = fence(normed2_low, all_cot, normed_low)
+    b1, b2, x0, c0 = z1(b0), z2(b0), across(b0), core(b0)
+    normed_sent = [shift(out_part(normed_low, r), r) for r in others]
+    all_cot = all_cot.reshape(owners, tokens, width)
+    slot_cot = jnp.concatenate(
+        [
+            dot(pick[b], lax.dynamic_index_in_dim(all_cot, source[b], 0, False), out=BF16)
+            for b in range(owners)
+        ],
+        axis=0,
+    )
     d_act_plain = dot(slot_cot, down_w, NT)
-
-    slot_in = gather_rows(all_normed2)
-    slot_logits = dot(slot_in, full_router)
-    slot_exp = jnp.exp(slot_logits - jnp.max(slot_logits, axis=1, keepdims=True))
-    is_mine = jnp.arange(expert_count, dtype=jnp.int32) == my_expert
-    slot_gate = jnp.sum(jnp.where(is_mine, slot_exp, 0.0), axis=1, keepdims=True) / jnp.sum(
-        slot_exp, axis=1, keepdims=True
-    )
-    gate_pre = dot(slot_in, gate_w, NT)
-    up_pre = dot(slot_in, up_w, NT)
-    sigmoid = jax.nn.sigmoid(gate_pre)
-    silu = gate_pre * sigmoid
-    act_low = (silu * up_pre).astype(BF16)
-    d_act = slot_gate * d_act_plain
-    d_gate = (d_act * up_pre * (sigmoid * (1.0 + gate_pre * (1.0 - sigmoid)))).astype(BF16)
-    d_up = (d_act * silu).astype(BF16)
-    slot_dprob = jnp.sum(act_low.astype(F32) * d_act_plain, axis=1).reshape(owners, slots)
-    token_dprob = jnp.sum(pick.astype(F32) * slot_dprob[:, :, None], axis=1)
+    b1, b2, x0, c0, d_act_plain, attended, *normed_sent = fence(
+        b1, b2, x0, c0, d_act_plain, attended, *normed_sent
+    )
+    normed_out = jnp.concatenate([out_part(normed_low, 0)] + normed_sent, axis=0)
+    b3, x1, c1, x0c = z1(b2), across(b1), core(b1), core(x0)
+    attended_sent = [shift(out_part(attended, r), r) for r in others]
+    b3, x1, c1, x0c, *attended_sent = fence(b3, x1, c1, x0c, *attended_sent)
+    attended_out = jnp.concatenate([out_part(attended, 0)] + attended_sent, axis=0)
+
+    def quarter(q, blocks, kept):
+        outs = expert_quarter(q, blocks, pick, d_act_plain, gate_w, up_w, full_router, mine, kept)
+        return outs[:5], outs[5], outs[6], outs[7]
+
+    x2, c2, c3, x1c = across(b2), core(b2), core(b3), core(x1)
+    kept, keep0, send0, dprob0 = quarter(0, (b0, c0, b1, c1), ())
+    x2, c2, c3, x1c, *kept = fence(x2, c2, c3, x1c, *kept)
+    x3, x2c = across(b3), core(x2)
+    kept, keep2, send2, dprob2 = quarter(2, (x0, x0c, x1, x1c), kept)
+    x3, x2c, send2, *kept = fence(x3, x2c, send2, *kept)
+    x3c, near2 = core(x3), core(send2)
+    x3c, near2, *kept = fence(x3c, near2, *kept)
+    got2 = across(plus(keep2, near2))
+    kept, keep1, send1, dprob1 = quarter(1, (b2, c2, b3, c3), kept)
+    kept, keep3, send3, dprob3 = quarter(3, (x2, x2c, x3, x3c), kept)
+    got2, send0, send1, send3, *kept = fence(got2, send0, send1, send3, *kept)
+    slot_in, act_low, d_gate, d_up, slot_gate = kept
+
+    piece = hidden // planes
+
+    def grad_rows(left, right, r):
+        cols = lax.dynamic_slice_in_dim(left, ((me + r) % planes) * piece, piece, axis=1)
+        return dot(cols, right, TN)
+
+    def grad_low(left, right):
+        return [grad_rows(left, right, r).astype(BF16) for r in others]
+
+    def send_rows(values, low, high):
+        at = slice(piece * low // 4, piece * high // 4)
+        return [shift(v[at], r) for r, v in zip(others, values)]
+
+    near0, near1, near3 = core(send0), core(send1), core(send3)
+    gate_low = grad_low(d_gate, slot_in)
+    near0, near1, near3, *gate_low = fence(near0, near1, near3, *gate_low)
+    first = plus(keep0, near0, got2)
+    got3, first_got = across(plus(keep3, near3)), z1(first[1])
+    gate_a = send_rows(gate_low, 0, 3)
+    up_low = grad_low(d_up, slot_in)
+    place = jnp.zeros((owners,), jnp.int32).at[source].set(jnp.arange(owners, dtype=jnp.int32))
+    token_dprob = jnp.take(
+        jnp.concatenate([dprob0, dprob1, dprob2, dprob3], axis=0), place, axis=0
+    )
     dprobs = lax.all_to_all(token_dprob, PLANE, split_axis=0, concat_axis=0, tiled=True).T
-    d_input = (dot(d_gate, gate_w) + dot(d_up, up_w)).astype(BF16)
-    d_normed2_moe = lax.psum_scatter(
-        spread_rows(d_input), PLANE, scatter_dimension=0, tiled=True
-    ).astype(F32)
-
+    got3, first_got, dprobs, *rest = fence(got3, first_got, dprobs, *gate_a, *up_low)
+    gate_a, up_low = rest[: planes - 1], rest[planes - 1 :]
+    second = plus(keep1, near1, got3)
+    second_got = z1(second[1])
+    gate_b = send_rows(gate_low, 3, 4)
+    up_a = send_rows(up_low, 0, 1)
     slot_dy = (slot_gate * slot_cot.astype(F32)).astype(BF16)
-    piece = hidden // planes
-
-    def expert_grad(left, right):
-        def rows(r):
-            cols = lax.dynamic_slice_in_dim(left, ((me + r) % planes) * piece, piece, axis=1)
-            return dot(cols, right, TN)
-
-        sent = [shift(rows(r).astype(BF16), r) for r in others]
-        return rows(0) + sum(s.astype(F32) for s in sent)
-
-    gate_grad = expert_grad(d_gate, slot_in)
-    up_grad = expert_grad(d_up, slot_in)
-    down_grad = expert_grad(act_low, slot_dy)
-
-    slot_out = (slot_gate * dot(act_low, down_w)).astype(BF16)
-    moe_out = lax.psum_scatter(
-        spread_rows(slot_out), PLANE, scatter_dimension=0, tiled=True
-    ).astype(F32)
-    out_rows = mixed_rows + moe_out
+    down_low = grad_low(act_low, slot_dy)
+    second_got, *rest = fence(second_got, *gate_b, *up_a, *down_low)
+    gate_b, up_a, down_low = (rest[k * (planes - 1) : (k + 1) * (planes - 1)] for k in range(3))
+    far_got = z2(plus(second[0], second_got))
+    up_b = send_rows(up_low, 1, 4)
+    slot_out = expert_out(source, pick, act_low, down_w, slot_gate)
+    far_got, slot_out, *up_b = fence(far_got, slot_out, *up_b)
+    d_normed2_moe = first[0].astype(F32) + first_got.astype(F32) + far_got.astype(F32)
 
     d_out = d_out_low.astype(F32)
     dlogit_low = (
@@ -410,18 +636,28 @@
     ffn_gain_grad = jnp.sum(d_normed2 * mixed_rows * inverse2, axis=0)
 
     branch_low = d_mixed.astype(BF16)
+    branch_low, slot_out = fence(branch_low, slot_out)
+    moe_out = lax.psum_scatter(
+        slot_out.reshape(owners * tokens, width), PLANE, scatter_dimension=0, tiled=True
+    ).astype(F32)
+    out_rows = mixed_rows + moe_out
     branches = [branch_low] + [shift(branch_low, r) for r in others]
-
-    def back_blocks(pairs_of):
-        sent = [shift(pairs_of(r).astype(BF16), planes - r) for r in others]
-        return [pairs_of(0)] + sent
-
-    d_attended = placed(
-        [p.astype(BF16) for p in back_blocks(lambda r: dot(branches[r], w_output, NT))]
-    )
-    output_grad = dot(attended_out, jnp.concatenate(branches, axis=0), TN).astype(BF16)
+    gate_own = grad_rows(d_gate, slot_in, 0)
+    up_own = grad_rows(d_up, slot_in, 0)
+    *branches, gate_own, up_own = fence(*branches, gate_own, up_own)
+    blocks_low = [dot(branches[r], w_output, NT).astype(BF16) for r in others]
+    blocks_low = fence(*blocks_low)
+    d_att_blocks = [dot(branches[0], w_output, NT).astype(BF16)] + [
+        shift(v, planes - r) for r, v in zip(others, blocks_low)
+    ]
+    output_rows = RowScatter(dot(attended_out, jnp.concatenate(branches, axis=0), TN).astype(BF16))
+    output_got = output_rows.start()
+    output_got, *d_att_blocks = fence(output_got, *d_att_blocks)
+    output_rows.finish(output_got)
+    d_attended = placed(d_att_blocks)
 
     key_total = prompt_total + cont_len
+    output_got = output_rows.start()
     d_queries, d_keys_all, d_values_all = attention_call(
         attend_back_kernel,
         "attend_back",
@@ -452,35 +688,65 @@
     d_key_low, key_gain_grad = qk_post_back(
         own_keys(d_keys_all), key_raw, gain_key, cosine, sine
     )
+    output_got, d_value_low, d_query_low, d_key_low = fence(
+        output_got, d_value_low, d_query_low, d_key_low
+    )
+    output_rows.finish(output_got)
 
     def spread(low):
-        return [low] + [shift(low, r) for r in others]
-
-    d_values, d_query_rows, d_key_rows = spread(d_value_low), spread(d_query_low), spread(d_key_low)
-    d_normed = placed(
-        [
-            p.astype(F32)
-            for p in back_blocks(
-                lambda r: dot(d_values[r], w_value, NT)
-                + dot(d_query_rows[r], w_query, NT)
-                + dot(d_key_rows[r], w_key, NT)
-            )
-        ]
-    )
-    value_grad = dot(normed_out, jnp.concatenate(d_values, axis=0), TN).astype(BF16)
-    query_grad = dot(normed_out, jnp.concatenate(d_query_rows, axis=0), TN).astype(BF16)
-    key_grad = dot(normed_out, jnp.concatenate(d_key_rows, axis=0), TN).astype(BF16)
-
+        return [shift(low, r) for r in others]
+
+    def weight_rows(own, got):
+        return RowScatter(dot(normed_out, jnp.concatenate([own, *got], axis=0), TN).astype(BF16))
+
+    got, output_got = spread(d_value_low), output_rows.start()
+    output_got, *d_values = fence(output_got, *got)
+    output_rows.finish(output_got)
+
+    value_rows = weight_rows(d_value_low, d_values)
+    got, output_got, value_got = spread(d_query_low), output_rows.start(), value_rows.start()
+    output_got, value_got, *d_query_got = fence(output_got, value_got, *got)
+    output_rows.finish(output_got)
+    value_rows.finish(value_got)
+
+    query_rows = weight_rows(d_query_low, d_query_got)
+    got, value_got, query_got = spread(d_key_low), value_rows.start(), query_rows.start()
+    partial = [
+        dot(d_values[k], w_value, NT) + dot(d_query_got[k], w_query, NT) for k in range(planes - 1)
+    ]
+    rest = fence(value_got, query_got, *got, *partial)
+    value_got, query_got = rest[:2]
+    d_key_got, partial = rest[2 : planes + 1], rest[planes + 1 :]
+    value_rows.finish(value_got)
+    query_rows.finish(query_got)
+
+    blocks_low = [
+        (partial[k] + dot(d_key_got[k], w_key, NT)).astype(BF16) for k in range(planes - 1)
+    ]
+    query_got, value_got = query_rows.start(), value_rows.start()
+    d_normed_got = [shift(v, planes - r) for r, v in zip(others, blocks_low)]
+    down_a = send_rows(down_low, 0, 1)
+    key_rows = weight_rows(d_key_low, d_key_got)
+    key_got = key_rows.start()
+    d_normed_own = (
+        dot(d_value_low, w_value, NT) + dot(d_query_low, w_query, NT) + dot(d_key_low, w_key, NT)
+    )
+    query_got, value_got, key_got, d_normed_own, *rest = fence(
+        query_got, value_got, key_got, d_normed_own, *d_normed_got, *down_a
+    )
+    d_normed_got, down_a = rest[: planes - 1], rest[planes - 1 :]
+    query_rows.finish(query_got)
+    value_rows.finish(value_got)
+    key_rows.finish(key_got)
+
+    d_normed = placed([d_normed_own] + [p.astype(F32) for p in d_normed_got])
+    key_got, query_got, value_got = key_rows.start(), query_rows.start(), value_rows.start()
+    down_b = send_rows(down_low, 1, 3)
     scaled = gain_attn * d_normed
     centre = jnp.mean(scaled * x_rows, axis=-1, keepdims=True)
     inv = inverse[:, None]
     d_x = d_mixed + inv * scaled - x_rows * (inv**3 * centre)
     attn_gain_grad = jnp.sum(d_normed * x_rows * inv, axis=0)
-
-    def scatter(value):
-        return lax.psum_scatter(value, PLANE, scatter_dimension=0, tiled=True).astype(F32)
-
-    everywhere = ("expert", "context", "dp")
     small_grads = jnp.concatenate(
         [
             jnp.stack([attn_gain_grad, query_gain_grad[0], key_gain_grad[0], ffn_gain_grad], axis=1),
@@ -488,7 +754,41 @@
         ],
         axis=1,
     )
-    small_grads = lax.psum_scatter(small_grads, everywhere, scatter_dimension=0, tiled=True)
+    by_plane = small_grads.reshape(rows_e, planes, out_group, small_grads.shape[1])
+
+    def plane_rows(r):
+        return lax.dynamic_index_in_dim(by_plane, (me + r) % planes, 1, False)
+
+    small_rows = RowScatter(plus(plane_rows(0), *[shift(plane_rows(r), r) for r in others]))
+    small_rows.finish(small_rows.start())
+    key_got, query_got, value_got, small_rows.value, *down_b = fence(
+        key_got, query_got, value_got, small_rows.value, *down_b
+    )
+    key_rows.finish(key_got)
+    query_rows.finish(query_got)
+    value_rows.finish(value_got)
+
+    key_got, query_got = key_rows.start(), query_rows.start()
+    small_rows.finish(small_rows.start())
+    down_c = send_rows(down_low, 3, 4)
+    down_own = grad_rows(act_low, slot_dy, 0)
+    key_got, query_got, small_rows.value, down_own, *down_c = fence(
+        key_got, query_got, small_rows.value, down_own, *down_c
+    )
+    key_rows.finish(key_got)
+    query_rows.finish(query_got)
+    key_rows.finish(key_rows.start())
+    small_rows.finish(small_rows.start())
+    small_rows.finish(small_rows.start())
+    small_grads = small_rows.result()
+
+    def total(own, *parts):
+        cuts = [jnp.concatenate([p[k] for p in parts], axis=0) for k in range(planes - 1)]
+        return own + sum(c.astype(F32) for c in cuts)
+
+    gate_grad = total(gate_own, gate_a, gate_b)
+    up_grad = total(up_own, up_a, up_b)
+    down_grad = total(down_own, down_a, down_b, down_c)
     return (
         out_rows[:prompt_dev].astype(BF16)[None],
         out_rows[prompt_dev:].astype(BF16)[None, None],
@@ -498,10 +798,10 @@
         small_grads[:, 1],
         small_grads[:, 2],
         small_grads[:, 3],
-        scatter(query_grad),
-        scatter(key_grad),
-        scatter(value_grad),
-        scatter(output_grad),
+        query_rows.result().astype(F32),
+        key_rows.result().astype(F32),
+        value_rows.result().astype(F32),
+        output_rows.result().astype(F32),
         small_grads[:, 4:],
         gate_grad[None],
         up_grad[None],

time: 1050 us -> 747 us (0.71)
  waiting for transfers between devices: 642 us -> 308 us
  matrix products: 223 us -> 122 us
  Pallas kernels: 22.7 us -> 116 us
  blocking collectives: 43.1 us -> 0 us
  starting transfers between devices: 31.3 us -> 71.5 us
  other arithmetic: 28.8 us -> 55.4 us
  local copies, waits for them, and re-layouts: 34.3 us -> 48 us
    reduce_scatter x6 -> x1, waiting for transfers between devices: 344 us -> 0.01 us  [shards(): lax.psum_scatter(slot_out.reshape(owners * tokens, width), PLANE, scatter...]
    ppermute x0 -> x44, waiting for transfers between devices: none -> 157 us  [swap(): lax.ppermute(value, axis, [(i, i ^ bit) for i in range(lax.axis_size(axis...]
    ppermute x22 -> x29, waiting for transfers between devices: 235 us -> 140 us  [shift(): lax.ppermute(value, 'context', [(i, (i + r) % planes) for i in range(plan...]
    pallas_call x0 -> x5, Pallas kernels: none -> 94.5 us  [the longest x4 72.7 us: expert_quarter(): pl.pallas_call(expert_kernel, grid=(hidden // tile,), in_specs=[whole(tok...]
    dot_general x38 -> x48, matrix products: 191 us -> 122 us  [dot(): lax.dot_general(left, right, (dims, ((), ())), preferred_element_type=out)]
    all_gather x1 -> x0, waiting for transfers between devices: 56.3 us -> none  [shards(): all_normed2 = lax.all_gather(normed2_low, PLANE, axis=0, tiled=True)]
    all_gather x2 -> x0, blocking collectives: 43.1 us -> none  [the longest x1 34.3 us: shards(): all_routes = lax.all_gather(routes, PLANE, axis=0, tiled=True)]
    dot_general x4 -> x0, matrix products: 31.8 us -> none  [the longest x2 17.6 us: gather_rows(): jnp.einsum('sjt,std->sjd', pick, values.reshape(owners, tokens, width), p...]
  transfers between devices with their start and end apart: 32 -> 77, of which waited for: 24 -> 38; matrix products, arithmetic and copies ran while one was open for 18% -> 25% of each run, Pallas kernels for 2% -> 14%
where the time goes in v2:
time: 747 us; the launch traced here: 738 us
  waiting for transfers between devices  308 us (41%)
  matrix products  122 us (16%)
  Pallas kernels  116 us (16%)
  starting transfers between devices  71.5 us (10%)
  other arithmetic  55.4 us (7%)
  local copies, waits for them, and re-layouts  48 us (6%)
  between operations  17.6 us (2%)
    ppermute x44, waiting for transfers between devices, swap(): lax.ppermute(value, axis, [(i, i ^ bit) for i in range(lax.axis_size(axis...  157 us
    ppermute x29, waiting for transfers between devices, shift(): lax.ppermute(value, 'context', [(i, (i + r) % planes) for i in range(plan...  140 us
    dot_general x48, matrix products, dot(): lax.dot_general(left, right, (dims, ((), ())), preferred_element_type=out)  122 us
    pallas_call x4, Pallas kernels, expert_quarter(): pl.pallas_call(expert_kernel, grid=(hidden // tile,), in_specs=[whole(tok...  72.7 us
    ppermute x29, starting transfers between devices, shift(): lax.ppermute(value, 'context', [(i, (i + r) % planes) for i in range(plan...  32.8 us
    ppermute x44, starting transfers between devices, swap(): lax.ppermute(value, axis, [(i, i ^ bit) for i in range(lax.axis_size(axis...  28.8 us
    convert_element_type x17, other arithmetic, plus(): return sum((v.astype(F32) for v in values)).astype(values[0].dtype)  25 us
    pallas_call x1, Pallas kernels, expert_out(): pl.pallas_call(expert_out_kernel, grid_spec=pltpu.PrefetchScalarGridSpec(...  21.8 us
  transfers between devices with their start and end apart: 77, of which 38 were waited for; matrix products, arithmetic and copies ran while one was open for 25% of the time, Pallas kernels for 14%

profile of v2, /device:TPU:0, one launch (start us, length us, event | category | flops | bytes accessed | tf_op | source)
XLA Modules:
  0.0 738.1 jit_solution(3390390205214496242)
XLA Ops:
  42.3 10.8 %collective-permute-done.6 = bf16[192,2048]{1,0:T(8,128)(2,1)S(1)} collective-permute-done((bf16[192,2048]{1,0:T(8,128)(2,1)S(1)}, bf16[192,2048]{1,0:T(8,128)(2,1)S(1)}, u32[]{:S(2)}, u32[]{:S(2)}) %collective-permute-start.6) | collective-permute-done | bytes 786464 | tf_op jit(solution)/shard_map/ppermute | solution.py:400
  54.3 15.8 %collective-permute-done.4.refs_1_ = bf16[192,2048]{1,0:T(8,128)(2,1)S(1)} collective-permute-done((bf16[192,2048]{1,0:T(8,128)(2,1)S(1)}, bf16[192,2048]{1,0:T(8,128)(2,1)S(1)}, u32[]{:S(2)}, u32[]{:S(2)}) %collective-permute-start.4) | collective-permute-done | bytes 786464 | tf_op jit(solution)/shard_map/ppermute | solution.py:400
  73.0 13.8 %collective-permute-done.2.refs_1_ = bf16[192,2048]{1,0:T(8,128)(2,1)S(1)} collective-permute-done((bf16[192,2048]{1,0:T(8,128)(2,1)S(1)}, bf16[192,2048]{1,0:T(8,128)(2,1)S(1)}, u32[]{:S(2)}, u32[]{:S(2)}) %collective-permute-start.2) | collective-permute-done | bytes 786464 | tf_op jit(solution)/shard_map/ppermute | solution.py:400
  103.1 9.2 %collective-permute-done.8 = bf16[192,1024]{1,0:T(8,128)(2,1)S(1)} collective-permute-done((bf16[192,1024]{1,0:T(8,128)(2,1)S(1)}, bf16[192,1024]{1,0:T(8,128)(2,1)S(1)}, u32[]{:S(2)}, u32[]{:S(2)}) %collective-permute-start.8) | collective-permute-done | bytes 393248 | tf_op jit(solution)/shard_map/ppermute | solution.py:400
  115.9 15.0 %collective-permute-done.9 = bf16[192,2048]{1,0:T(8,128)(2,1)S(1)} collective-permute-done((bf16[192,2048]{1,0:T(8,128)(2,1)S(1)}, bf16[192,2048]{1,0:T(8,128)(2,1)S(1)}, u32[]{:S(2)}, u32[]{:S(2)}) %collective-permute-start.9) | collective-permute-done | bytes 786464 | tf_op jit(solution)/shard_map/ppermute | solution.py:400
  162.8 10.8 %fusion.145.refs_5_ = f32[1792,1024]{1,0:T(8,128)} fusion(bf16[1792,2048]{1,0:T(8,128)(2,1)S(1)} %convolution_dynamic-update-slice_fusion, bf16[1,1024,2048]{2,1,0:T(8,128)(2,1)S(1)} %copy-done.55), kind=kOutput, calls=%fused_computation.400 | convolution fusion | flops 7516192768 | bytes 18874368 | tf_op jit(solution)/shard_map/dot_general | solution.py:20
  178.5 9.3 %collective-permute-done.19 = bf16[192,1024]{1,0:T(8,128)(2,1)S(1)} collective-permute-done((bf16[192,1024]{1,0:T(8,128)(2,1)S(1)}, bf16[192,1024]{1,0:T(8,128)(2,1)S(1)}, u32[]{:S(2)}, u32[]{:S(2)}) %collective-permute-start.19) | collective-permute-done | bytes 393248 | tf_op jit(solution)/shard_map/ppermute | solution.py:400
  198.9 6.5 collective-permute-done.20
  208.0 17.4 %expert.4 = (bf16[1792,2048]{1,0:T(8,128)(2,1)}, bf16[1792,1024]{1,0:T(8,128)(2,1)}, bf16[1792,1024]{1,0:T(8,128)(2,1)}, bf16[1792,1024]{1,0:T(8,128)(2,1)}, f32...) custom-call(bf16[192,2048]{1,0:T(8,128)(2,1)S(1)} %multiply_convert_fu, ...), custom_call_target="tpu_custom_call" | custom-call | tf_op jit(solution)/shard_map/expert/pallas_call | solution.py:237
  225.5 18.1 %expert.5 = (bf16[1792,2048]{1,0:T(8,128)(2,1)}, bf16[1792,1024]{1,0:T(8,128)(2,1)}, bf16[1792,1024]{1,0:T(8,128)(2,1)}, bf16[1792,1024]{1,0:T(8,128)(2,1)}, f32...) custom-call(bf16[192,2048]{1,0:T(8,128)(2,1)S(1)} %copy-done.19, ...), custom_call_target="tpu_custom_call", output_to_operand_aliasing={{0}: (10, {}), {1}: (11, {}), {2}: (12, {}), {3}: (13, {}),... | custom-call | tf_op jit(solution)/shard_map/expert/pallas_call | solution.py:237
  253.5 19.2 %expert.6 = (bf16[1792,2048]{1,0:T(8,128)(2,1)}, bf16[1792,1024]{1,0:T(8,128)(2,1)}, bf16[1792,1024]{1,0:T(8,128)(2,1)}, bf16[1792,1024]{1,0:T(8,128)(2,1)}, f32...) custom-call(bf16[192,2048]{1,0:T(8,128)(2,1)} %collective-permute-do, ...), custom_call_target="tpu_custom_call", output_to_operand_aliasing={{0}: (10, {}), {1}: (11, {}), {2}: (12, {}), {3}: (13, {}),... | custom-call | tf_op jit(solution)/shard_map/expert/pallas_call | solution.py:237
  272.8 18.0 %expert.7 = (bf16[1792,2048]{1,0:T(8,128)(2,1)}, bf16[1792,1024]{1,0:T(8,128)(2,1)}, bf16[1792,1024]{1,0:T(8,128)(2,1)}, bf16[1792,1024]{1,0:T(8,128)(2,1)}, f32...) custom-call(bf16[192,2048]{1,0:T(8,128)(2,1)} %collective-permute-do, ...), custom_call_target="tpu_custom_call", output_to_operand_aliasing={{0}: (10, {}), {1}: (11, {}), {2}: (12, {}), {3}: (13, {}),... | custom-call | tf_op jit(solution)/shard_map/expert/pallas_call | solution.py:237
  297.0 6.4 all-to-all-done.1
  303.8 7.8 %convolution_convert_fusion.6 = bf16[512,2048]{1,0:T(8,128)(2,1)S(1)} fusion(bf16[1792,2048]{1,0:T(8,128)(2,1)} %get-tuple-element.247, bf16[1792,1024]{1,0:T(8,128)(2,1)} %get-tuple-element.246, s32[]{:T(128)S(6)} %select_n.398), kind=kOutput, calls=%fused_computation.31 | convolution fusion | flops 3759144960 | bytes 11272196 | tf_op jit(solution)/shard_map/dot_general | solution.py:20
  325.2 12.8 %collective-permute-done.34 = bf16[192,2048]{1,0:T(8,128)(2,1)S(1)} collective-permute-done((bf16[192,2048]{1,0:T(8,128)(2,1)S(1)}, bf16[192,2048]{1,0:T(8,128)(2,1)S(1)}, u32[]{:S(2)}, u32[]{:S(2)}) %collective-permute-start.34) | collective-permute-done | bytes 786464 | tf_op jit(solution)/shard_map/ppermute | solution.py:312
  338.0 11.9 %collective-permute-done.33 = bf16[2,192,2048]{2,1,0:T(8,128)(2,1)S(1)} collective-permute-done((bf16[2,192,2048]{2,1,0:T(8,128)(2,1)S(1)}, bf16[2,192,2048]{2,1,0:T(8,128)(2,1)S(1)}, u32[]{:S(2)}, u32[]{:S(2)}) %collective-permute-start.33) | collective-permute-done | bytes 1572896 | tf_op jit(solution)/shard_map/ppermute | solution.py:312
  357.5 8.5 %convolution_convert_fusion.4 = bf16[512,2048]{1,0:T(8,128)(2,1)} fusion(bf16[1792,2048]{1,0:T(8,128)(2,1)} %copy-done.92, f32[1792]{0:T(1024)S(1)} %reduce, bf16[1792,1024]{1,0:T(8,128)(2,1)S(1)} %copy-done, s32[]{:T(128)S(6)} %select_n.398), kind=kOutput, calls=%fused_computation.29 | convolution fusion | flops 3770155008 | bytes 11280388 | tf_op jit(solution)/shard_map/dot_general | solution.py:20
  381.7 21.8 %expert_out.1 = bf16[16,192,2048]{2,1,0:T(8,128)(2,1)} custom-call(s32[16]{0:T(128)S(1)} %stack.131.source_ref, bf16[16,112,192]{2,1,0:T(8,128)(2,1)S(1)} %get-tuple-element.373.refs_4_.pick_ref, bf16[1792,1024]{1,0:T(8,128)(2,1)S(1)} %copy-done, bf16[1024,2048]{1,0:T(8,128)(2,1)} %bitcast.387, f32[1792,1]{1,0:T(8,128)S(1)} %get-tuple-element.264.prob_ref), custom_call_target="tpu_custom_call" | custom-call | tf_op jit(solution)/shard_map/expert_out/pallas_call | solution.py:291
  403.6 7.2 collective-permute-done.39
  421.8 12.1 %collective-permute-done.41 = bf16[192,2048]{1,0:T(8,128)(2,1)S(1)} collective-permute-done((bf16[192,2048]{1,0:T(8,128)(2,1)S(1)}, bf16[192,2048]{1,0:T(8,128)(2,1)S(1)}, u32[]{:S(2)}, u32[]{:S(2)}) %collective-permute-start.41) | collective-permute-done | bytes 786464 | tf_op jit(solution)/shard_map/ppermute | solution.py:400
  444.2 8.8 %fusion.4 = f32[512,2048]{1,0:T(8,128)} fusion(bf16[1792,2048]{1,0:T(8,128)(2,1)} %copy-done.92, f32[1792]{0:T(1024)S(1)} %reduce, bf16[1792,1024]{1,0:T(8,128)(2,1)S(1)} %copy-done.1, s32[]{:T(128)S(6)} %select_n.404), kind=kOutput, calls=%fused_computation.32 | convolution fusion | flops 3769106432 | bytes 13377540 | tf_op jit(solution)/shard_map/dot_general | solution.py:20
  456.1 11.1 %attend_back.1 = (f32[192,2048]{1,0:T(8,128)S(1)}, f32[256,2048]{1,0:T(8,128)}, f32[256,2048]{1,0:T(8,128)}) custom-call(s32[2]{0:T(128)S(1)} %pad_add_fusion.1.meta_ref, bf16[192,2048]{1,0:T(8,128)(2,1)S(1)} %copy-done.7, bf16[256,2048]{1,0:T(8,128)(2,1)S(1)} %copy-done.5, bf16[256,2048]{1,0:T(8,128)(2,1)S(1)} %copy-done.3, ...), custom_call_target="tpu_custom_call" | custom-call | tf_op jit(solution)/shard_map/attend_back/pallas_call | solution.py:154
  484.2 15.0 %collective-permute-done.44 = bf16[4,1,64,2048]{3,2,0,1:T(8,128)(2,1)S(1)} collective-permute-done((bf16[4,1,64,2048]{3,2,0,1:T(8,128)(2,1)S(1)}, bf16[4,1,64,2048]{3,2,0,1:T(8,128)(2,1)S(1)}, u32[]{:S(2)}, u32[]{:S(2)}) %collective-permute-start.44) | collective-permute-done | bytes 1048608 | tf_op jit(solution)/shard_map/ppermute | solution.py:312
  507.5 7.1 collective-permute-done.47
  546.2 12.2 %collective-permute-done.51 = bf16[192,2048]{1,0:T(8,128)(2,1)S(1)} collective-permute-done((bf16[192,2048]{1,0:T(8,128)(2,1)S(1)}, bf16[192,2048]{1,0:T(8,128)(2,1)S(1)}, u32[]{:S(2)}, u32[]{:S(2)}) %collective-permute-start.51) | collective-permute-done | bytes 786464 | tf_op jit(solution)/shard_map/ppermute | solution.py:400
  558.4 9.4 %collective-permute-done.49 = bf16[1,1,64,2048]{3,2,0,1:T(8,128)(2,1)S(1)} collective-permute-done((bf16[1,1,64,2048]{3,2,0,1:T(8,128)(2,1)S(1)}, bf16[1,1,64,2048]{3,2,0,1:T(8,128)(2,1)S(1)}, u32[]{:S(2)}, u32[]{:S(2)}) %collective-permute-start.49) | collective-permute-done | bytes 262176 | tf_op jit(solution)/shard_map/ppermute | solution.py:312
  584.8 24.9 %collective-permute-done.52 = bf16[4,1,64,2048]{3,2,0,1:T(8,128)(2,1)S(1)} collective-permute-done((bf16[4,1,64,2048]{3,2,0,1:T(8,128)(2,1)S(1)}, bf16[4,1,64,2048]{3,2,0,1:T(8,128)(2,1)S(1)}, u32[]{:S(2)}, u32[]{:S(2)}) %collective-permute-start.52) | collective-permute-done | bytes 1048608 | tf_op jit(solution)/shard_map/ppermute | solution.py:312
  620.4 8.9 %collective-permute-done.58 = bf16[192,1024]{1,0:T(8,128)(2,1)S(1)} collective-permute-done((bf16[192,1024]{1,0:T(8,128)(2,1)S(1)}, bf16[192,1024]{1,0:T(8,128)(2,1)S(1)}, u32[]{:S(2)}, u32[]{:S(2)}) %collective-permute-start.58) | collective-permute-done | bytes 393248 | tf_op jit(solution)/shard_map/ppermute | solution.py:400
  629.4 20.4 %collective-permute-done.55 = bf16[4,1,64,2048]{3,2,0,1:T(8,128)(2,1)S(1)} collective-permute-done((bf16[4,1,64,2048]{3,2,0,1:T(8,128)(2,1)S(1)}, bf16[4,1,64,2048]{3,2,0,1:T(8,128)(2,1)S(1)}, u32[]{:S(2)}, u32[]{:S(2)}) %collective-permute-start.55) | collective-permute-done | bytes 1048608 | tf_op jit(solution)/shard_map/ppermute | solution.py:312
  674.9 9.5 %collective-permute-done.61 = bf16[2,1,64,2048]{3,2,0,1:T(8,128)(2,1)} collective-permute-done((bf16[2,1,64,2048]{3,2,0,1:T(8,128)(2,1)}, bf16[2,1,64,2048]{3,2,0,1:T(8,128)(2,1)}, u32[]{:S(2)}, u32[]{:S(2)}) %collective-permute-start.61) | collective-permute-done | bytes 524320 | tf_op jit(solution)/shard_map/ppermute | solution.py:312
  696.0 6.8 collective-permute-done.67
  702.8 7.3 collective-permute-done.66
  (584 shorter events, 326.5 us)
Async XLA Ops:
  7.2 126.8 %all-gather.2.cloned.1.call-start = ((), (), s32[]{:S(2)}) async-start(), calls=%async_computation.3 | async-start | bytes 13369344 | tf_op jit(solution)/shard_map/all_gather | solution.py:455
  35.7 34.3 %collective-permute-start.4 = (bf16[192,2048]{1,0:T(8,128)(2,1)S(1)}, bf16[192,2048]{1,0:T(8,128)(2,1)S(1)}, u32[]{:S(2)}, u32[]{:S(2)}) collective-permute-start(bf16[192,2048]{1,0:T(8,128)(2,1)S(1)} %convolution_convert_fusion.9), channel_id=1, source_target_pairs={{0,4},{4,0},{1,5},{5,1},{2,6},{6,2},{3,7},{7,3},{8,12},{12,8},{9,1... | collective-permute-start | bytes 2359304 | tf_op jit(solution)/shard_map/ppermute | solution.py:400
  39.1 47.8 %collective-permute-start.2 = (bf16[192,2048]{1,0:T(8,128)(2,1)S(1)}, bf16[192,2048]{1,0:T(8,128)(2,1)S(1)}, u32[]{:S(2)}, u32[]{:S(2)}) collective-permute-start(bf16[192,2048]{1,0:T(8,128)(2,1)S(1)} %convolution_convert_fusion.10), channel_id=1, source_target_pairs={{0,4},{4,0},{1,5},{5,1},{2,6},{6,2},{3,7},{7,3},{8,12},{12,8},{9,1... | collective-permute-start | bytes 2359304 | tf_op jit(solution)/shard_map/ppermute | solution.py:400
  53.6 38.9 %collective-permute-start.7 = (bf16[64,2048]{1,0:T(8,128)(2,1)S(1)}, bf16[64,2048]{1,0:T(8,128)(2,1)S(1)}, u32[]{:S(2)}, u32[]{:S(2)}) collective-permute-start(bf16[64,2048]{1,0:T(8,128)(2,1)S(1)} %get-tuple-element.363), channel_id=1, source_target_pairs={{0,4},{4,0},{1,5},{5,1},{2,6},{6,2},{3,7},{7,3},{8,12},{12,8},{9,1... | collective-permute-start | bytes 786440 | tf_op jit(solution)/shard_map/ppermute | solution.py:400
  71.3 25.6 %collective-permute-start.5 = (bf16[64,2048]{1,0:T(8,128)(2,1)S(1)}, bf16[64,2048]{1,0:T(8,128)(2,1)S(1)}, u32[]{:S(2)}, u32[]{:S(2)}) collective-permute-start(bf16[64,2048]{1,0:T(8,128)(2,1)S(1)} %get-tuple-element.365), channel_id=1, source_target_pairs={{0,4},{4,0},{1,5},{5,1},{2,6},{6,2},{3,7},{7,3},{8,12},{12,8},{9,1... | collective-permute-start | bytes 786440 | tf_op jit(solution)/shard_map/ppermute | solution.py:400
  134.0 39.7 %collective-permute-start.10 = (bf16[192,2048]{1,0:T(8,128)(2,1)S(1)}, bf16[192,2048]{1,0:T(8,128)(2,1)S(1)}, u32[]{:S(2)}, u32[]{:S(2)}) collective-permute-start(bf16[192,2048]{1,0:T(8,128)(2,1)S(1)} %multiply_convert_fusion.3.refs_0_), channel_id=1, source_target_pairs={{0,8},{8,0},{16,24},{24,16},{1,9},{9,1},{17,25},{25,17},{2,10},{10... | collective-permute-start | bytes 2359304 | tf_op jit(solution)/shard_map/ppermute | solution.py:312
  135.2 38.5 %collective-permute-start.11 = (bf16[192,2048]{1,0:T(8,128)(2,1)S(1)}, bf16[192,2048]{1,0:T(8,128)(2,1)}, u32[]{:S(2)}, u32[]{:S(2)}) collective-permute-start(bf16[192,2048]{1,0:T(8,128)(2,1)S(1)} %multiply_convert_fusion.3.refs_0_), channel_id=1, source_target_pairs={{0,16},{8,24},{16,0},{24,8},{1,17},{9,25},{17,1},{25,9},{2,18},{10... | collective-permute-start | bytes 2359304 | tf_op jit(solution)/shard_map/ppermute | solution.py:312
  136.6 37.1 %collective-permute-start.12 = (bf16[192,2048]{1,0:T(8,128)(2,1)S(1)}, bf16[192,2048]{1,0:T(8,128)(2,1)S(1)}, u32[]{:S(2)}, u32[]{:S(2)}) collective-permute-start(bf16[192,2048]{1,0:T(8,128)(2,1)S(1)} %multiply_convert_fusion.3.refs_0_), channel_id=1, source_target_pairs={{0,2},{1,3},{2,0},{3,1},{4,6},{5,7},{6,4},{7,5},{8,10},{9,11},{10,... | collective-permute-start | bytes 2359304 | tf_op jit(solution)/shard_map/ppermute | solution.py:312
  138.3 35.4 %collective-permute-start.13 = (bf16[192,2048]{1,0:T(8,128)(2,1)S(1)}, bf16[192,2048]{1,0:T(8,128)(2,1)S(1)}, u32[]{:S(2)}, u32[]{:S(2)}) collective-permute-start(bf16[192,2048]{1,0:T(8,128)(2,1)S(1)} %multiply_convert_fusion.3.refs_0_), channel_id=1, source_target_pairs={{0,1},{1,0},{2,3},{3,2},{4,5},{5,4},{6,7},{7,6},{8,9},{9,8},{10,11... | collective-permute-start | bytes 2359304 | tf_op jit(solution)/shard_map/ppermute | solution.py:312
  139.1 34.5 %collective-permute-start.14 = (bf16[192,1024]{1,0:T(8,128)(2,1)S(1)}, bf16[192,1024]{1,0:T(8,128)(2,1)S(1)}, u32[]{:S(2)}, u32[]{:S(2)}) collective-permute-start(bf16[192,1024]{1,0:T(8,128)(2,1)S(1)} %pad_maximum_fusion.5), channel_id=1, source_target_pairs={{0,4},{4,0},{1,5},{5,1},{2,6},{6,2},{3,7},{7,3},{8,12},{12,8},{9,1... | collective-permute-start | bytes 1179656 | tf_op jit(solution)/shard_map/ppermute | solution.py:400
  187.8 37.6 %collective-permute-start.21 = (bf16[192,2048]{1,0:T(8,128)(2,1)}, bf16[192,2048]{1,0:T(8,128)(2,1)}, u32[]{:S(2)}, u32[]{:S(2)}) collective-permute-start(bf16[192,2048]{1,0:T(8,128)(2,1)} %collective-permute-done.11.refs_0_), channel_id=1, source_target_pairs={{0,2},{1,3},{2,0},{3,1},{4,6},{5,7},{6,4},{7,5},{8,10},{9,11},{10,... | collective-permute-start | bytes 2359304 | tf_op jit(solution)/shard_map/ppermute | solution.py:312
  193.8 31.6 %collective-permute-start.22 = (bf16[192,2048]{1,0:T(8,128)(2,1)}, bf16[192,2048]{1,0:T(8,128)(2,1)}, u32[]{:S(2)}, u32[]{:S(2)}) collective-permute-start(bf16[192,2048]{1,0:T(8,128)(2,1)} %collective-permute-done.11.refs_0_), channel_id=1, source_target_pairs={{0,1},{1,0},{2,3},{3,2},{4,5},{5,4},{6,7},{7,6},{8,9},{9,8},{10,11... | collective-permute-start | bytes 2359304 | tf_op jit(solution)/shard_map/ppermute | solution.py:312
  196.4 29.0 %collective-permute-start.23 = (bf16[192,2048]{1,0:T(8,128)(2,1)}, bf16[192,2048]{1,0:T(8,128)(2,1)}, u32[]{:S(2)}, u32[]{:S(2)}) collective-permute-start(bf16[192,2048]{1,0:T(8,128)(2,1)} %collective-permute-done.15.refs_2_), channel_id=1, source_target_pairs={{0,1},{1,0},{2,3},{3,2},{4,5},{5,4},{6,7},{7,6},{8,9},{9,8},{10,11... | collective-permute-start | bytes 2359304 | tf_op jit(solution)/shard_map/ppermute | solution.py:312
  196.4 29.0 %collective-permute-start.24 = (bf16[192,2048]{1,0:T(8,128)(2,1)}, bf16[192,2048]{1,0:T(8,128)(2,1)}, u32[]{:S(2)}, u32[]{:S(2)}) collective-permute-start(bf16[192,2048]{1,0:T(8,128)(2,1)} %collective-permute-done.16.refs_2_), channel_id=1, source_target_pairs={{0,1},{1,0},{2,3},{3,2},{4,5},{5,4},{6,7},{7,6},{8,9},{9,8},{10,11... | collective-permute-start | bytes 2359304 | tf_op jit(solution)/shard_map/ppermute | solution.py:312
  205.5 38.2 %collective-permute-start.25 = (bf16[192,2048]{1,0:T(8,128)(2,1)}, bf16[192,2048]{1,0:T(8,128)(2,1)S(1)}, u32[]{:S(2)}, u32[]{:S(2)}) collective-permute-start(bf16[192,2048]{1,0:T(8,128)(2,1)} %collective-permute-done.15.refs_2_), channel_id=1, source_target_pairs={{0,2},{1,3},{2,0},{3,1},{4,6},{5,7},{6,4},{7,5},{8,10},{9,11},{10,... | collective-permute-start | bytes 2359304 | tf_op jit(solution)/shard_map/ppermute | solution.py:312
  251.9 38.9 %collective-permute-start.29 = (bf16[2,192,2048]{2,1,0:T(8,128)(2,1)}, bf16[2,192,2048]{2,1,0:T(8,128)(2,1)}, u32[]{:S(2)}, u32[]{:S(2)}) collective-permute-start(bf16[2,192,2048]{2,1,0:T(8,128)(2,1)} %add_convert_fusion.3), channel_id=1, source_target_pairs={{0,2},{1,3},{2,0},{3,1},{4,6},{5,7},{6,4},{7,5},{8,10},{9,11},{10,... | collective-permute-start | bytes 4718600 | tf_op jit(solution)/shard_map/ppermute | solution.py:312
  296.9 427.7 %reduce-scatter.2.cloned.1.call-start = ((), (), s32[]{:S(2)}) async-start(), calls=%async_computation.4 | async-start | bytes 13369344 | tf_op jit(solution)/shard_map/reduce_scatter | solution.py:640
  313.8 36.1 %collective-permute-start.33 = (bf16[2,192,2048]{2,1,0:T(8,128)(2,1)S(1)}, bf16[2,192,2048]{2,1,0:T(8,128)(2,1)S(1)}, u32[]{:S(2)}, u32[]{:S(2)}) collective-permute-start(bf16[2,192,2048]{2,1,0:T(8,128)(2,1)S(1)} %add_convert_fusion.1), channel_id=1, source_target_pairs={{0,2},{1,3},{2,0},{3,1},{4,6},{5,7},{6,4},{7,5},{8,10},{9,11},{10,... | collective-permute-start | bytes 4718600 | tf_op jit(solution)/shard_map/ppermute | solution.py:312
  314.4 37.3 %collective-permute-start.35 = (bf16[384,2048]{1,0:T(8,128)(2,1)S(1)}, bf16[384,2048]{1,0:T(8,128)(2,1)S(1)}, u32[]{:S(2)}, u32[]{:S(2)}) collective-permute-start(bf16[384,2048]{1,0:T(8,128)(2,1)S(1)} %slice.211), channel_id=1, source_target_pairs={{0,4},{4,0},{1,5},{5,1},{2,6},{6,2},{3,7},{7,3},{8,12},{12,8},{9,1... | collective-permute-start | bytes 4718600 | tf_op jit(solution)/shard_map/ppermute | solution.py:400
  324.3 43.6 %collective-permute-start.37 = (bf16[128,2048]{1,0:T(8,128)(2,1)S(1)}, bf16[128,2048]{1,0:T(8,128)(2,1)S(1)}, u32[]{:S(2)}, u32[]{:S(2)}) collective-permute-start(bf16[128,2048]{1,0:T(8,128)(2,1)S(1)} %slice.214), channel_id=1, source_target_pairs={{0,4},{4,0},{1,5},{5,1},{2,6},{6,2},{3,7},{7,3},{8,12},{12,8},{9,1... | collective-permute-start | bytes 1572872 | tf_op jit(solution)/shard_map/ppermute | solution.py:400
  367.4 43.4 %collective-permute-start.40 = (bf16[384,2048]{1,0:T(8,128)(2,1)}, bf16[384,2048]{1,0:T(8,128)(2,1)}, u32[]{:S(2)}, u32[]{:S(2)}) collective-permute-start(bf16[384,2048]{1,0:T(8,128)(2,1)} %slice.216), channel_id=1, source_target_pairs={{0,4},{4,0},{1,5},{5,1},{2,6},{6,2},{3,7},{7,3},{8,12},{12,8},{9,1... | collective-permute-start | bytes 4718600 | tf_op jit(solution)/shard_map/ppermute | solution.py:400
  375.4 35.3 %collective-permute-start.39 = (bf16[192,2048]{1,0:T(8,128)(2,1)}, bf16[192,2048]{1,0:T(8,128)(2,1)}, u32[]{:S(2)}, u32[]{:S(2)}) collective-permute-start(bf16[192,2048]{1,0:T(8,128)(2,1)} %fusion.32), channel_id=1, source_target_pairs={{0,16},{8,24},{16,0},{24,8},{1,17},{9,25},{17,1},{25,9},{2,18},{10... | collective-permute-start | bytes 2359304 | tf_op jit(solution)/shard_map/ppermute | solution.py:312
  505.9 113.2 %collective-permute-start.59 = (bf16[128,2048]{1,0:T(8,128)(2,1)}, bf16[128,2048]{1,0:T(8,128)(2,1)}, u32[]{:S(2)}, u32[]{:S(2)}) collective-permute-start(bf16[128,2048]{1,0:T(8,128)(2,1)} %get-tuple-element.341), channel_id=1, source_target_pairs={{0,4},{4,0},{1,5},{5,1},{2,6},{6,2},{3,7},{7,3},{8,12},{12,8},{9,1... | collective-permute-start | bytes 1572872 | tf_op jit(solution)/shard_map/ppermute | solution.py:400
  527.0 40.8 %collective-permute-start.50 = (bf16[4,2,64,2048]{3,2,0,1:T(8,128)(2,1)}, bf16[4,2,64,2048]{3,2,0,1:T(8,128)(2,1)}, u32[]{:S(2)}, u32[]{:S(2)}) collective-permute-start(bf16[4,2,64,2048]{3,2,0,1:T(8,128)(2,1)} %bitcast.336), channel_id=1, source_target_pairs={{0,1},{1,0},{2,3},{3,2},{4,5},{5,4},{6,7},{7,6},{8,9},{9,8},{10,11... | collective-permute-start | bytes 6291464 | tf_op jit(solution)/shard_map/ppermute | solution.py:312
  538.6 46.2 %collective-permute-start.54 = (bf16[192,2048]{1,0:T(8,128)(2,1)S(1)}, bf16[192,2048]{1,0:T(8,128)(2,1)S(1)}, u32[]{:S(2)}, u32[]{:S(2)}) collective-permute-start(bf16[192,2048]{1,0:T(8,128)(2,1)S(1)} %get-tuple-element.292), channel_id=1, source_target_pairs={{0,4},{4,0},{1,5},{5,1},{2,6},{6,2},{3,7},{7,3},{8,12},{12,8},{9,1... | collective-permute-start | bytes 2359304 | tf_op jit(solution)/shard_map/ppermute | solution.py:400
  541.3 26.5 %collective-permute-start.49 = (bf16[1,1,64,2048]{3,2,0,1:T(8,128)(2,1)S(1)}, bf16[1,1,64,2048]{3,2,0,1:T(8,128)(2,1)S(1)}, u32[]{:S(2)}, u32[]{:S(2)}) collective-permute-start(bf16[1,1,64,2048]{3,2,0,1:T(8,128)(2,1)S(1)} %constant_dynamic-slice_fusion.21), channel_id=1, source_target_pairs={{0,16},{8,24},{16,0},{24,8},{1,17},{9,25},{17,1},{25,9},{2,18},{10... | collective-permute-start | bytes 786440 | tf_op jit(solution)/shard_map/ppermute | solution.py:312
  571.0 38.7 %collective-permute-start.53 = (bf16[4,2,64,2048]{3,2,0,1:T(8,128)(2,1)S(1)}, bf16[4,2,64,2048]{3,2,0,1:T(8,128)(2,1)S(1)}, u32[]{:S(2)}, u32[]{:S(2)}) collective-permute-start(bf16[4,2,64,2048]{3,2,0,1:T(8,128)(2,1)S(1)} %bitcast.404), channel_id=1, source_target_pairs={{0,1},{1,0},{2,3},{3,2},{4,5},{5,4},{6,7},{7,6},{8,9},{9,8},{10,11... | collective-permute-start | bytes 6291464 | tf_op jit(solution)/shard_map/ppermute | solution.py:312
  577.1 32.7 %collective-permute-start.52 = (bf16[4,1,64,2048]{3,2,0,1:T(8,128)(2,1)S(1)}, bf16[4,1,64,2048]{3,2,0,1:T(8,128)(2,1)S(1)}, u32[]{:S(2)}, u32[]{:S(2)}) collective-permute-start(bf16[4,1,64,2048]{3,2,0,1:T(8,128)(2,1)S(1)} %constant_dynamic-slice_fusion.17), channel_id=1, source_target_pairs={{0,2},{1,3},{2,0},{3,1},{4,6},{5,7},{6,4},{7,5},{8,10},{9,11},{10,... | collective-permute-start | bytes 3145736 | tf_op jit(solution)/shard_map/ppermute | solution.py:312
  614.1 35.7 %collective-permute-start.57 = (bf16[4,2,64,2048]{3,2,0,1:T(8,128)(2,1)S(1)}, bf16[4,2,64,2048]{3,2,0,1:T(8,128)(2,1)S(1)}, u32[]{:S(2)}, u32[]{:S(2)}) collective-permute-start(bf16[4,2,64,2048]{3,2,0,1:T(8,128)(2,1)S(1)} %bitcast.403), channel_id=1, source_target_pairs={{0,1},{1,0},{2,3},{3,2},{4,5},{5,4},{6,7},{7,6},{8,9},{9,8},{10,11... | collective-permute-start | bytes 6291464 | tf_op jit(solution)/shard_map/ppermute | solution.py:312
  615.6 34.2 %collective-permute-start.55 = (bf16[4,1,64,2048]{3,2,0,1:T(8,128)(2,1)S(1)}, bf16[4,1,64,2048]{3,2,0,1:T(8,128)(2,1)S(1)}, u32[]{:S(2)}, u32[]{:S(2)}) collective-permute-start(bf16[4,1,64,2048]{3,2,0,1:T(8,128)(2,1)S(1)} %constant_dynamic-slice_fusion.15), channel_id=1, source_target_pairs={{0,2},{1,3},{2,0},{3,1},{4,6},{5,7},{6,4},{7,5},{8,10},{9,11},{10,... | collective-permute-start | bytes 3145736 | tf_op jit(solution)/shard_map/ppermute | solution.py:312
  619.2 50.2 %collective-permute-start.65 = (bf16[256,2048]{1,0:T(8,128)(2,1)}, bf16[256,2048]{1,0:T(8,128)(2,1)}, u32[]{:S(2)}, u32[]{:S(2)}) collective-permute-start(bf16[256,2048]{1,0:T(8,128)(2,1)} %slice.224), channel_id=1, source_target_pairs={{0,4},{4,0},{1,5},{5,1},{2,6},{6,2},{3,7},{7,3},{8,12},{12,8},{9,1... | collective-permute-start | bytes 3145736 | tf_op jit(solution)/shard_map/ppermute | solution.py:400
  667.9 28.0 %collective-permute-start.69 = (bf16[128,2048]{1,0:T(8,128)(2,1)}, bf16[128,2048]{1,0:T(8,128)(2,1)S(1)}, u32[]{:S(2)}, u32[]{:S(2)}) collective-permute-start(bf16[128,2048]{1,0:T(8,128)(2,1)} %get-tuple-element.340), channel_id=1, source_target_pairs={{0,4},{4,0},{1,5},{5,1},{2,6},{6,2},{3,7},{7,3},{8,12},{12,8},{9,1... | collective-permute-start | bytes 1572872 | tf_op jit(solution)/shard_map/ppermute | solution.py:400
  (156 other events, 1952.0 us)
Sparse Core Ops, SparseCore 0:
  10.9 103.4 all-gather.1
  507.6 164.8 reduce-scatter.1

commit v3 on v2

--- a/solution.py
+++ b/solution.py
@@ -1,4 +1,5 @@
 import functools
+import math
 
 import jax
 import jax.numpy as jnp
@@ -169,9 +170,9 @@
     refs = refs[:10] + refs[-10:]
     (
         x0_ref, x1_ref, x2_ref, x3_ref, pick_ref, plain_ref, gate_w_ref, up_w_ref, router_ref, mine_ref,
-        in_ref, act_ref, dg_ref, du_ref, prob_ref,
+        in_ref, act_ref, dg_ref, du_ref,
         keep_ref, send_ref, dprob_ref,
-        total_ref, dp_ref,
+        total_ref, dp_ref, prob_ref,
     ) = refs
     step = pl.program_id(0)
     slots = pick_ref.shape[1]
@@ -192,14 +193,15 @@
     plain = plain_ref[...]
     sigmoid = 1.0 / (1.0 + jnp.exp(-gate_pre))
     silu = gate_pre * sigmoid
-    act = (silu * up_pre).astype(BF16)
-    act_ref[...] = act
-    d_act = prob_ref[...] * plain
+    act = silu * up_pre
+    prob = prob_ref[...]
+    act_ref[...] = (prob * act).astype(BF16)
+    d_act = prob * plain
     d_gate = (d_act * up_pre * (sigmoid * (1.0 + gate_pre * (1.0 - sigmoid)))).astype(BF16)
     d_up = (d_act * silu).astype(BF16)
     dg_ref[...] = d_gate
     du_ref[...] = d_up
-    d_prob = jnp.sum(act.astype(F32) * plain, axis=1, keepdims=True)
+    d_prob = jnp.sum(act * plain, axis=1, keepdims=True)
     d_in = dot(d_gate, gate_w) + dot(d_up, up_w)
 
     @pl.when(step == 0)
@@ -252,7 +254,6 @@
             tiled,
             tiled,
             tiled,
-            pl.BlockSpec((rows, 1), lambda f: (quarter, 0)),
         ]
         + [whole(2, tokens, width)] * 2
         + [whole(4, tokens)],
@@ -261,51 +262,234 @@
             jax.ShapeDtypeStruct((every, hidden), BF16),
             jax.ShapeDtypeStruct((every, hidden), BF16),
             jax.ShapeDtypeStruct((every, hidden), BF16),
-            jax.ShapeDtypeStruct((every, 1), F32),
             pair,
             pair,
             jax.ShapeDtypeStruct((4, tokens), F32),
         ],
-        scratch_shapes=[pltpu.VMEM((rows, width), F32), pltpu.VMEM((rows, 1), F32)],
+        scratch_shapes=[
+            pltpu.VMEM((rows, width), F32),
+            pltpu.VMEM((rows, 1), F32),
+            pltpu.VMEM((rows, 1), F32),
+        ],
         input_output_aliases={10 + k: k for k in range(len(kept))},
         compiler_params=pltpu.CompilerParams(vmem_limit_bytes=VMEM_LIMIT),
         name="expert",
     )(*blocks, pick, plain, gate_w, up_w, router, mine, *kept)
 
 
-def expert_out_kernel(source_ref, pick_ref, act_ref, down_ref, prob_ref, out_ref, values_ref):
+def expert_out_kernel(pick_ref, act_ref, down_ref, keep_ref, send_ref, values_ref):
     s = pl.program_id(1)
 
     @pl.when(s == 0)
     def _():
-        values = (prob_ref[...] * dot(act_ref[...], down_ref[...])).astype(BF16)
+        values = dot(act_ref[...], down_ref[...]).astype(BF16)
         values_ref[...] = values.reshape(values_ref.shape)
 
-    out_ref[0] = dot(pick_ref[0], values_ref[s], TN).astype(BF16)
-
-
-def expert_out(source, pick, act, down_w, prob):
+    rows = dot(pick_ref[0], values_ref[s], TN).astype(BF16)
+
+    @pl.when(s % 2 == 0)
+    def _():
+        keep_ref[0, 0] = rows
+
+    @pl.when(s % 2 == 1)
+    def _():
+        send_ref[0, 0] = rows
+
+
+def expert_out(pick, act, down_w):
     hidden, width = down_w.shape
     owners, slots, tokens = pick.shape
     rows = 4 * slots
+    block = pl.BlockSpec((1, 1, tokens, width), lambda q, s: (q, s // 2, 0, 0))
     return pl.pallas_call(
         expert_out_kernel,
+        grid=(owners // 4, 4),
+        in_specs=[
+            pl.BlockSpec((1, slots, tokens), lambda q, s: (4 * q + s, 0, 0)),
+            pl.BlockSpec((rows, hidden), lambda q, s: (q, 0)),
+            pl.BlockSpec((hidden, width), lambda q, s: (0, 0)),
+        ],
+        out_specs=[block, block],
+        out_shape=[jax.ShapeDtypeStruct((owners // 4, 2, tokens, width), BF16)] * 2,
+        scratch_shapes=[pltpu.VMEM((4, slots, width), BF16)],
+        compiler_params=pltpu.CompilerParams(vmem_limit_bytes=VMEM_LIMIT),
+        name="expert_out",
+    )(pick, act, down_w)
+
+
+def cot_kernel(source_ref, c0_ref, c1_ref, c2_ref, c3_ref, pick_ref, down_ref, slot_ref, plain_ref):
+    slots = pick_ref.shape[1]
+
+    @pl.when(pl.program_id(1) == 0)
+    def _():
+        for s, cot_ref in enumerate((c0_ref, c1_ref, c2_ref, c3_ref)):
+            slot_ref[s * slots : (s + 1) * slots, :] = dot(pick_ref[s], cot_ref[0]).astype(BF16)
+
+    plain_ref[...] = dot(slot_ref[...], down_ref[...], NT)
+
+
+def gather_cot(source, all_cot, pick, down_w):
+    hidden, width = down_w.shape
+    owners, slots, tokens = pick.shape
+    rows = 4 * slots
+    tile = hidden // 2
+
+    def block(s):
+        return pl.BlockSpec((1, tokens, width), lambda q, f, m: (m[4 * q + s], 0, 0))
+
+    return pl.pallas_call(
+        cot_kernel,
         grid_spec=pltpu.PrefetchScalarGridSpec(
             num_scalar_prefetch=1,
-            grid=(owners // 4, 4),
+            grid=(owners // 4, hidden // tile),
+            in_specs=[block(s) for s in range(4)]
+            + [
+                pl.BlockSpec((4, slots, tokens), lambda q, f, m: (q, 0, 0)),
+                pl.BlockSpec((tile, width), lambda q, f, m: (f, 0)),
+            ],
+            out_specs=[
+                pl.BlockSpec((rows, width), lambda q, f, m: (q, 0)),
+                pl.BlockSpec((rows, tile), lambda q, f, m: (q, f)),
+            ],
+        ),
+        out_shape=[
+            jax.ShapeDtypeStruct((owners * slots, width), BF16),
+            jax.ShapeDtypeStruct((owners * slots, hidden), F32),
+        ],
+        compiler_params=pltpu.CompilerParams(vmem_limit_bytes=VMEM_LIMIT),
+        name="gather_cot",
+    )(source, all_cot, all_cot, all_cot, all_cot, pick, down_w)
+
+
+def row_grads_kernel(cuts, me_ref, left_ref, right_ref, *outs):
+    pieces, own_ref = outs[:-1], outs[-1]
+    product = dot(left_ref[...], right_ref[...], TN)
+    mine = pl.program_id(1) == me_ref[0]
+
+    @pl.when(mine)
+    def _():
+        own_ref[...] = product
+
+    @pl.when(jnp.logical_not(mine))
+    def _():
+        low = product.astype(BF16)
+        for k, piece_ref in enumerate(pieces):
+            piece_ref[0] = low[cuts[k] : cuts[k + 1], :]
+
+
+def row_grads(me, planes, left, right, shares):
+    count, hidden = left.shape
+    width = right.shape[1]
+    piece = hidden // planes
+    tile = width // 2
+    cuts = [piece * sum(shares[:k]) // sum(shares) for k in range(len(shares) + 1)]
+    sizes = [high - low for low, high in zip(cuts, cuts[1:])]
+
+    def place(n, p, m):
+        ahead = (p - m[0] + planes) % planes
+        idle = jnp.where(m[0] == planes - 1, planes - 2, 0)
+        return (jnp.where(ahead == 0, idle, ahead - 1), 0, n)
+
+    return pl.pallas_call(
+        functools.partial(row_grads_kernel, cuts),
+        grid_spec=pltpu.PrefetchScalarGridSpec(
+            num_scalar_prefetch=1,
+            grid=(width // tile, planes),
             in_specs=[
-                pl.BlockSpec((1, slots, tokens), lambda q, s, m: (4 * q + s, 0, 0)),
-                pl.BlockSpec((rows, hidden), lambda q, s, m: (q, 0)),
-                pl.BlockSpec((hidden, width), lambda q, s, m: (0, 0)),
-                pl.BlockSpec((rows, 1), lambda q, s, m: (q, 0)),
+                pl.BlockSpec((count, piece), lambda n, p, m: (0, p)),
+                pl.BlockSpec((count, tile), lambda n, p, m: (0, n)),
             ],
-            out_specs=pl.BlockSpec((1, tokens, width), lambda q, s, m: (m[4 * q + s], 0, 0)),
-            scratch_shapes=[pltpu.VMEM((4, slots, width), BF16)],
+            out_specs=[pl.BlockSpec((1, size, tile), place) for size in sizes]
+            + [pl.BlockSpec((piece, tile), lambda n, p, m: (0, n))],
         ),
-        out_shape=jax.ShapeDtypeStruct((owners, tokens, width), BF16),
+        out_shape=[jax.ShapeDtypeStruct((planes - 1, size, width), BF16) for size in sizes]
+        + [jax.ShapeDtypeStruct((piece, width), F32)],
         compiler_params=pltpu.CompilerParams(vmem_limit_bytes=VMEM_LIMIT),
-        name="expert_out",
-    )(source, pick, act, down_w, prob)
+        name="row_grads",
+    )(me.reshape(1).astype(jnp.int32), left, right)
+
+
+def weight_grad_kernel(planes, core_ref, left_ref, *refs):
+    rights, (keep_ref, send_ref) = refs[:-2], refs[-2:]
+    rows_e, pairs, size, tile = keep_ref.shape
+    tokens = left_ref.shape[0] // planes
+    count = len(rights) // planes
+    size = size // count
+    for k in range(count):
+        product = sum(
+            dot(left_ref[r * tokens : (r + 1) * tokens, :], rights[k * planes + r][...], TN)
+            for r in range(planes)
+        )
+        split_rows = product.astype(BF16).reshape(rows_e, pairs, 2, size, tile)
+        at = slice(k * size, (k + 1) * size)
+
+        @pl.when(core_ref[0] == 0)
+        def _():
+            keep_ref[:, :, at, :] = split_rows[:, :, 0]
+            send_ref[:, :, at, :] = split_rows[:, :, 1]
+
+        @pl.when(core_ref[0] != 0)
+        def _():
+            keep_ref[:, :, at, :] = split_rows[:, :, 1]
+            send_ref[:, :, at, :] = split_rows[:, :, 0]
+
+
+def weight_grads(left, *rights):
+    rows_e, rows_d = lax.axis_size("expert"), lax.axis_size("dp")
+    planes = len(rights[0])
+    total, part = left.shape
+    width = rights[0][0].shape[1]
+    tile = width // 4
+    size = part // (rows_e * rows_d) * len(rights)
+    core = (lax.axis_index("dp") % 2).reshape(1).astype(jnp.int32)
+    block = pl.BlockSpec((rows_e, rows_d // 2, size, tile), lambda n, m: (0, 0, 0, n))
+    return pl.pallas_call(
+        functools.partial(weight_grad_kernel, planes),
+        grid_spec=pltpu.PrefetchScalarGridSpec(
+            num_scalar_prefetch=1,
+            grid=(width // tile,),
+            in_specs=[pl.BlockSpec((total, part), lambda n, m: (0, 0))]
+            + [pl.BlockSpec((total // planes, tile), lambda n, m: (0, n))] * (planes * len(rights)),
+            out_specs=[block, block],
+        ),
+        out_shape=[jax.ShapeDtypeStruct((rows_e, rows_d // 2, size, width), BF16)] * 2,
+        compiler_params=pltpu.CompilerParams(vmem_limit_bytes=VMEM_LIMIT),
+        name="weight_grads",
+    )(core, left, *[array for right in rights for array in right])
+
+
+def add_rows_kernel(counts, *refs):
+    own_ref, parts, out_ref = refs[0], refs[1:-1], refs[-1]
+    step = pl.program_id(0)
+    at = 0
+    for count, ref in zip(counts, parts):
+
+        @pl.when((step >= at) & (step < at + count))
+        def _():
+            out_ref[...] = own_ref[...] + ref[...].astype(F32)
+
+        at += count
+
+
+def add_rows(own, parts):
+    width = own.shape[1]
+    step = math.gcd(*(p.shape[0] for p in parts))
+    counts = [p.shape[0] // step for p in parts]
+    starts = [sum(counts[:k]) for k in range(len(counts))]
+
+    def spec(start, count):
+        return pl.BlockSpec((step, width), lambda i: (jnp.clip(i - start, 0, count - 1), 0))
+
+    rows = pl.BlockSpec((step, width), lambda i: (i, 0))
+    return pl.pallas_call(
+        functools.partial(add_rows_kernel, counts),
+        grid=(own.shape[0] // step,),
+        in_specs=[rows] + [spec(a, c) for a, c in zip(starts, counts)],
+        out_specs=rows,
+        out_shape=jax.ShapeDtypeStruct(own.shape, F32),
+        compiler_params=pltpu.CompilerParams(vmem_limit_bytes=VMEM_LIMIT),
+        name="add_rows",
+    )(own, *parts)
 
 
 def swap(value, axis, bit):
@@ -325,35 +509,41 @@
     return lax.optimization_barrier(values)
 
 
-def split(value, axis_name, bit, at):
+def split(values, axis_name, bit, at):
     mine = (lax.axis_index(axis_name) // bit) % 2
-    shape = value.shape
-    pairs = value.reshape(shape[:at] + (shape[at] // 2, 2) + shape[at + 1 :])
-    keep = lax.dynamic_index_in_dim(pairs, mine, at + 1, keepdims=False)
-    send = lax.dynamic_index_in_dim(pairs, 1 - mine, at + 1, keepdims=False)
-    return keep, send
+
+    def half(index):
+        parts = []
+        for value in values:
+            shape = value.shape
+            pairs = value.reshape(shape[:at] + (shape[at] // 2, 2) + shape[at + 1 :])
+            parts.append(lax.dynamic_index_in_dim(pairs, index, at + 1, keepdims=False))
+        return plus(*parts)
+
+    return half(mine), half(1 - mine)
 
 
 STAGES = (("dp", 1, 1), ("dp", 2, 1), ("expert", 1, 0), ("expert", 2, 0))
 
 
 class RowScatter:
-    def __init__(self, value):
-        rows_e, rows_d = lax.axis_size("expert"), lax.axis_size("dp")
-        self.value = value.reshape((rows_e, rows_d, -1, value.shape[-1]))
+    def __init__(self, keep, send):
+        self.keep, self.send = keep, send
         self.stage = 0
 
     def start(self):
         axis, bit, at = STAGES[self.stage]
-        self.keep, send = split(self.value, axis, bit, at)
+        if self.stage:
+            self.keep, self.send = split(self.parts, axis, bit, at)
         self.stage += 1
-        return swap(send, axis, bit)
+        return swap(self.send, axis, bit)
 
     def finish(self, received):
-        self.value = plus(self.keep, received)
+        self.parts = (self.keep, received)
 
     def result(self):
-        return self.value.reshape(self.value.shape[-2:])
+        value = plus(*self.parts)
+        return value.reshape(value.shape[-2:])
 
 
 def shards(
@@ -441,9 +631,7 @@
             full = lax.dynamic_update_slice_in_dim(full, piece, at, axis=axis)
         return full
 
-    gains = gathered(jnp.stack([attn_gain, query_gain, key_gain, ffn_gain]), 1).astype(F32)
-    gain_attn, gain_query, gain_key, gain_ffn = [gains[i : i + 1] for i in range(4)]
-    full_router = gathered(w_router, 0)
+    gains_in = jnp.stack([attn_gain, query_gain, key_gain, ffn_gain])
 
     d_out_low = jnp.concatenate([prompt_cot[0], cont_cot[0, 0]], axis=0)
     routes = jnp.concatenate([prompt_routes[0], cont_routes[0, 0]], axis=0)
@@ -451,7 +639,6 @@
         (routes[:, k : k + 1] == jnp.arange(expert_count, dtype=jnp.int32)[None, :]).astype(F32)
         for k in range(top_count)
     )
-    member = lax.all_to_all(named.T, PLANE, split_axis=0, concat_axis=0, tiled=True)
     all_cot = lax.all_gather(d_out_low, PLANE, axis=0, tiled=True)
 
     start_len = prefix[0, 0]
@@ -472,10 +659,16 @@
         return [dot(products[0], weight)] + sent
 
     key_parts = project(normed_blocks, w_key)
+    key_parts[0], named, gains_in, w_router = fence(key_parts[0], named, gains_in, w_router)
+    gains = gathered(gains_in, 1).astype(F32)
+    gain_attn, gain_query, gain_key, gain_ffn = [gains[i : i + 1] for i in range(4)]
+    full_router = gathered(w_router, 0)
+    member = lax.all_to_all(named.T, PLANE, split_axis=0, concat_axis=0, tiled=True)
     value_parts = project(normed_blocks, w_value)
     query_parts = project(normed_blocks, w_query)
     key_raw, key_low = qk_post(key_parts, gain_key, cosine, sine)
     value_low = sum(p.astype(F32) for p in value_parts).astype(BF16)
+    query_parts[0], full_router, member = fence(query_parts[0], full_router, member)
     query_raw, query_low = qk_post(query_parts, gain_query, cosine, sine)
 
     def with_prompt(rows):
@@ -547,27 +740,20 @@
     b0, all_cot, normed_low = fence(normed2_low, all_cot, normed_low)
     b1, b2, x0, c0 = z1(b0), z2(b0), across(b0), core(b0)
     normed_sent = [shift(out_part(normed_low, r), r) for r in others]
+    attended_sent = [shift(out_part(attended, r), r) for r in others]
     all_cot = all_cot.reshape(owners, tokens, width)
-    slot_cot = jnp.concatenate(
-        [
-            dot(pick[b], lax.dynamic_index_in_dim(all_cot, source[b], 0, False), out=BF16)
-            for b in range(owners)
-        ],
-        axis=0,
-    )
-    d_act_plain = dot(slot_cot, down_w, NT)
-    b1, b2, x0, c0, d_act_plain, attended, *normed_sent = fence(
-        b1, b2, x0, c0, d_act_plain, attended, *normed_sent
-    )
-    normed_out = jnp.concatenate([out_part(normed_low, 0)] + normed_sent, axis=0)
+    slot_cot, d_act_plain = gather_cot(source, all_cot, pick, down_w)
+    b1, b2, x0, c0, d_act_plain, *rest = fence(
+        b1, b2, x0, c0, d_act_plain, *normed_sent, *attended_sent
+    )
+    normed_out = jnp.concatenate([out_part(normed_low, 0), *rest[: planes - 1]], axis=0)
+    attended_out = jnp.concatenate([out_part(attended, 0), *rest[planes - 1 :]], axis=0)
     b3, x1, c1, x0c = z1(b2), across(b1), core(b1), core(x0)
-    attended_sent = [shift(out_part(attended, r), r) for r in others]
-    b3, x1, c1, x0c, *attended_sent = fence(b3, x1, c1, x0c, *attended_sent)
-    attended_out = jnp.concatenate([out_part(attended, 0)] + attended_sent, axis=0)
+    b3, x1, c1, x0c = fence(b3, x1, c1, x0c)
 
     def quarter(q, blocks, kept):
         outs = expert_quarter(q, blocks, pick, d_act_plain, gate_w, up_w, full_router, mine, kept)
-        return outs[:5], outs[5], outs[6], outs[7]
+        return outs[:4], outs[4], outs[5], outs[6]
 
     x2, c2, c3, x1c = across(b2), core(b2), core(b3), core(x1)
     kept, keep0, send0, dprob0 = quarter(0, (b0, c0, b1, c1), ())
@@ -575,54 +761,54 @@
     x3, x2c = across(b3), core(x2)
     kept, keep2, send2, dprob2 = quarter(2, (x0, x0c, x1, x1c), kept)
     x3, x2c, send2, *kept = fence(x3, x2c, send2, *kept)
-    x3c, near2 = core(x3), core(send2)
-    x3c, near2, *kept = fence(x3c, near2, *kept)
-    got2 = across(plus(keep2, near2))
+    x3c, near2, near0 = core(x3), core(send2), core(send0)
+    x3c, near2, near0, *kept = fence(x3c, near2, near0, *kept)
+    pair2 = plus(keep2, near2)
+    got21 = across(pair2[1])
+    kept, keep3, send3, dprob3 = quarter(3, (x2, x2c, x3, x3c), kept)
+    got21, pair20, send3, *kept = fence(got21, pair2[0], send3, *kept)
+    got20, near3 = across(pair20), core(send3)
     kept, keep1, send1, dprob1 = quarter(1, (b2, c2, b3, c3), kept)
-    kept, keep3, send3, dprob3 = quarter(3, (x2, x2c, x3, x3c), kept)
-    got2, send0, send1, send3, *kept = fence(got2, send0, send1, send3, *kept)
-    slot_in, act_low, d_gate, d_up, slot_gate = kept
+    got20, near3, send1, *kept = fence(got20, near3, send1, *kept)
+    slot_in, act_low, d_gate, d_up = kept
 
     piece = hidden // planes
 
-    def grad_rows(left, right, r):
-        cols = lax.dynamic_slice_in_dim(left, ((me + r) % planes) * piece, piece, axis=1)
-        return dot(cols, right, TN)
-
-    def grad_low(left, right):
-        return [grad_rows(left, right, r).astype(BF16) for r in others]
-
-    def send_rows(values, low, high):
-        at = slice(piece * low // 4, piece * high // 4)
-        return [shift(v[at], r) for r, v in zip(others, values)]
-
-    near0, near1, near3 = core(send0), core(send1), core(send3)
-    gate_low = grad_low(d_gate, slot_in)
-    near0, near1, near3, *gate_low = fence(near0, near1, near3, *gate_low)
-    first = plus(keep0, near0, got2)
-    got3, first_got = across(plus(keep3, near3)), z1(first[1])
-    gate_a = send_rows(gate_low, 0, 3)
-    up_low = grad_low(d_up, slot_in)
+    def send_rows(values):
+        return [shift(values[r - 1], r) for r in others]
+
+    pair3 = plus(keep3, near3)
+    first_got, got31, near1 = z1(plus(keep0[1], near0[1], got21)), across(pair3[1]), core(send1)
+    *gate_low, gate_own = row_grads(me, planes, d_gate, slot_in, (1, 1))
+    first_got, got31, near1, gate_own, pair30, d_up, slot_in, *gate_low = fence(
+        first_got, got31, near1, gate_own, pair3[0], d_up, slot_in, *gate_low
+    )
+    second_got, got30 = z1(plus(keep1[1], near1[1], got31)), across(pair30)
+    gate_a = send_rows(gate_low[0])
+    *up_low, up_own = row_grads(me, planes, d_up, slot_in, (1, 2, 1))
     place = jnp.zeros((owners,), jnp.int32).at[source].set(jnp.arange(owners, dtype=jnp.int32))
     token_dprob = jnp.take(
         jnp.concatenate([dprob0, dprob1, dprob2, dprob3], axis=0), place, axis=0
     )
+    second_got, got30, token_dprob, act_low, up_own, gate_b, up_0, up_1, up_2, *gate_a = fence(
+        second_got, got30, token_dprob, act_low, up_own, gate_low[1], *up_low, *gate_a
+    )
+    far_got = z2(plus(keep1[0], near1[0], got30, second_got))
+    gate_b, up_a = send_rows(gate_b), send_rows(up_0)
+    out_keep, out_send = expert_out(pick, act_low, down_w)
     dprobs = lax.all_to_all(token_dprob, PLANE, split_axis=0, concat_axis=0, tiled=True).T
-    got3, first_got, dprobs, *rest = fence(got3, first_got, dprobs, *gate_a, *up_low)
-    gate_a, up_low = rest[: planes - 1], rest[planes - 1 :]
-    second = plus(keep1, near1, got3)
-    second_got = z1(second[1])
-    gate_b = send_rows(gate_low, 3, 4)
-    up_a = send_rows(up_low, 0, 1)
-    slot_dy = (slot_gate * slot_cot.astype(F32)).astype(BF16)
-    down_low = grad_low(act_low, slot_dy)
-    second_got, *rest = fence(second_got, *gate_b, *up_a, *down_low)
-    gate_b, up_a, down_low = (rest[k * (planes - 1) : (k + 1) * (planes - 1)] for k in range(3))
-    far_got = z2(plus(second[0], second_got))
-    up_b = send_rows(up_low, 1, 4)
-    slot_out = expert_out(source, pick, act_low, down_w, slot_gate)
-    far_got, slot_out, *up_b = fence(far_got, slot_out, *up_b)
-    d_normed2_moe = first[0].astype(F32) + first_got.astype(F32) + far_got.astype(F32)
+    out_near = core(out_send)
+    far_got, dprobs, act_low, out_keep, out_near, *rest = fence(
+        far_got, dprobs, act_low, out_keep, out_near, *gate_b, *up_a
+    )
+    gate_b, up_a = rest[: planes - 1], rest[planes - 1 :]
+    d_normed2_moe = (
+        keep0[0].astype(F32)
+        + near0[0].astype(F32)
+        + got20.astype(F32)
+        + first_got.astype(F32)
+        + far_got.astype(F32)
+    )
 
     d_out = d_out_low.astype(F32)
     dlogit_low = (
@@ -636,28 +822,32 @@
     ffn_gain_grad = jnp.sum(d_normed2 * mixed_rows * inverse2, axis=0)
 
     branch_low = d_mixed.astype(BF16)
-    branch_low, slot_out = fence(branch_low, slot_out)
-    moe_out = lax.psum_scatter(
-        slot_out.reshape(owners * tokens, width), PLANE, scatter_dimension=0, tiled=True
-    ).astype(F32)
-    out_rows = mixed_rows + moe_out
-    branches = [branch_low] + [shift(branch_low, r) for r in others]
-    gate_own = grad_rows(d_gate, slot_in, 0)
-    up_own = grad_rows(d_up, slot_in, 0)
-    *branches, gate_own, up_own = fence(*branches, gate_own, up_own)
+    def out_sum(q, i):
+        return plus(out_keep[q, i], out_near[q, i])
+
+    branch_low, out31, act_low = fence(branch_low, out_sum(3, 1), act_low)
+    sent = [shift(branch_low, r) for r in others]
+    out_got31 = across(out31)
+    *down_low, down_own = row_grads(me, planes, act_low, slot_cot, (1, 1))
+    out30 = out_sum(3, 0)
+    out_got31, out30, out_keep, out_near, down_own, down_0, down_1, branch_low, *sent = fence(
+        out_got31, out30, out_keep, out_near, down_own, *down_low, branch_low, *sent
+    )
+    branches = [branch_low, *sent]
     blocks_low = [dot(branches[r], w_output, NT).astype(BF16) for r in others]
-    blocks_low = fence(*blocks_low)
-    d_att_blocks = [dot(branches[0], w_output, NT).astype(BF16)] + [
-        shift(v, planes - r) for r, v in zip(others, blocks_low)
-    ]
-    output_rows = RowScatter(dot(attended_out, jnp.concatenate(branches, axis=0), TN).astype(BF16))
-    output_got = output_rows.start()
-    output_got, *d_att_blocks = fence(output_got, *d_att_blocks)
-    output_rows.finish(output_got)
-    d_attended = placed(d_att_blocks)
+    d_att_blocks = [shift(v, planes - r) for r, v in zip(others, blocks_low)]
+    d_att_own = dot(branches[0], w_output, NT).astype(BF16)
+    out_second = plus(out_keep[1, 1], out_near[1, 1], out_got31)
+    d_att_own, up_1, out_second, gate_own, branch_low, *d_att_blocks = fence(
+        d_att_own, up_1, out_second, gate_own, branch_low, *d_att_blocks
+    )
+    branches[0] = branch_low
+    d_attended = placed([d_att_own, *d_att_blocks])
 
     key_total = prompt_total + cont_len
-    output_got = output_rows.start()
+    out_got30, out_second = across(out30), z1(out_second)
+    up_b = send_rows(up_1)
+    output_keep, output_send = weight_grads(attended_out, branches)
     d_queries, d_keys_all, d_values_all = attention_call(
         attend_back_kernel,
         "attend_back",
@@ -671,77 +861,98 @@
         prompt_dev,
         prompt_total,
     )
-
-    def own_keys(rows):
-        def prompt_rows(r):
-            return lax.dynamic_slice_in_dim(
-                rows, ((me + r) % planes) * prompt_dev, prompt_dev, axis=0
+    out21 = out_sum(2, 1)
+    out_got30, out_second, output_keep, output_send, out21, d_queries, d_keys_all, d_values_all, *up_b = fence(
+        out_got30, out_second, output_keep, output_send, out21, d_queries, d_keys_all, d_values_all, *up_b
+    )
+    output_rows = RowScatter(output_keep, output_send)
+
+    def prompt_sent(rows):
+        return [
+            shift(
+                lax.dynamic_slice_in_dim(
+                    rows, ((me + r) % planes) * prompt_dev, prompt_dev, axis=0
+                ).astype(BF16),
+                r,
             )
-
-        total = prompt_rows(0)
-        for r in others:
-            total = total + shift(prompt_rows(r).astype(BF16), r).astype(F32)
+            for r in others
+        ]
+
+    def own_keys(rows, got):
+        total = lax.dynamic_slice_in_dim(rows, me * prompt_dev, prompt_dev, axis=0)
+        for part in got:
+            total = total + part.astype(F32)
         return jnp.concatenate([total, rows[prompt_total:]], axis=0)
 
-    d_value_low = own_keys(d_values_all).astype(BF16)
+    value_prompt, key_prompt = prompt_sent(d_values_all), prompt_sent(d_keys_all)
+    out_got21, output_got = across(out21), output_rows.start()
     d_query_low, query_gain_grad = qk_post_back(d_queries, query_raw, gain_query, cosine, sine)
-    d_key_low, key_gain_grad = qk_post_back(
-        own_keys(d_keys_all), key_raw, gain_key, cosine, sine
-    )
-    output_got, d_value_low, d_query_low, d_key_low = fence(
-        output_got, d_value_low, d_query_low, d_key_low
+    out20, out_far = out_sum(2, 0), plus(out_keep[1, 0], out_near[1, 0], out_got30, out_second)
+    out_got21, output_got, out20, out_far, d_query_low, gate_own, *rest = fence(
+        out_got21, output_got, out20, out_far, d_query_low, gate_own, *value_prompt, *key_prompt
     )
     output_rows.finish(output_got)
+    d_value_low = own_keys(d_values_all, rest[: planes - 1]).astype(BF16)
+    d_keys = own_keys(d_keys_all, rest[planes - 1 :])
 
     def spread(low):
         return [shift(low, r) for r in others]
 
-    def weight_rows(own, got):
-        return RowScatter(dot(normed_out, jnp.concatenate([own, *got], axis=0), TN).astype(BF16))
-
-    got, output_got = spread(d_value_low), output_rows.start()
-    output_got, *d_values = fence(output_got, *got)
-    output_rows.finish(output_got)
-
-    value_rows = weight_rows(d_value_low, d_values)
-    got, output_got, value_got = spread(d_query_low), output_rows.start(), value_rows.start()
-    output_got, value_got, *d_query_got = fence(output_got, value_got, *got)
-    output_rows.finish(output_got)
-    value_rows.finish(value_got)
-
-    query_rows = weight_rows(d_query_low, d_query_got)
-    got, value_got, query_got = spread(d_key_low), value_rows.start(), query_rows.start()
+    def total(own, *parts):
+        for k in range(planes - 1):
+            own = add_rows(own, [p[k] for p in parts])
+        return own
+
+    d_value_low, d_keys = fence(d_value_low, d_keys)
+    got = spread(d_value_low) + spread(d_query_low)
+    out_got20, out_far = across(out20), z2(out_far)
+    d_key_low, key_gain_grad = qk_post_back(d_keys, key_raw, gain_key, cosine, sine)
+    gate_grad = total(gate_own, gate_a, gate_b)
+    out_first = plus(out_keep[0, 1], out_near[0, 1], out_got21)
+    out_got20, out_far, out_first, d_key_low, gate_grad, *rest = fence(
+        out_got20, out_far, out_first, d_key_low, gate_grad, *got
+    )
+    d_values, d_query_got = rest[: planes - 1], rest[planes - 1 :]
+
+    got, output_got, out_first = spread(d_key_low), output_rows.start(), z1(out_first)
+    early_keep, early_send = weight_grads(
+        normed_out, [d_value_low, *d_values], [d_query_low, *d_query_got]
+    )
     partial = [
         dot(d_values[k], w_value, NT) + dot(d_query_got[k], w_query, NT) for k in range(planes - 1)
     ]
-    rest = fence(value_got, query_got, *got, *partial)
-    value_got, query_got = rest[:2]
-    d_key_got, partial = rest[2 : planes + 1], rest[planes + 1 :]
-    value_rows.finish(value_got)
-    query_rows.finish(query_got)
-
+    output_got, out_first, early_keep, early_send, *rest = fence(
+        output_got, out_first, early_keep, early_send, *got, *partial
+    )
+    d_key_got, partial = rest[: planes - 1], rest[planes - 1 :]
+    output_rows.finish(output_got)
+    early_rows = RowScatter(early_keep, early_send)
+    out_rows = (
+        mixed_rows
+        + plus(out_keep[0, 0].astype(F32), out_near[0, 0])
+        + out_got20.astype(F32)
+        + out_first.astype(F32)
+        + out_far.astype(F32)
+    )
+
+    early_got = early_rows.start()
+    key_keep, key_send = weight_grads(normed_out, [d_key_low, *d_key_got])
     blocks_low = [
         (partial[k] + dot(d_key_got[k], w_key, NT)).astype(BF16) for k in range(planes - 1)
     ]
-    query_got, value_got = query_rows.start(), value_rows.start()
+    early_got, key_keep, key_send, up_2, down_0, *blocks_low = fence(
+        early_got, key_keep, key_send, up_2, down_0, *blocks_low
+    )
+    early_rows.finish(early_got)
+    key_rows = RowScatter(key_keep, key_send)
+
     d_normed_got = [shift(v, planes - r) for r, v in zip(others, blocks_low)]
-    down_a = send_rows(down_low, 0, 1)
-    key_rows = weight_rows(d_key_low, d_key_got)
-    key_got = key_rows.start()
+    early_got, key_got, output_got = early_rows.start(), key_rows.start(), output_rows.start()
+    up_c, down_a = send_rows(up_2), send_rows(down_0)
     d_normed_own = (
         dot(d_value_low, w_value, NT) + dot(d_query_low, w_query, NT) + dot(d_key_low, w_key, NT)
     )
-    query_got, value_got, key_got, d_normed_own, *rest = fence(
-        query_got, value_got, key_got, d_normed_own, *d_normed_got, *down_a
-    )
-    d_normed_got, down_a = rest[: planes - 1], rest[planes - 1 :]
-    query_rows.finish(query_got)
-    value_rows.finish(value_got)
-    key_rows.finish(key_got)
-
     d_normed = placed([d_normed_own] + [p.astype(F32) for p in d_normed_got])
-    key_got, query_got, value_got = key_rows.start(), query_rows.start(), value_rows.start()
-    down_b = send_rows(down_low, 1, 3)
     scaled = gain_attn * d_normed
     centre = jnp.mean(scaled * x_rows, axis=-1, keepdims=True)
     inv = inverse[:, None]
@@ -754,41 +965,48 @@
         ],
         axis=1,
     )
+    early_got, key_got, output_got, d_x, small_grads, down_1, *rest = fence(
+        early_got, key_got, output_got, d_x, small_grads, down_1, *up_c, *down_a
+    )
+    up_c, down_a = rest[: planes - 1], rest[planes - 1 :]
+    early_rows.finish(early_got)
+    key_rows.finish(key_got)
+    output_rows.finish(output_got)
+
+    key_got, early_got, output_got = key_rows.start(), early_rows.start(), output_rows.start()
+    down_b = send_rows(down_1)
     by_plane = small_grads.reshape(rows_e, planes, out_group, small_grads.shape[1])
 
     def plane_rows(r):
         return lax.dynamic_index_in_dim(by_plane, (me + r) % planes, 1, False)
 
-    small_rows = RowScatter(plus(plane_rows(0), *[shift(plane_rows(r), r) for r in others]))
+    small_sum = plus(plane_rows(0), *[shift(plane_rows(r), r) for r in others])
+    small_rows = RowScatter(
+        *split([small_sum.reshape(rows_e, rows_d, -1, small_sum.shape[-1])], *STAGES[0])
+    )
     small_rows.finish(small_rows.start())
-    key_got, query_got, value_got, small_rows.value, *down_b = fence(
-        key_got, query_got, value_got, small_rows.value, *down_b
+    up_grad = total(up_own, up_a, up_b, up_c)
+    key_got, early_got, output_got, small_rows.parts, up_grad, *down_b = fence(
+        key_got, early_got, output_got, small_rows.parts, up_grad, *down_b
     )
     key_rows.finish(key_got)
-    query_rows.finish(query_got)
-    value_rows.finish(value_got)
-
-    key_got, query_got = key_rows.start(), query_rows.start()
+    early_rows.finish(early_got)
+    output_rows.finish(output_got)
+
+    key_got, early_got = key_rows.start(), early_rows.start()
     small_rows.finish(small_rows.start())
-    down_c = send_rows(down_low, 3, 4)
-    down_own = grad_rows(act_low, slot_dy, 0)
-    key_got, query_got, small_rows.value, down_own, *down_c = fence(
-        key_got, query_got, small_rows.value, down_own, *down_c
+    small_rows.finish(small_rows.start())
+    down_grad = total(down_own, down_a, down_b)
+    key_got, early_got, small_rows.parts, down_grad = fence(
+        key_got, early_got, small_rows.parts, down_grad
     )
     key_rows.finish(key_got)
-    query_rows.finish(query_got)
+    early_rows.finish(early_got)
     key_rows.finish(key_rows.start())
     small_rows.finish(small_rows.start())
-    small_rows.finish(small_rows.start())
     small_grads = small_rows.result()
-
-    def total(own, *parts):
-        cuts = [jnp.concatenate([p[k] for p in parts], axis=0) for k in range(planes - 1)]
-        return own + sum(c.astype(F32) for c in cuts)
-
-    gate_grad = total(gate_own, gate_a, gate_b)
-    up_grad = total(up_own, up_a, up_b)
-    down_grad = total(down_own, down_a, down_b, down_c)
+    early_grads = early_rows.result().astype(F32)
+    size = early_grads.shape[0] // 2
     return (
         out_rows[:prompt_dev].astype(BF16)[None],
         out_rows[prompt_dev:].astype(BF16)[None, None],
@@ -798,9 +1016,9 @@
         small_grads[:, 1],
         small_grads[:, 2],
         small_grads[:, 3],
-        query_rows.result().astype(F32),
+        early_grads[size:],
         key_rows.result().astype(F32),
-        value_rows.result().astype(F32),
+        early_grads[:size],
         output_rows.result().astype(F32),
         small_grads[:, 4:],
         gate_grad[None],

time: 747 us -> 718 us (0.961)
  Pallas kernels: 116 us -> 205 us
  matrix products: 122 us -> 44.6 us
  waiting for transfers between devices: 308 us -> 236 us
  other arithmetic: 55.4 us -> 73.4 us
  starting transfers between devices: 71.5 us -> 85.3 us
    pallas_call x1 -> x11, Pallas kernels: 21.8 us -> 116 us  [the longest x3 40.3 us: row_grads(): pl.pallas_call(functools.partial(row_grads_kernel, cuts), grid_spec=pltpu...]
    dot_general x48 -> x21, matrix products: 122 us -> 44.6 us  [dot(): lax.dot_general(left, right, (dims, ((), ())), preferred_element_type=out)]
    ppermute x44 -> x50, waiting for transfers between devices: 157 us -> 88.6 us  [swap(): lax.ppermute(value, axis, [(i, i ^ bit) for i in range(lax.axis_size(axis...]
    ppermute x29, waiting for transfers between devices: 140 us -> 111 us  [shift(): lax.ppermute(value, 'context', [(i, (i + r) % planes) for i in range(plan...]
    convert_element_type x17 -> x22, other arithmetic: 25 us -> 50.9 us  [plus(): return sum((v.astype(F32) for v in values)).astype(values[0].dtype)]
    all_to_all x1, waiting for transfers between devices: 6.42 us -> 31.5 us  [shards(): lax.all_to_all(token_dprob, PLANE, split_axis=0, concat_axis=0, tiled=True)]
    ppermute x44 -> x50, starting transfers between devices: 28.8 us -> 41.9 us  [swap(): lax.ppermute(value, axis, [(i, i ^ bit) for i in range(lax.axis_size(axis...]
    broadcast_in_dim x3 -> x0, other arithmetic: 11.1 us -> none  [the longest x1 4.3 us: shards(): up_grad[None]]
  transfers between devices with their start and end apart: 77 -> 82, of which waited for: 38 -> 34; matrix products, arithmetic and copies ran while one was open for 25% -> 17% of each run, Pallas kernels for 14% -> 26%
where the time goes in v3:
time: 718 us; the launch traced here: 711 us
  waiting for transfers between devices  236 us (33%)
  Pallas kernels  205 us (29%)
  starting transfers between devices  85.3 us (12%)
  other arithmetic  73.4 us (10%)
  local copies, waits for them, and re-layouts  48.6 us (7%)
  matrix products  44.6 us (6%)
  between operations  17 us (2%)
    ppermute x29, waiting for transfers between devices, shift(): lax.ppermute(value, 'context', [(i, (i + r) % planes) for i in range(plan...  111 us
    ppermute x50, waiting for transfers between devices, swap(): lax.ppermute(value, axis, [(i, i ^ bit) for i in range(lax.axis_size(axis...  88.6 us
    pallas_call x4, Pallas kernels, expert_quarter(): pl.pallas_call(expert_kernel, grid=(hidden // tile,), in_specs=[whole(tok...  67.1 us
    convert_element_type x22, other arithmetic, plus(): return sum((v.astype(F32) for v in values)).astype(values[0].dtype)  50.9 us
    dot_general x21, matrix products, dot(): lax.dot_general(left, right, (dims, ((), ())), preferred_element_type=out)  44.6 us
    ppermute x50, starting transfers between devices, swap(): lax.ppermute(value, axis, [(i, i ^ bit) for i in range(lax.axis_size(axis...  41.9 us
    pallas_call x3, Pallas kernels, row_grads(): pl.pallas_call(functools.partial(row_grads_kernel, cuts), grid_spec=pltpu...  40.3 us
    ppermute x29, starting transfers between devices, shift(): lax.ppermute(value, 'context', [(i, (i + r) % planes) for i in range(plan...  32.7 us
  transfers between devices with their start and end apart: 82, of which 34 were waited for; matrix products, arithmetic and copies ran while one was open for 17% of the time, Pallas kernels for 26%

profile of v3, /device:TPU:0, one launch (start us, length us, event | category | flops | bytes accessed | tf_op | source)
XLA Modules:
  0.0 710.6 jit_solution(12934670319347345016)
XLA Ops:
  15.4 6.3 collective-permute-done.1
  45.2 6.7 all-to-all-start
  53.2 5.1 all-to-all-done
  70.7 15.8 %collective-permute-done.3.refs_1_ = bf16[192,2048]{1,0:T(8,128)(2,1)S(1)} collective-permute-done((bf16[192,2048]{1,0:T(8,128)(2,1)}, bf16[192,2048]{1,0:T(8,128)(2,1)S(1)}, u32[]{:S(2)}, u32[]{:S(2)}) %collective-permute-start.3) | collective-permute-done | bytes 786464 | tf_op jit(solution)/shard_map/ppermute | solution.py:590
  96.1 4.8 attend.1
  103.1 7.5 %collective-permute-done.9 = bf16[192,1024]{1,0:T(8,128)(2,1)} collective-permute-done((bf16[192,1024]{1,0:T(8,128)(2,1)S(1)}, bf16[192,1024]{1,0:T(8,128)(2,1)}, u32[]{:S(2)}, u32[]{:S(2)}) %collective-permute-start.9) | collective-permute-done | bytes 393248 | tf_op jit(solution)/shard_map/ppermute | solution.py:590
  119.2 15.6 %collective-permute-done.10 = bf16[192,2048]{1,0:T(8,128)(2,1)S(1)} collective-permute-done((bf16[192,2048]{1,0:T(8,128)(2,1)S(1)}, bf16[192,2048]{1,0:T(8,128)(2,1)S(1)}, u32[]{:S(2)}, u32[]{:S(2)}) %collective-permute-start.10) | collective-permute-done | bytes 786464 | tf_op jit(solution)/shard_map/ppermute | solution.py:590
  148.4 21.4 %gather_cot.1 = (bf16[1792,2048]{1,0:T(8,128)(2,1)}, f32[1792,1024]{1,0:T(8,128)}) custom-call(s32[16]{0:T(128)S(1)} %stack.135.source_ref, bf16[16,192,2048]{2,1,0:T(8,128)(2,1)} %bitcast.297, bf16[16,192,2048]{2,1,0:T(8,128)(2,1)} %bitcast.298, bf16[16,192,2048]{2,1,0:T(8,128)(2,1)} %bitcast.299, bf16[16,192,2048]{2,1,0:T(8,128)(2,1)} %bitcast.300, ...), custom_call_target="tpu_custom_call" | custom-call | tf_op jit(solution)/shard_map/gather_cot/pallas_call | solution.py:340
  172.9 16.7 %collective-permute-done.17.refs_2_ = bf16[192,2048]{1,0:T(8,128)(2,1)S(1)} collective-permute-done((bf16[192,2048]{1,0:T(8,128)(2,1)S(1)}, bf16[192,2048]{1,0:T(8,128)(2,1)S(1)}, u32[]{:S(2)}, u32[]{:S(2)}) %collective-permute-start.17) | collective-permute-done | bytes 786464 | tf_op jit(solution)/shard_map/ppermute | solution.py:496
  193.2 16.8 %expert.4 = (bf16[1792,2048]{1,0:T(8,128)(2,1)}, bf16[1792,1024]{1,0:T(8,128)(2,1)}, bf16[1792,1024]{1,0:T(8,128)(2,1)}, bf16[1792,1024]{1,0:T(8,128)(2,1)}, bf1...) custom-call(bf16[192,2048]{1,0:T(8,128)(2,1)S(1)} %multiply_convert_fusion.refs_0_, ...), custom_call_target="tpu_custom_call" | custom-call | tf_op jit(solution)/shard_map/expert/pallas_call | solution.py:239
  215.0 16.7 %expert.5 = (bf16[1792,2048]{1,0:T(8,128)(2,1)}, bf16[1792,1024]{1,0:T(8,128)(2,1)}, bf16[1792,1024]{1,0:T(8,128)(2,1)}, bf16[1792,1024]{1,0:T(8,128)(2,1)}, bf1...) custom-call(bf16[192,2048]{1,0:T(8,128)(2,1)S(1)} %collective-permut, ...), custom_call_target="tpu_custom_call", output_to_operand_aliasing={{0}: (10, {}), {1}: (11, {}), {2}: (12, {}), {3}: (13, {})} | custom-call | tf_op jit(solution)/shard_map/expert/pallas_call | solution.py:239
  240.4 16.9 %expert.6 = (bf16[1792,2048]{1,0:T(8,128)(2,1)}, bf16[1792,1024]{1,0:T(8,128)(2,1)}, bf16[1792,1024]{1,0:T(8,128)(2,1)}, bf16[1792,1024]{1,0:T(8,128)(2,1)}, bf1...) custom-call(bf16[192,2048]{1,0:T(8,128)(2,1)S(1)} %collective-permut, ...), custom_call_target="tpu_custom_call", output_to_operand_aliasing={{0}: (10, {}), {1}: (11, {}), {2}: (12, {}), {3}: (13, {})} | custom-call | tf_op jit(solution)/shard_map/expert/pallas_call | solution.py:239
  262.9 16.7 %expert.7 = (bf16[1792,2048]{1,0:T(8,128)(2,1)}, bf16[1792,1024]{1,0:T(8,128)(2,1)}, bf16[1792,1024]{1,0:T(8,128)(2,1)}, bf16[1792,1024]{1,0:T(8,128)(2,1)}, bf1...) custom-call(bf16[192,2048]{1,0:T(8,128)(2,1)S(1)} %collective-permut, ...), custom_call_target="tpu_custom_call", output_to_operand_aliasing={{0}: (10, {}), {1}: (11, {}), {2}: (12, {}), {3}: (13, {})} | custom-call | tf_op jit(solution)/shard_map/expert/pallas_call | solution.py:239
  286.2 13.5 %row_grads.3 = (bf16[1,256,2048]{2,1,0:T(8,128)(2,1)}, bf16[1,256,2048]{2,1,0:T(8,128)(2,1)}, f32[512,2048]{1,0:T(8,128)}) custom-call(s32[1]{0:T(128)} %bitcast.45.me_ref, bf16[1792,1024]{1,0:T(8,128)(2,1)S(1)} %copy-done.2, bf16[1792,2048]{1,0:T(8,128)(2,1)} %get-tuple-element.345.right_ref), custom_call_target="tpu_custom_call" | custom-call | tf_op jit(solution)/shard_map/row_grads/pallas_call | solution.py:393
  310.3 13.3 %row_grads.4 = (bf16[1,128,2048]{2,1,0:T(8,128)(2,1)}, bf16[1,256,2048]{2,1,0:T(8,128)(2,1)}, bf16[1,128,2048]{2,1,0:T(8,128)(2,1)S(1)}, f32[512,2048]{1,0:T(8,128)}) custom-call(s32[1]{0:T(128)} %bitcast.45.me_ref, bf16[1792,1024]{1,0:T(8,128)(2,1)S(1)} %copy-done.3, bf16[1792,2048]{1,0:T(8,128)(2,1)} %get-tuple-element.345.right_ref), custom_call_target="tpu_custom_call" | custom-call | tf_op jit(solution)/shard_map/row_grads/pallas_call | solution.py:393
  326.5 22.3 %expert_out.1 = (bf16[4,2,192,2048]{3,2,1,0:T(8,128)(2,1)}, bf16[4,2,192,2048]{3,2,1,0:T(8,128)(2,1)}) custom-call(bf16[16,112,192]{2,1,0:T(8,128)(2,1)S(1)} %fusion.pick_ref.refs_4_, bf16[1792,1024]{1,0:T(8,128)(2,1)S(1)} %copy-done, bf16[1024,2048]{1,0:T(8,128)(2,1)} %bitcast.292), custom_call_target="tpu_custom_call" | custom-call | tf_op jit(solution)/shard_map/expert_out/pallas_call | solution.py:304
  359.9 31.5 %all-to-all-done.1 = f32[16,1,192]{2,1,0:T(1,128)S(1)} async-done(((f32[16,1,192]{2,1,0:T(1,128)}), f32[16,1,192]{2,1,0:T(1,128)S(1)}, u32[]{:S(2)}, u32[]{:S(2)}) %all-to-all-start.1) | async-done | bytes 12320 | tf_op jit(solution)/shard_map/all_to_all | solution.py:799
  402.9 13.4 %row_grads.5 = (bf16[1,256,2048]{2,1,0:T(8,128)(2,1)}, bf16[1,256,2048]{2,1,0:T(8,128)(2,1)}, f32[512,2048]{1,0:T(8,128)}) custom-call(s32[1]{0:T(128)} %bitcast.45.me_ref, bf16[1792,1024]{1,0:T(8,128)(2,1)S(1)} %copy-done.1, bf16[1792,2048]{1,0:T(8,128)(2,1)} %get-tuple-element.367.right_ref), custom_call_target="tpu_custom_call" | custom-call | tf_op jit(solution)/shard_map/row_grads/pallas_call | solution.py:393
  416.3 4.6 collective-permute-done.43
  441.8 11.1 %attend_back.1 = (f32[192,2048]{1,0:T(8,128)S(1)}, f32[256,2048]{1,0:T(8,128)}, f32[256,2048]{1,0:T(8,128)}) custom-call(s32[2]{0:T(128)S(1)} %pad_add_fusion.1.meta_ref, bf16[192,2048]{1,0:T(8,128)(2,1)S(1)} %copy-done.13, bf16[256,2048]{1,0:T(8,128)(2,1)S(1)} %constant_dynamic-update-slice_fusion.4.k_ref, bf16[256,2048]{1,0:T(8,128)(2,1)S(1)} %copy-done.6, ...), custom_call_target="tpu_custom_call" | custom-call | tf_op jit(solution)/shard_map/attend_back/pallas_call | solution.py:155
  454.1 4.6 weight_grads.3
  495.7 4.6 add_rows.3
  504.0 16.4 %collective-permute-done.54 = bf16[192,2048]{1,0:T(8,128)(2,1)S(1)} collective-permute-done((bf16[192,2048]{1,0:T(8,128)(2,1)}, bf16[192,2048]{1,0:T(8,128)(2,1)S(1)}, u32[]{:S(2)}, u32[]{:S(2)}) %collective-permute-start.54) | collective-permute-done | bytes 786464 | tf_op jit(solution)/shard_map/ppermute | solution.py:496
  521.5 8.5 %weight_grads.4 = (bf16[4,2,128,2048]{3,2,1,0:T(8,128)(2,1)}, bf16[4,2,128,2048]{3,2,1,0:T(8,128)(2,1)}) custom-call(s32[1]{0:T(128)} %bitcast.75.core_ref, bf16[384,1024]{1,0:T(8,128)(2,1)S(1)} %pad_maximum_fusion.5.left_ref, bf16[192,2048]{1,0:T(8,128)(2,1)S(1)} %pad_maximum_fusion.4.refs_0_, bf16[192,2048]{1,0:T(8,128)(2,1)S(1)} %collective-permute-done.55.refs_1_, ...), custom_call_target="tpu_custom_call" | custom-call | tf_op jit(solution)/shard_map/weight_grads/pallas_call | solution.py:446
  549.5 4.8 weight_grads.5
  560.4 6.3 add_convert_fusion
  581.5 23.6 %collective-permute-done.65.refs_3_ = bf16[128,2048]{1,0:T(8,128)(2,1)S(1)} collective-permute-done((bf16[128,2048]{1,0:T(8,128)(2,1)S(1)}, bf16[128,2048]{1,0:T(8,128)(2,1)S(1)}, u32[]{:S(2)}, u32[]{:S(2)}) %collective-permute-start.65) | collective-permute-done | bytes 524320 | tf_op jit(solution)/shard_map/ppermute | solution.py:590
  605.1 9.6 %collective-permute-done.61 = bf16[4,1,128,2048]{3,2,1,0:T(8,128)(2,1)} collective-permute-done((bf16[4,1,128,2048]{3,2,1,0:T(8,128)(2,1)}, bf16[4,1,128,2048]{3,2,1,0:T(8,128)(2,1)}, u32[]{:S(2)}, u32[]{:S(2)}) %collective-permute-start.61) | collective-permute-done | bytes 2097184 | tf_op jit(solution)/shard_map/ppermute | solution.py:496
  631.2 18.3 %collective-permute-done.70 = f32[4,256,20]{1,0,2:T(4,128)S(1)} collective-permute-done((f32[4,256,20]{1,0,2:T(4,128)S(1)}, f32[4,256,20]{1,0,2:T(4,128)S(1)}, u32[]{:S(2)}, u32[]{:S(2)}) %collective-permute-start.70) | collective-permute-done | bytes 81952 | tf_op jit(solution)/shard_map/ppermute | solution.py:590
  651.9 5.1 add_rows.4
  671.9 15.3 %collective-permute-done.76 = f32[2,1,64,20]{2,0,3,1:T(2,128)S(1)} collective-permute-done((f32[2,1,64,20]{2,0,3,1:T(2,128)S(1)}, f32[2,1,64,20]{2,0,3,1:T(2,128)S(1)}, u32[]{:S(2)}, u32[]{:S(2)}) %collective-permute-start.76) | collective-permute-done | bytes 10272 | tf_op jit(solution)/shard_map/ppermute | solution.py:496
  692.7 8.5 %collective-permute-done.77 = f32[1,1,64,20]{2,0,3,1:T(1,128)S(1)} collective-permute-done((f32[1,1,64,20]{2,0,3,1:T(1,128)S(1)}, f32[1,1,64,20]{2,0,3,1:T(1,128)S(1)}, u32[]{:S(2)}, u32[]{:S(2)}) %collective-permute-start.77) | collective-permute-done | bytes 5152 | tf_op jit(solution)/shard_map/ppermute | solution.py:496
  (543 shorter events, 290.8 us)
Async XLA Ops:
  7.2 130.8 %all-gather.2.cloned.1.call-start = ((), (), s32[]{:S(2)}) async-start(), calls=%async_computation.2 | async-start | bytes 13369344 | tf_op jit(solution)/shard_map/all_gather | solution.py:642
  26.2 32.1 %collective-permute-start.7 = (bf16[192,2048]{1,0:T(8,128)(2,1)}, bf16[192,2048]{1,0:T(8,128)(2,1)}, u32[]{:S(2)}, u32[]{:S(2)}) collective-permute-start(bf16[192,2048]{1,0:T(8,128)(2,1)} %convolution_convert_fusion.1), channel_id=1, source_target_pairs={{0,4},{4,0},{1,5},{5,1},{2,6},{6,2},{3,7},{7,3},{8,12},{12,8},{9,1... | collective-permute-start | bytes 2359304 | tf_op jit(solution)/shard_map/ppermute | solution.py:590
  31.3 32.7 %collective-permute-start.5 = (bf16[192,2048]{1,0:T(8,128)(2,1)}, bf16[192,2048]{1,0:T(8,128)(2,1)}, u32[]{:S(2)}, u32[]{:S(2)}) collective-permute-start(bf16[192,2048]{1,0:T(8,128)(2,1)} %convolution_convert_fusion.2), channel_id=1, source_target_pairs={{0,4},{4,0},{1,5},{5,1},{2,6},{6,2},{3,7},{7,3},{8,12},{12,8},{9,1... | collective-permute-start | bytes 2359304 | tf_op jit(solution)/shard_map/ppermute | solution.py:590
  34.0 35.7 %collective-permute-start.2 = (bf16[1024,16]{1,0:T(8,128)(2,1)}, bf16[1024,16]{1,0:T(8,128)(2,1)}, u32[]{:S(2)}, u32[]{:S(2)}) collective-permute-start(bf16[1024,16]{1,0:T(8,128)(2,1)} %copy.114), channel_id=1, source_target_pairs={{0,4},{4,0},{1,5},{5,1},{2,6},{6,2},{3,7},{7,3},{8,12},{12,8},{9,1... | collective-permute-start | bytes 98312 | tf_op jit(solution)/shard_map/ppermute | solution.py:590
  51.9 34.5 %collective-permute-start.3 = (bf16[192,2048]{1,0:T(8,128)(2,1)}, bf16[192,2048]{1,0:T(8,128)(2,1)S(1)}, u32[]{:S(2)}, u32[]{:S(2)}) collective-permute-start(bf16[192,2048]{1,0:T(8,128)(2,1)} %convolution_convert_fusion.3), channel_id=1, source_target_pairs={{0,4},{4,0},{1,5},{5,1},{2,6},{6,2},{3,7},{7,3},{8,12},{12,8},{9,1... | collective-permute-start | bytes 2359304 | tf_op jit(solution)/shard_map/ppermute | solution.py:590
  60.3 31.7 %collective-permute-start.8 = (bf16[64,2048]{1,0:T(8,128)(2,1)S(1)}, bf16[64,2048]{1,0:T(8,128)(2,1)S(1)}, u32[]{:S(2)}, u32[]{:S(2)}) collective-permute-start(bf16[64,2048]{1,0:T(8,128)(2,1)S(1)} %get-tuple-element.513), channel_id=1, source_target_pairs={{0,4},{4,0},{1,5},{5,1},{2,6},{6,2},{3,7},{7,3},{8,12},{12,8},{9,1... | collective-permute-start | bytes 786440 | tf_op jit(solution)/shard_map/ppermute | solution.py:590
  67.8 28.2 %collective-permute-start.6 = (bf16[64,2048]{1,0:T(8,128)(2,1)S(1)}, bf16[64,2048]{1,0:T(8,128)(2,1)S(1)}, u32[]{:S(2)}, u32[]{:S(2)}) collective-permute-start(bf16[64,2048]{1,0:T(8,128)(2,1)S(1)} %get-tuple-element.515), channel_id=1, source_target_pairs={{0,4},{4,0},{1,5},{5,1},{2,6},{6,2},{3,7},{7,3},{8,12},{12,8},{9,1... | collective-permute-start | bytes 786440 | tf_op jit(solution)/shard_map/ppermute | solution.py:590
  117.1 27.3 %collective-permute-start.16 = (bf16[192,1024]{1,0:T(8,128)(2,1)}, bf16[192,1024]{1,0:T(8,128)(2,1)}, u32[]{:S(2)}, u32[]{:S(2)}) collective-permute-start(bf16[192,1024]{1,0:T(8,128)(2,1)} %pad_maximum_fusion.7), channel_id=1, source_target_pairs={{0,4},{4,0},{1,5},{5,1},{2,6},{6,2},{3,7},{7,3},{8,12},{12,8},{9,1... | collective-permute-start | bytes 1179656 | tf_op jit(solution)/shard_map/ppermute | solution.py:590
  138.0 31.8 %collective-permute-start.11 = (bf16[192,2048]{1,0:T(8,128)(2,1)S(1)}, bf16[192,2048]{1,0:T(8,128)(2,1)S(1)}, u32[]{:S(2)}, u32[]{:S(2)}) collective-permute-start(bf16[192,2048]{1,0:T(8,128)(2,1)S(1)} %multiply_convert_fusion.refs_0_), channel_id=1, source_target_pairs={{0,8},{8,0},{16,24},{24,16},{1,9},{9,1},{17,25},{25,17},{2,10},{10... | collective-permute-start | bytes 2359304 | tf_op jit(solution)/shard_map/ppermute | solution.py:496
  139.3 30.6 %collective-permute-start.12 = (bf16[192,2048]{1,0:T(8,128)(2,1)S(1)}, bf16[192,2048]{1,0:T(8,128)(2,1)S(1)}, u32[]{:S(2)}, u32[]{:S(2)}) collective-permute-start(bf16[192,2048]{1,0:T(8,128)(2,1)S(1)} %multiply_convert_fusion.refs_0_), channel_id=1, source_target_pairs={{0,16},{8,24},{16,0},{24,8},{1,17},{9,25},{17,1},{25,9},{2,18},{10... | collective-permute-start | bytes 2359304 | tf_op jit(solution)/shard_map/ppermute | solution.py:496
  141.9 27.9 %collective-permute-start.13 = (bf16[192,2048]{1,0:T(8,128)(2,1)S(1)}, bf16[192,2048]{1,0:T(8,128)(2,1)S(1)}, u32[]{:S(2)}, u32[]{:S(2)}) collective-permute-start(bf16[192,2048]{1,0:T(8,128)(2,1)S(1)} %multiply_convert_fusion.refs_0_), channel_id=1, source_target_pairs={{0,2},{1,3},{2,0},{3,1},{4,6},{5,7},{6,4},{7,5},{8,10},{9,11},{10,... | collective-permute-start | bytes 2359304 | tf_op jit(solution)/shard_map/ppermute | solution.py:496
  171.8 38.3 %collective-permute-start.22 = (bf16[192,2048]{1,0:T(8,128)(2,1)S(1)}, bf16[192,2048]{1,0:T(8,128)(2,1)S(1)}, u32[]{:S(2)}, u32[]{:S(2)}) collective-permute-start(bf16[192,2048]{1,0:T(8,128)(2,1)S(1)} %collective-permute-done.12.refs_0_), channel_id=1, source_target_pairs={{0,2},{1,3},{2,0},{3,1},{4,6},{5,7},{6,4},{7,5},{8,10},{9,11},{10,... | collective-permute-start | bytes 2359304 | tf_op jit(solution)/shard_map/ppermute | solution.py:496
  192.2 39.5 %collective-permute-start.21 = (bf16[192,2048]{1,0:T(8,128)(2,1)S(1)}, bf16[192,2048]{1,0:T(8,128)(2,1)S(1)}, u32[]{:S(2)}, u32[]{:S(2)}) collective-permute-start(bf16[192,2048]{1,0:T(8,128)(2,1)S(1)} %collective-permute-done.17.refs_2_), channel_id=1, source_target_pairs={{0,2},{1,3},{2,0},{3,1},{4,6},{5,7},{6,4},{7,5},{8,10},{9,11},{10,... | collective-permute-start | bytes 2359304 | tf_op jit(solution)/shard_map/ppermute | solution.py:496
  261.3 38.4 %collective-permute-start.33 = (bf16[192,2048]{1,0:T(8,128)(2,1)}, bf16[192,2048]{1,0:T(8,128)(2,1)}, u32[]{:S(2)}, u32[]{:S(2)}) collective-permute-start(bf16[192,2048]{1,0:T(8,128)(2,1)} %fusion.19), channel_id=1, source_target_pairs={{0,8},{8,0},{16,24},{24,16},{1,9},{9,1},{17,25},{25,17},{2,10},{10... | collective-permute-start | bytes 2359304 | tf_op jit(solution)/shard_map/ppermute | solution.py:496
  348.8 42.7 %collective-permute-start.40 = (bf16[4,2,192,2048]{3,2,1,0:T(8,128)(2,1)}, bf16[4,2,192,2048]{3,2,1,0:T(8,128)(2,1)}, u32[]{:S(2)}, u32[]{:S(2)}) collective-permute-start(bf16[4,2,192,2048]{3,2,1,0:T(8,128)(2,1)} %get-tuple-element.357), channel_id=1, source_target_pairs={{0,1},{1,0},{2,3},{3,2},{4,5},{5,4},{6,7},{7,6},{8,9},{9,8},{10,11... | collective-permute-start | bytes 18874376 | tf_op jit(solution)/shard_map/ppermute | solution.py:496
  348.8 42.7 %collective-permute-start.41 = (bf16[256,2048]{1,0:T(8,128)(2,1)}, bf16[256,2048]{1,0:T(8,128)(2,1)}, u32[]{:S(2)}, u32[]{:S(2)}) collective-permute-start(bf16[256,2048]{1,0:T(8,128)(2,1)} %bitcast.69), channel_id=1, source_target_pairs={{0,4},{4,0},{1,5},{5,1},{2,6},{6,2},{3,7},{7,3},{8,12},{12,8},{9,1... | collective-permute-start | bytes 3145736 | tf_op jit(solution)/shard_map/ppermute | solution.py:590
  352.8 38.6 %collective-permute-start.39 = (bf16[192,2048]{1,0:T(8,128)(2,1)}, bf16[192,2048]{1,0:T(8,128)(2,1)}, u32[]{:S(2)}, u32[]{:S(2)}) collective-permute-start(bf16[192,2048]{1,0:T(8,128)(2,1)} %fusion.18), channel_id=1, source_target_pairs={{0,16},{8,24},{16,0},{24,8},{1,17},{9,25},{17,1},{25,9},{2,18},{10... | collective-permute-start | bytes 2359304 | tf_op jit(solution)/shard_map/ppermute | solution.py:496
  354.4 37.0 %collective-permute-start.42 = (bf16[128,2048]{1,0:T(8,128)(2,1)}, bf16[128,2048]{1,0:T(8,128)(2,1)S(1)}, u32[]{:S(2)}, u32[]{:S(2)}) collective-permute-start(bf16[128,2048]{1,0:T(8,128)(2,1)} %bitcast.70), channel_id=1, source_target_pairs={{0,4},{4,0},{1,5},{5,1},{2,6},{6,2},{3,7},{7,3},{8,12},{12,8},{9,1... | collective-permute-start | bytes 1572872 | tf_op jit(solution)/shard_map/ppermute | solution.py:590
  355.9 35.5 %all-to-all-start.1 = ((f32[16,1,192]{2,1,0:T(1,128)}), f32[16,1,192]{2,1,0:T(1,128)S(1)}, u32[]{:S(2)}, u32[]{:S(2)}) async-start(f32[16,1,192]{2,1,0:T(1,128)} %copy.116), calls=%async_computation.1 | async-start | bytes 32768 | tf_op jit(solution)/shard_map/all_to_all | solution.py:799
  433.0 27.1 %collective-permute-start.48 = (bf16[256,2048]{1,0:T(8,128)(2,1)}, bf16[256,2048]{1,0:T(8,128)(2,1)}, u32[]{:S(2)}, u32[]{:S(2)}) collective-permute-start(bf16[256,2048]{1,0:T(8,128)(2,1)} %bitcast.77), channel_id=1, source_target_pairs={{0,4},{4,0},{1,5},{5,1},{2,6},{6,2},{3,7},{7,3},{8,12},{12,8},{9,1... | collective-permute-start | bytes 3145736 | tf_op jit(solution)/shard_map/ppermute | solution.py:590
  483.9 36.5 %collective-permute-start.54 = (bf16[192,2048]{1,0:T(8,128)(2,1)}, bf16[192,2048]{1,0:T(8,128)(2,1)S(1)}, u32[]{:S(2)}, u32[]{:S(2)}) collective-permute-start(bf16[192,2048]{1,0:T(8,128)(2,1)} %fusion.10), channel_id=1, source_target_pairs={{0,16},{8,24},{16,0},{24,8},{1,17},{9,25},{17,1},{25,9},{2,18},{10... | collective-permute-start | bytes 2359304 | tf_op jit(solution)/shard_map/ppermute | solution.py:496
  486.6 33.9 %collective-permute-start.56 = (bf16[192,2048]{1,0:T(8,128)(2,1)S(1)}, bf16[192,2048]{1,0:T(8,128)(2,1)S(1)}, u32[]{:S(2)}, u32[]{:S(2)}) collective-permute-start(bf16[192,2048]{1,0:T(8,128)(2,1)S(1)} %get-tuple-element.413.refs_2_), channel_id=1, source_target_pairs={{0,4},{4,0},{1,5},{5,1},{2,6},{6,2},{3,7},{7,3},{8,12},{12,8},{9,1... | collective-permute-start | bytes 2359304 | tf_op jit(solution)/shard_map/ppermute | solution.py:590
  490.3 46.0 %collective-permute-start.57 = (bf16[4,1,64,2048]{3,2,1,0:T(8,128)(2,1)S(1)}, bf16[4,1,64,2048]{3,2,1,0:T(8,128)(2,1)S(1)}, u32[]{:S(2)}, u32[]{:S(2)}) collective-permute-start(bf16[4,1,64,2048]{3,2,1,0:T(8,128)(2,1)S(1)} %get-tuple-element.485), channel_id=1, source_target_pairs={{0,2},{1,3},{2,0},{3,1},{4,6},{5,7},{6,4},{7,5},{8,10},{9,11},{10,... | collective-permute-start | bytes 3145736 | tf_op jit(solution)/shard_map/ppermute | solution.py:496
  566.7 48.0 %collective-permute-start.61 = (bf16[4,1,128,2048]{3,2,1,0:T(8,128)(2,1)}, bf16[4,1,128,2048]{3,2,1,0:T(8,128)(2,1)}, u32[]{:S(2)}, u32[]{:S(2)}) collective-permute-start(bf16[4,1,128,2048]{3,2,1,0:T(8,128)(2,1)} %get-tuple-element.481), channel_id=1, source_target_pairs={{0,2},{1,3},{2,0},{3,1},{4,6},{5,7},{6,4},{7,5},{8,10},{9,11},{10,... | collective-permute-start | bytes 6291464 | tf_op jit(solution)/shard_map/ppermute | solution.py:496
  568.1 46.7 %collective-permute-start.62 = (bf16[4,2,64,2048]{3,2,1,0:T(8,128)(2,1)}, bf16[4,2,64,2048]{3,2,1,0:T(8,128)(2,1)}, u32[]{:S(2)}, u32[]{:S(2)}) collective-permute-start(bf16[4,2,64,2048]{3,2,1,0:T(8,128)(2,1)} %get-tuple-element.435), channel_id=1, source_target_pairs={{0,1},{1,0},{2,3},{3,2},{4,5},{5,4},{6,7},{7,6},{8,9},{9,8},{10,11... | collective-permute-start | bytes 6291464 | tf_op jit(solution)/shard_map/ppermute | solution.py:496
  568.1 37.0 %collective-permute-start.66 = (bf16[256,2048]{1,0:T(8,128)(2,1)}, bf16[256,2048]{1,0:T(8,128)(2,1)}, u32[]{:S(2)}, u32[]{:S(2)}) collective-permute-start(bf16[256,2048]{1,0:T(8,128)(2,1)} %bitcast.91), channel_id=1, source_target_pairs={{0,4},{4,0},{1,5},{5,1},{2,6},{6,2},{3,7},{7,3},{8,12},{12,8},{9,1... | collective-permute-start | bytes 3145736 | tf_op jit(solution)/shard_map/ppermute | solution.py:590
  569.7 35.5 %collective-permute-start.65 = (bf16[128,2048]{1,0:T(8,128)(2,1)S(1)}, bf16[128,2048]{1,0:T(8,128)(2,1)S(1)}, u32[]{:S(2)}, u32[]{:S(2)}) collective-permute-start(bf16[128,2048]{1,0:T(8,128)(2,1)S(1)} %bitcast.296), channel_id=1, source_target_pairs={{0,4},{4,0},{1,5},{5,1},{2,6},{6,2},{3,7},{7,3},{8,12},{12,8},{9,1... | collective-permute-start | bytes 1572872 | tf_op jit(solution)/shard_map/ppermute | solution.py:590
  617.7 39.3 %collective-permute-start.68 = (bf16[2,1,128,2048]{3,2,1,0:T(8,128)(2,1)}, bf16[2,1,128,2048]{3,2,1,0:T(8,128)(2,1)}, u32[]{:S(2)}, u32[]{:S(2)}) collective-permute-start(bf16[2,1,128,2048]{3,2,1,0:T(8,128)(2,1)} %fusion.24), channel_id=1, source_target_pairs={{0,8},{8,0},{16,24},{24,16},{1,9},{9,1},{17,25},{25,17},{2,10},{10... | collective-permute-start | bytes 3145736 | tf_op jit(solution)/shard_map/ppermute | solution.py:496
  622.2 34.9 %collective-permute-start.67 = (bf16[4,1,64,2048]{3,2,1,0:T(8,128)(2,1)}, bf16[4,1,64,2048]{3,2,1,0:T(8,128)(2,1)}, u32[]{:S(2)}, u32[]{:S(2)}) collective-permute-start(bf16[4,1,64,2048]{3,2,1,0:T(8,128)(2,1)} %get-tuple-element.483), channel_id=1, source_target_pairs={{0,2},{1,3},{2,0},{3,1},{4,6},{5,7},{6,4},{7,5},{8,10},{9,11},{10,... | collective-permute-start | bytes 3145736 | tf_op jit(solution)/shard_map/ppermute | solution.py:496
  623.5 33.5 %collective-permute-start.72 = (bf16[256,2048]{1,0:T(8,128)(2,1)}, bf16[256,2048]{1,0:T(8,128)(2,1)S(1)}, u32[]{:S(2)}, u32[]{:S(2)}) collective-permute-start(bf16[256,2048]{1,0:T(8,128)(2,1)} %bitcast.103), channel_id=1, source_target_pairs={{0,4},{4,0},{1,5},{5,1},{2,6},{6,2},{3,7},{7,3},{8,12},{12,8},{9,1... | collective-permute-start | bytes 3145736 | tf_op jit(solution)/shard_map/ppermute | solution.py:590
  629.6 27.5 %collective-permute-start.69 = (bf16[1,1,64,2048]{3,2,1,0:T(8,128)(2,1)}, bf16[1,1,64,2048]{3,2,1,0:T(8,128)(2,1)}, u32[]{:S(2)}, u32[]{:S(2)}) collective-permute-start(bf16[1,1,64,2048]{3,2,1,0:T(8,128)(2,1)} %fusion.37), channel_id=1, source_target_pairs={{0,16},{8,24},{16,0},{24,8},{1,17},{9,25},{17,1},{25,9},{2,18},{10... | collective-permute-start | bytes 786440 | tf_op jit(solution)/shard_map/ppermute | solution.py:496
  659.1 28.2 %collective-permute-start.74 = (bf16[1,1,128,2048]{3,2,1,0:T(8,128)(2,1)S(1)}, bf16[1,1,128,2048]{3,2,1,0:T(8,128)(2,1)S(1)}, u32[]{:S(2)}, u32[]{:S(2)}) collective-permute-start(bf16[1,1,128,2048]{3,2,1,0:T(8,128)(2,1)S(1)} %fusion.26), channel_id=1, source_target_pairs={{0,16},{8,24},{16,0},{24,8},{1,17},{9,25},{17,1},{25,9},{2,18},{10... | collective-permute-start | bytes 1572872 | tf_op jit(solution)/shard_map/ppermute | solution.py:496
  (162 other events, 1680.3 us)
Sparse Core Ops, SparseCore 0:
  10.3 103.4 all-gather.1

commit v4 on v3

--- a/solution.py
+++ b/solution.py
@@ -61,14 +61,23 @@
     )(*parts, gain, cosine, sine)
 
 
-def post_back_kernel(grad_ref, raw_ref, gain_ref, cos_ref, sin_ref, low_ref, gain_grad_ref):
+def post_back_kernel(grad_ref, raw_ref, gain_ref, cos_ref, sin_ref, *refs):
+    got, (low_ref, gain_grad_ref, sum_ref) = refs[:-3], refs[-3:]
+    sum_ref[...] = grad_ref[...]
+    if got:
+
+        @pl.when(pl.program_id(0) == 0)
+        def _():
+            for ref in got:
+                sum_ref[...] += ref[...].astype(F32)
+
     raw = raw_ref[...]
     inverse = lax.rsqrt(jnp.mean(raw * raw, axis=-1, keepdims=True) + EPSILON)
     cosine, sine = cos_ref[...], sin_ref[...]
     head = cosine.shape[1]
     pieces = []
     for h in range(raw.shape[1] // head):
-        piece = grad_ref[:, h * head : (h + 1) * head]
+        piece = sum_ref[:, h * head : (h + 1) * head]
         pieces.append(piece * cosine - pltpu.roll(piece, head // 2, 1) * sine)
     grad = jnp.concatenate(pieces, axis=1)
     scaled = grad * gain_ref[...]
@@ -85,24 +94,100 @@
         gain_grad_ref[...] += total
 
 
-def qk_post_back(grad, raw, gain, cosine, sine):
+def qk_post_back(grad, raw, gain, cosine, sine, got=()):
     rows, width = raw.shape
     head = cosine.shape[1]
-    step = 64
+    step = got[0].shape[0] if got else 64
     row = lambda w: pl.BlockSpec((step, w), lambda i: (i, 0))
     whole = pl.BlockSpec((1, width), lambda i: (0, 0))
     return pl.pallas_call(
         post_back_kernel,
         grid=(rows // step,),
-        in_specs=[row(width), row(width), whole, row(head), row(head)],
+        in_specs=[row(width), row(width), whole, row(head), row(head)]
+        + [pl.BlockSpec((step, width), lambda i: (0, 0))] * len(got),
         out_specs=[row(width), whole],
         out_shape=[
             jax.ShapeDtypeStruct((rows, width), BF16),
             jax.ShapeDtypeStruct((1, width), F32),
         ],
+        scratch_shapes=[pltpu.VMEM((step, width), F32)],
         compiler_params=pltpu.CompilerParams(vmem_limit_bytes=VMEM_LIMIT),
         name="qk_post_back",
-    )(grad, raw, gain, cosine, sine)
+    )(grad, raw, gain, cosine, sine, *got)
+
+
+def row_specs(items, step):
+    pairs = [item if isinstance(item, tuple) else (item,) for item in items]
+
+    def spec(array, at):
+        width = array.shape[-1]
+        return pl.BlockSpec((None,) * len(at) + (step, width), lambda i: at + (i, 0))
+
+    return [p[0] for p in pairs], [spec(p[0], p[1:]) for p in pairs]
+
+
+def add_blocks(*items):
+    return plus(*[item[0][item[1:]] if isinstance(item, tuple) else item for item in items])
+
+
+def norm_back_kernel(count, *refs):
+    parts = refs[:count]
+    (
+        d_out_ref, mixed_ref, gain_ref, probs_ref, d_probs_ref, router_ref,
+        d_mixed_ref, branch_ref, d_logit_ref, gain_grad_ref,
+    ) = refs[count:]
+    probs, d_probs = probs_ref[...], d_probs_ref[...]
+    centre = jnp.sum(probs * d_probs, axis=1, keepdims=True)
+    d_logit = (probs * (d_probs - centre)).astype(BF16)
+    d_logit_ref[...] = d_logit
+    grad = dot(d_logit, router_ref[...], NT)
+    for part in parts:
+        grad = grad + part[...].astype(F32)
+    mixed = mixed_ref[...]
+    inverse = lax.rsqrt(jnp.mean(mixed * mixed, axis=-1, keepdims=True) + EPSILON)
+    scaled = grad * gain_ref[...]
+    centre = jnp.mean(scaled * mixed, axis=-1, keepdims=True)
+    d_mixed = (
+        d_out_ref[...].astype(F32)
+        + inverse * scaled
+        - mixed * (inverse * inverse * inverse * centre)
+    )
+    d_mixed_ref[...] = d_mixed
+    branch_ref[...] = d_mixed.astype(BF16)
+    total = jnp.sum(grad * mixed * inverse, axis=0, keepdims=True)
+
+    @pl.when(pl.program_id(0) == 0)
+    def _():
+        gain_grad_ref[...] = total
+
+    @pl.when(pl.program_id(0) > 0)
+    def _():
+        gain_grad_ref[...] += total
+
+
+def norm_back(parts, d_out, mixed, gain, probs, d_probs, router):
+    rows, width = mixed.shape
+    experts = probs.shape[1]
+    step = 64
+    row = lambda w: pl.BlockSpec((step, w), lambda i: (i, 0))
+    whole = lambda *shape: pl.BlockSpec(shape, lambda i: (0, 0))
+    parts, specs = row_specs(parts, step)
+    return pl.pallas_call(
+        functools.partial(norm_back_kernel, len(parts)),
+        grid=(rows // step,),
+        in_specs=specs
+        + [row(width)] * 2
+        + [whole(1, width), row(experts), row(experts), whole(width, experts)],
+        out_specs=[row(width), row(width), row(experts), whole(1, width)],
+        out_shape=[
+            jax.ShapeDtypeStruct((rows, width), F32),
+            jax.ShapeDtypeStruct((rows, width), BF16),
+            jax.ShapeDtypeStruct((rows, experts), BF16),
+            jax.ShapeDtypeStruct((1, width), F32),
+        ],
+        compiler_params=pltpu.CompilerParams(vmem_limit_bytes=VMEM_LIMIT),
+        name="norm_back",
+    )(*parts, d_out, mixed, gain, probs, d_probs, router)
 
 
 def read_mask(meta_ref, rows, keys, prompt_dev, prompt_total):
@@ -132,10 +217,19 @@
 
 
 def attend_back_kernel(
-    heads, prompt_dev, prompt_total, meta_ref, q_ref, k_ref, v_ref, d_ref, dq_ref, dk_ref, dv_ref
+    heads, prompt_dev, prompt_total, meta_ref, q_ref, k_ref, v_ref, d_ref,
+    dq_ref, dk_ref, dv_ref, dk_low_ref, dv_low_ref, rows_ref,
 ):
     mask = read_mask(meta_ref, q_ref.shape[0], k_ref.shape[0], prompt_dev, prompt_total)
     head = q_ref.shape[1] // heads
+    mine = pl.ds(pl.multiple_of(meta_ref[0], prompt_dev), prompt_dev)
+
+    def store(rows, own_ref, low_ref, at):
+        low_ref[:, at] = rows[:prompt_total].astype(BF16)
+        rows_ref[...] = rows[:prompt_total]
+        own_ref[:prompt_dev, at] = rows_ref[mine, :]
+        own_ref[prompt_dev:, at] = rows[prompt_total:]
+
     for h in range(heads):
         at = slice(h * head, (h + 1) * head)
         query, key, grad = q_ref[:, at], k_ref[:, at], d_ref[:, at]
@@ -144,11 +238,42 @@
         centre = jnp.sum(probs * d_probs, axis=-1, keepdims=True)
         d_scores = (probs * (d_probs - centre) * head**-0.5).astype(BF16)
         dq_ref[:, at] = dot(d_scores, key)
-        dk_ref[:, at] = dot(d_scores, query, TN)
-        dv_ref[:, at] = dot(probs.astype(BF16), grad, TN)
-
-
-def attention_call(kernel, name, arrays, outs, meta, prompt_dev, prompt_total):
+        store(dot(d_scores, query, TN), dk_ref, dk_low_ref, at)
+        store(dot(probs.astype(BF16), grad, TN), dv_ref, dv_low_ref, at)
+
+
+def value_kernel(own_ref, *refs):
+    got, low_ref = refs[:-1], refs[-1]
+
+    @pl.when(pl.program_id(0) == 0)
+    def _():
+        total = own_ref[...]
+        for ref in got:
+            total = total + ref[...].astype(F32)
+        low_ref[...] = total.astype(BF16)
+
+    @pl.when(pl.program_id(0) > 0)
+    def _():
+        low_ref[...] = own_ref[...].astype(BF16)
+
+
+def value_rows_low(own, got):
+    rows, width = own.shape
+    step = got[0].shape[0] if got else 64
+    row = pl.BlockSpec((step, width), lambda i: (i, 0))
+    first = pl.BlockSpec((step, width), lambda i: (0, 0))
+    return pl.pallas_call(
+        value_kernel,
+        grid=(rows // step,),
+        in_specs=[row] + [first] * len(got),
+        out_specs=row,
+        out_shape=jax.ShapeDtypeStruct((rows, width), BF16),
+        compiler_params=pltpu.CompilerParams(vmem_limit_bytes=VMEM_LIMIT),
+        name="value_rows",
+    )(own, *got)
+
+
+def attention_call(kernel, name, arrays, outs, meta, prompt_dev, prompt_total, scratch=()):
     width = arrays[0].shape[1]
     heads = 4
     spec = lambda a: pl.BlockSpec((a.shape[0], width * heads // HEADS), lambda i, m: (0, i))
@@ -159,6 +284,7 @@
             grid=(HEADS // heads,),
             in_specs=[spec(a) for a in arrays],
             out_specs=[spec(a) for a in outs],
+            scratch_shapes=scratch,
         ),
         out_shape=outs,
         compiler_params=pltpu.CompilerParams(vmem_limit_bytes=VMEM_LIMIT),
@@ -654,21 +780,34 @@
 
     def project(pieces, weight):
         products = [dot(pieces[r], weight).astype(BF16) for r in others]
-        products = fence(pieces[0], *products)
-        sent = [shift(product, planes - r) for r, product in zip(others, products[1:])]
-        return [dot(products[0], weight)] + sent
-
-    key_parts = project(normed_blocks, w_key)
-    key_parts[0], named, gains_in, w_router = fence(key_parts[0], named, gains_in, w_router)
-    gains = gathered(gains_in, 1).astype(F32)
+        fenced = fence(*pieces, *products)
+        pieces, products = fenced[:planes], fenced[planes:]
+        sent = [shift(product, planes - r) for r, product in zip(others, products)]
+        return [dot(pieces[0], weight)] + sent, pieces
+
+    def products(weight):
+        return [dot(normed_blocks[r], weight).astype(BF16) for r in others]
+
+    def shift_back(values):
+        return [shift(v, planes - r) for r, v in zip(others, values)]
+
+    key_low, value_low, named, gains_in, w_router, d_out_low, *normed_blocks = fence(
+        products(w_key), products(w_value), named, gains_in, w_router, d_out_low, *normed_blocks
+    )
+    key_got, value_got = shift_back(key_low), shift_back(value_low)
+    query_low = products(w_query)
+    key_own, value_own = dot(normed_blocks[0], w_key), dot(normed_blocks[0], w_value)
+    member = lax.all_to_all(named.T, PLANE, split_axis=0, concat_axis=0, tiled=True)
+    gains = gathered(gains_in, 1)
+    full_router = gathered(w_router, 0)
+    key_got, value_got, query_low, key_own, value_own, member, gains, full_router, *normed_blocks = fence(
+        key_got, value_got, query_low, key_own, value_own, member, gains, full_router, *normed_blocks
+    )
+    gains = gains.astype(F32)
     gain_attn, gain_query, gain_key, gain_ffn = [gains[i : i + 1] for i in range(4)]
-    full_router = gathered(w_router, 0)
-    member = lax.all_to_all(named.T, PLANE, split_axis=0, concat_axis=0, tiled=True)
-    value_parts = project(normed_blocks, w_value)
-    query_parts = project(normed_blocks, w_query)
-    key_raw, key_low = qk_post(key_parts, gain_key, cosine, sine)
-    value_low = sum(p.astype(F32) for p in value_parts).astype(BF16)
-    query_parts[0], full_router, member = fence(query_parts[0], full_router, member)
+    query_parts = [dot(normed_blocks[0], w_query)] + shift_back(query_low)
+    key_raw, key_low = qk_post([key_own, *key_got], gain_key, cosine, sine)
+    value_low = plus(value_own, *value_got).astype(BF16)
     query_raw, query_low = qk_post(query_parts, gain_query, cosine, sine)
 
     def with_prompt(rows):
@@ -696,7 +835,7 @@
     )
 
     attended_blocks = [block(attended, 0)] + [shift(block(attended, r), r) for r in others]
-    mixed_rows = x_rows + sum(p.astype(F32) for p in project(attended_blocks, w_output))
+    mixed_rows = x_rows + sum(p.astype(F32) for p in project(attended_blocks, w_output)[0])
     inverse2 = lax.rsqrt(jnp.mean(mixed_rows * mixed_rows, axis=-1, keepdims=True) + EPSILON)
     normed2_low = (mixed_rows * inverse2 * gain_ffn).astype(BF16)
 
@@ -763,10 +902,10 @@
     x3, x2c, send2, *kept = fence(x3, x2c, send2, *kept)
     x3c, near2, near0 = core(x3), core(send2), core(send0)
     x3c, near2, near0, *kept = fence(x3c, near2, near0, *kept)
-    pair2 = plus(keep2, near2)
-    got21 = across(pair2[1])
+    got21 = across(add_blocks((keep2, 1), (near2, 1)))
+    pair20 = add_blocks((keep2, 0), (near2, 0))
     kept, keep3, send3, dprob3 = quarter(3, (x2, x2c, x3, x3c), kept)
-    got21, pair20, send3, *kept = fence(got21, pair2[0], send3, *kept)
+    got21, pair20, send3, *kept = fence(got21, pair20, send3, *kept)
     got20, near3 = across(pair20), core(send3)
     kept, keep1, send1, dprob1 = quarter(1, (b2, c2, b3, c3), kept)
     got20, near3, send1, *kept = fence(got20, near3, send1, *kept)
@@ -777,93 +916,94 @@
     def send_rows(values):
         return [shift(values[r - 1], r) for r in others]
 
-    pair3 = plus(keep3, near3)
-    first_got, got31, near1 = z1(plus(keep0[1], near0[1], got21)), across(pair3[1]), core(send1)
+    first_got, near1 = z1(add_blocks((keep0, 1), (near0, 1), got21)), core(send1)
+    got31 = across(add_blocks((keep3, 1), (near3, 1)))
+    pair30 = add_blocks((keep3, 0), (near3, 0))
     *gate_low, gate_own = row_grads(me, planes, d_gate, slot_in, (1, 1))
-    first_got, got31, near1, gate_own, pair30, d_up, slot_in, *gate_low = fence(
-        first_got, got31, near1, gate_own, pair3[0], d_up, slot_in, *gate_low
-    )
-    second_got, got30 = z1(plus(keep1[1], near1[1], got31)), across(pair30)
-    gate_a = send_rows(gate_low[0])
-    *up_low, up_own = row_grads(me, planes, d_up, slot_in, (1, 2, 1))
-    place = jnp.zeros((owners,), jnp.int32).at[source].set(jnp.arange(owners, dtype=jnp.int32))
+    towards = jnp.arange(owners, dtype=jnp.int32)
+    i_of, j_of = (towards // rows_d) ^ my_e, (towards % rows_d) ^ my_d
+    place = (j_of // 2) * 8 + (i_of // 2) * 4 + (i_of % 2) * 2 + j_of % 2
     token_dprob = jnp.take(
         jnp.concatenate([dprob0, dprob1, dprob2, dprob3], axis=0), place, axis=0
     )
-    second_got, got30, token_dprob, act_low, up_own, gate_b, up_0, up_1, up_2, *gate_a = fence(
-        second_got, got30, token_dprob, act_low, up_own, gate_low[1], *up_low, *gate_a
-    )
-    far_got = z2(plus(keep1[0], near1[0], got30, second_got))
+    first_got, got31, near1, gate_own, pair30, d_up, slot_in, token_dprob, *gate_low = fence(
+        first_got, got31, near1, gate_own, pair30, d_up, slot_in, token_dprob, *gate_low
+    )
+    dprobs = lax.all_to_all(token_dprob, PLANE, split_axis=0, concat_axis=0, tiled=True).T
+    second_got, got30 = z1(add_blocks((keep1, 1), (near1, 1), got31)), across(pair30)
+    gate_a = send_rows(gate_low[0])
+    *up_low, up_own = row_grads(me, planes, d_up, slot_in, (2, 4, 2))
+    second_got, got30, dprobs, act_low, up_own, gate_b, up_0, up_1, up_2, *gate_a = fence(
+        second_got, got30, dprobs, act_low, up_own, gate_low[1], *up_low, *gate_a
+    )
+    far_got = z2(add_blocks((keep1, 0), (near1, 0), got30, second_got))
     gate_b, up_a = send_rows(gate_b), send_rows(up_0)
     out_keep, out_send = expert_out(pick, act_low, down_w)
-    dprobs = lax.all_to_all(token_dprob, PLANE, split_axis=0, concat_axis=0, tiled=True).T
+    far_got, act_low, out_keep, out_send, *rest = fence(
+        far_got, act_low, out_keep, out_send, *gate_b, *up_a
+    )
+    gate_b, up_a = rest[: planes - 1], rest[planes - 1 :]
+
     out_near = core(out_send)
-    far_got, dprobs, act_low, out_keep, out_near, *rest = fence(
-        far_got, dprobs, act_low, out_keep, out_near, *gate_b, *up_a
-    )
-    gate_b, up_a = rest[: planes - 1], rest[planes - 1 :]
-    d_normed2_moe = (
-        keep0[0].astype(F32)
-        + near0[0].astype(F32)
-        + got20.astype(F32)
-        + first_got.astype(F32)
-        + far_got.astype(F32)
-    )
-
-    d_out = d_out_low.astype(F32)
-    dlogit_low = (
-        router_probs * (dprobs - jnp.sum(router_probs * dprobs, axis=1, keepdims=True))
-    ).astype(BF16)
+    d_mixed, branch_low, dlogit_low, ffn_gain_grad = norm_back(
+        [(keep0, 0), (near0, 0), got20, first_got, far_got],
+        d_out_low,
+        mixed_rows,
+        gain_ffn,
+        router_probs,
+        dprobs,
+        full_router,
+    )
     router_grad = dot(normed2_low, dlogit_low, TN)
-    d_normed2 = d_normed2_moe + dot(dlogit_low, full_router, NT)
-    scaled2 = gain_ffn * d_normed2
-    centre2 = jnp.mean(scaled2 * mixed_rows, axis=-1, keepdims=True)
-    d_mixed = d_out + inverse2 * scaled2 - mixed_rows * (inverse2**3 * centre2)
-    ffn_gain_grad = jnp.sum(d_normed2 * mixed_rows * inverse2, axis=0)
-
-    branch_low = d_mixed.astype(BF16)
+    branch_low, act_low, out_near = fence(branch_low, act_low, out_near)
+
     def out_sum(q, i):
-        return plus(out_keep[q, i], out_near[q, i])
-
-    branch_low, out31, act_low = fence(branch_low, out_sum(3, 1), act_low)
+        return add_blocks((out_keep, q, i), (out_near, q, i))
+
     sent = [shift(branch_low, r) for r in others]
-    out_got31 = across(out31)
-    *down_low, down_own = row_grads(me, planes, act_low, slot_cot, (1, 1))
-    out30 = out_sum(3, 0)
-    out_got31, out30, out_keep, out_near, down_own, down_0, down_1, branch_low, *sent = fence(
-        out_got31, out30, out_keep, out_near, down_own, *down_low, branch_low, *sent
+    out_got31, out_got30 = across(out_sum(3, 1)), across(out_sum(3, 0))
+    *down_low, down_own = row_grads(me, planes, act_low, slot_cot, (1, 4, 3))
+    out_got31, out_keep, out_near, down_own, down_0, down_1, down_2, branch_low, *sent = fence(
+        out_got31, out_keep, out_near, down_own, *down_low, branch_low, *sent
     )
     branches = [branch_low, *sent]
     blocks_low = [dot(branches[r], w_output, NT).astype(BF16) for r in others]
     d_att_blocks = [shift(v, planes - r) for r, v in zip(others, blocks_low)]
     d_att_own = dot(branches[0], w_output, NT).astype(BF16)
-    out_second = plus(out_keep[1, 1], out_near[1, 1], out_got31)
-    d_att_own, up_1, out_second, gate_own, branch_low, *d_att_blocks = fence(
-        d_att_own, up_1, out_second, gate_own, branch_low, *d_att_blocks
+    out_second = add_blocks((out_keep, 1, 1), (out_near, 1, 1), out_got31)
+    out21 = out_sum(2, 1)
+    d_att_own, up_1, out_second, out_got30, out21, gate_own, branch_low, *d_att_blocks = fence(
+        d_att_own, up_1, out_second, out_got30, out21, gate_own, branch_low, *d_att_blocks
     )
     branches[0] = branch_low
     d_attended = placed([d_att_own, *d_att_blocks])
 
-    key_total = prompt_total + cont_len
-    out_got30, out_second = across(out30), z1(out_second)
+    out_got21, out_second = across(out21), z1(out_second)
     up_b = send_rows(up_1)
     output_keep, output_send = weight_grads(attended_out, branches)
-    d_queries, d_keys_all, d_values_all = attention_call(
+    d_queries, d_keys, d_values_own, d_keys_low, d_values_low = attention_call(
         attend_back_kernel,
         "attend_back",
         [query_low, key_set, value_set, d_attended],
         [
             jax.ShapeDtypeStruct((tokens, width), F32),
-            jax.ShapeDtypeStruct((key_total, width), F32),
-            jax.ShapeDtypeStruct((key_total, width), F32),
+            jax.ShapeDtypeStruct((tokens, width), F32),
+            jax.ShapeDtypeStruct((tokens, width), F32),
+            jax.ShapeDtypeStruct((prompt_total, width), BF16),
+            jax.ShapeDtypeStruct((prompt_total, width), BF16),
         ],
         meta,
         prompt_dev,
         prompt_total,
-    )
-    out21 = out_sum(2, 1)
-    out_got30, out_second, output_keep, output_send, out21, d_queries, d_keys_all, d_values_all, *up_b = fence(
-        out_got30, out_second, output_keep, output_send, out21, d_queries, d_keys_all, d_values_all, *up_b
+        [pltpu.VMEM((prompt_total, head_dim), F32)],
+    )
+    out20 = out_sum(2, 0)
+    (
+        out_got21, out_second, output_keep, output_send, out20,
+        d_queries, d_keys, d_values_own, d_keys_low, d_values_low, *up_b,
+    ) = fence(
+        out_got21, out_second, output_keep, output_send, out20,
+        d_queries, d_keys, d_values_own, d_keys_low, d_values_low, *up_b,
     )
     output_rows = RowScatter(output_keep, output_send)
 
@@ -872,28 +1012,28 @@
             shift(
                 lax.dynamic_slice_in_dim(
                     rows, ((me + r) % planes) * prompt_dev, prompt_dev, axis=0
-                ).astype(BF16),
+                ),
                 r,
             )
             for r in others
         ]
 
-    def own_keys(rows, got):
-        total = lax.dynamic_slice_in_dim(rows, me * prompt_dev, prompt_dev, axis=0)
-        for part in got:
-            total = total + part.astype(F32)
-        return jnp.concatenate([total, rows[prompt_total:]], axis=0)
-
-    value_prompt, key_prompt = prompt_sent(d_values_all), prompt_sent(d_keys_all)
-    out_got21, output_got = across(out21), output_rows.start()
+    value_prompt, key_prompt = prompt_sent(d_values_low), prompt_sent(d_keys_low)
+    out_got20, output_got = across(out20), output_rows.start()
     d_query_low, query_gain_grad = qk_post_back(d_queries, query_raw, gain_query, cosine, sine)
-    out20, out_far = out_sum(2, 0), plus(out_keep[1, 0], out_near[1, 0], out_got30, out_second)
-    out_got21, output_got, out20, out_far, d_query_low, gate_own, *rest = fence(
-        out_got21, output_got, out20, out_far, d_query_low, gate_own, *value_prompt, *key_prompt
+    half = tokens // 2
+    query_got_a = [shift(d_query_low[:half], r) for r in others]
+    out_far = add_blocks((out_keep, 1, 0), (out_near, 1, 0), out_got30, out_second)
+    out_first = z1(add_blocks((out_keep, 0, 1), (out_near, 0, 1), out_got21))
+    out_got20, output_got, out_far, out_first, d_query_low, gate_own, *rest = fence(
+        out_got20, output_got, out_far, out_first, d_query_low, gate_own,
+        *value_prompt, *key_prompt, *query_got_a,
     )
     output_rows.finish(output_got)
-    d_value_low = own_keys(d_values_all, rest[: planes - 1]).astype(BF16)
-    d_keys = own_keys(d_keys_all, rest[planes - 1 :])
+    value_prompt, key_prompt, query_got_a = (
+        rest[k * (planes - 1) : (k + 1) * (planes - 1)] for k in range(3)
+    )
+    d_value_low = value_rows_low(d_values_own, value_prompt)
 
     def spread(low):
         return [shift(low, r) for r in others]
@@ -903,55 +1043,71 @@
             own = add_rows(own, [p[k] for p in parts])
         return own
 
-    d_value_low, d_keys = fence(d_value_low, d_keys)
-    got = spread(d_value_low) + spread(d_query_low)
-    out_got20, out_far = across(out20), z2(out_far)
-    d_key_low, key_gain_grad = qk_post_back(d_keys, key_raw, gain_key, cosine, sine)
+    d_value_low, *key_prompt = fence(d_value_low, *key_prompt)
+    got = spread(d_value_low) + [shift(d_query_low[half:], r) for r in others]
+    out_far_a, output_got = z2(out_far[:half]), output_rows.start()
+    d_key_low, key_gain_grad = qk_post_back(
+        d_keys, key_raw, gain_key, cosine, sine, key_prompt
+    )
     gate_grad = total(gate_own, gate_a, gate_b)
-    out_first = plus(out_keep[0, 1], out_near[0, 1], out_got21)
-    out_got20, out_far, out_first, d_key_low, gate_grad, *rest = fence(
-        out_got20, out_far, out_first, d_key_low, gate_grad, *got
-    )
-    d_values, d_query_got = rest[: planes - 1], rest[planes - 1 :]
-
-    got, output_got, out_first = spread(d_key_low), output_rows.start(), z1(out_first)
-    early_keep, early_send = weight_grads(
-        normed_out, [d_value_low, *d_values], [d_query_low, *d_query_got]
-    )
+    out_far_a, out_far_b, output_got, d_key_low, gate_grad, *rest = fence(
+        out_far_a, out_far[half:], output_got, d_key_low, gate_grad, *got
+    )
+    d_values = rest[: planes - 1]
+    d_query_got = [
+        jnp.concatenate([top, bottom], axis=0)
+        for top, bottom in zip(query_got_a, rest[planes - 1 :])
+    ]
+    output_rows.finish(output_got)
+
+    got, output_got, out_far_b = spread(d_key_low), output_rows.start(), z2(out_far_b)
+    value_pair = weight_grads(normed_out, [d_value_low, *d_values])
+    query_pair = weight_grads(normed_out, [d_query_low, *d_query_got])
     partial = [
         dot(d_values[k], w_value, NT) + dot(d_query_got[k], w_query, NT) for k in range(planes - 1)
     ]
-    output_got, out_first, early_keep, early_send, *rest = fence(
-        output_got, out_first, early_keep, early_send, *got, *partial
+    output_got, out_far_b, value_pair, query_pair, up_2, down_0, *rest = fence(
+        output_got, out_far_b, value_pair, query_pair, up_2, down_0, *got, *partial
     )
     d_key_got, partial = rest[: planes - 1], rest[planes - 1 :]
     output_rows.finish(output_got)
-    early_rows = RowScatter(early_keep, early_send)
+    value_rows, query_rows = RowScatter(*value_pair), RowScatter(*query_pair)
     out_rows = (
         mixed_rows
         + plus(out_keep[0, 0].astype(F32), out_near[0, 0])
         + out_got20.astype(F32)
         + out_first.astype(F32)
-        + out_far.astype(F32)
-    )
-
-    early_got = early_rows.start()
-    key_keep, key_send = weight_grads(normed_out, [d_key_low, *d_key_got])
+        + jnp.concatenate([out_far_a, out_far_b], axis=0).astype(F32)
+    )
+
+    value_got, query_got = value_rows.start(), query_rows.start()
+    key_pair = weight_grads(normed_out, [d_key_low, *d_key_got])
     blocks_low = [
         (partial[k] + dot(d_key_got[k], w_key, NT)).astype(BF16) for k in range(planes - 1)
     ]
-    early_got, key_keep, key_send, up_2, down_0, *blocks_low = fence(
-        early_got, key_keep, key_send, up_2, down_0, *blocks_low
-    )
-    early_rows.finish(early_got)
-    key_rows = RowScatter(key_keep, key_send)
+    value_got, query_got, key_pair, d_key_low, *blocks_low = fence(
+        value_got, query_got, key_pair, d_key_low, *blocks_low
+    )
+    value_rows.finish(value_got)
+    query_rows.finish(query_got)
+    key_rows = RowScatter(*key_pair)
 
     d_normed_got = [shift(v, planes - r) for r, v in zip(others, blocks_low)]
-    early_got, key_got, output_got = early_rows.start(), key_rows.start(), output_rows.start()
+    value_got, output_got, key_got = value_rows.start(), output_rows.start(), key_rows.start()
     up_c, down_a = send_rows(up_2), send_rows(down_0)
     d_normed_own = (
         dot(d_value_low, w_value, NT) + dot(d_query_low, w_query, NT) + dot(d_key_low, w_key, NT)
     )
+    value_got, output_got, key_got, d_normed_own, down_1, *rest = fence(
+        value_got, output_got, key_got, d_normed_own, down_1, *d_normed_got, *up_c, *down_a
+    )
+    d_normed_got, up_c, down_a = (rest[k * (planes - 1) : (k + 1) * (planes - 1)] for k in range(3))
+    value_rows.finish(value_got)
+    output_rows.finish(output_got)
+    key_rows.finish(key_got)
+
+    query_got, value_got = query_rows.start(), value_rows.start()
+    down_b = send_rows(down_1)
     d_normed = placed([d_normed_own] + [p.astype(F32) for p in d_normed_got])
     scaled = gain_attn * d_normed
     centre = jnp.mean(scaled * x_rows, axis=-1, keepdims=True)
@@ -960,53 +1116,56 @@
     attn_gain_grad = jnp.sum(d_normed * x_rows * inv, axis=0)
     small_grads = jnp.concatenate(
         [
-            jnp.stack([attn_gain_grad, query_gain_grad[0], key_gain_grad[0], ffn_gain_grad], axis=1),
+            jnp.stack(
+                [attn_gain_grad, query_gain_grad[0], key_gain_grad[0], ffn_gain_grad[0]], axis=1
+            ),
             router_grad,
         ],
         axis=1,
     )
-    early_got, key_got, output_got, d_x, small_grads, down_1, *rest = fence(
-        early_got, key_got, output_got, d_x, small_grads, down_1, *up_c, *down_a
-    )
-    up_c, down_a = rest[: planes - 1], rest[planes - 1 :]
-    early_rows.finish(early_got)
-    key_rows.finish(key_got)
-    output_rows.finish(output_got)
-
-    key_got, early_got, output_got = key_rows.start(), early_rows.start(), output_rows.start()
-    down_b = send_rows(down_1)
+    query_got, value_got, d_x, small_grads, down_2, *down_b = fence(
+        query_got, value_got, d_x, small_grads, down_2, *down_b
+    )
+    query_rows.finish(query_got)
+    value_rows.finish(value_got)
+
+    def laid(own, *parts):
+        for k in range(planes - 1):
+            own = own + jnp.concatenate([p[k] for p in parts], axis=0).astype(F32)
+        return own
+
+    key_got, query_got, value_got = key_rows.start(), query_rows.start(), value_rows.start()
     by_plane = small_grads.reshape(rows_e, planes, out_group, small_grads.shape[1])
 
     def plane_rows(r):
         return lax.dynamic_index_in_dim(by_plane, (me + r) % planes, 1, False)
 
     small_sum = plus(plane_rows(0), *[shift(plane_rows(r), r) for r in others])
+    down_c = send_rows(down_2)
+    up_grad = laid(up_own, up_a, up_b, up_c)
+    key_got, query_got, value_got, small_sum, up_grad, *down_c = fence(
+        key_got, query_got, value_got, small_sum, up_grad, *down_c
+    )
+    key_rows.finish(key_got)
+    query_rows.finish(query_got)
+    value_rows.finish(value_got)
+
+    key_got, query_got = key_rows.start(), query_rows.start()
     small_rows = RowScatter(
         *split([small_sum.reshape(rows_e, rows_d, -1, small_sum.shape[-1])], *STAGES[0])
     )
-    small_rows.finish(small_rows.start())
-    up_grad = total(up_own, up_a, up_b, up_c)
-    key_got, early_got, output_got, small_rows.parts, up_grad, *down_b = fence(
-        key_got, early_got, output_got, small_rows.parts, up_grad, *down_b
+    for _ in range(2):
+        small_rows.finish(small_rows.start())
+    down_grad = laid(down_own, down_a, down_b, down_c)
+    key_got, query_got, small_rows.parts, down_grad = fence(
+        key_got, query_got, small_rows.parts, down_grad
     )
     key_rows.finish(key_got)
-    early_rows.finish(early_got)
-    output_rows.finish(output_got)
-
-    key_got, early_got = key_rows.start(), early_rows.start()
-    small_rows.finish(small_rows.start())
-    small_rows.finish(small_rows.start())
-    down_grad = total(down_own, down_a, down_b)
-    key_got, early_got, small_rows.parts, down_grad = fence(
-        key_got, early_got, small_rows.parts, down_grad
-    )
-    key_rows.finish(key_got)
-    early_rows.finish(early_got)
+    query_rows.finish(query_got)
     key_rows.finish(key_rows.start())
-    small_rows.finish(small_rows.start())
+    for _ in range(2):
+        small_rows.finish(small_rows.start())
     small_grads = small_rows.result()
-    early_grads = early_rows.result().astype(F32)
-    size = early_grads.shape[0] // 2
     return (
         out_rows[:prompt_dev].astype(BF16)[None],
         out_rows[prompt_dev:].astype(BF16)[None, None],
@@ -1016,9 +1175,9 @@
         small_grads[:, 1],
         small_grads[:, 2],
         small_grads[:, 3],
-        early_grads[size:],
+        query_rows.result().astype(F32),
         key_rows.result().astype(F32),
-        early_grads[:size],
+        value_rows.result().astype(F32),
         output_rows.result().astype(F32),
         small_grads[:, 4:],
         gate_grad[None],

time: 718 us -> 688 us (0.958)
  waiting for transfers between devices: 236 us -> 189 us
  other arithmetic: 73.4 us -> 90.1 us
  starting transfers between devices: 85.3 us -> 98 us
    all_to_all x1, waiting for transfers between devices: 31.5 us -> 0.01 us  [shards(): lax.all_to_all(token_dprob, PLANE, split_axis=0, concat_axis=0, tiled=True)]
    ppermute x50 -> x55, waiting for transfers between devices: 88.6 us -> 66.2 us  [swap(): lax.ppermute(value, axis, [(i, i ^ bit) for i in range(lax.axis_size(axis...]
    ppermute x50 -> x55, starting transfers between devices: 41.9 us -> 54.3 us  [swap(): lax.ppermute(value, axis, [(i, i ^ bit) for i in range(lax.axis_size(axis...]
    ppermute x29 -> x31, waiting for transfers between devices: 111 us -> 123 us  [shift(): lax.ppermute(value, 'context', [(i, (i + r) % planes) for i in range(plan...]
    add x1 -> x2, other arithmetic: 0.05 us -> 9.66 us  [laid(): own = own + jnp.concatenate([p[k] for p in parts], axis=0).astype(F32)]
    pallas_call x3 -> x1, Pallas kernels: 13.8 us -> 4.33 us  [add_rows(): pl.pallas_call(functools.partial(add_rows_kernel, counts), grid=(own.shap...]
    convert_element_type x22 -> x25, other arithmetic: 50.9 us -> 56.7 us  [plus(): return sum((v.astype(F32) for v in values)).astype(values[0].dtype)]
    dot_general x21 -> x20, matrix products: 44.6 us -> 38.8 us  [dot(): lax.dot_general(left, right, (dims, ((), ())), preferred_element_type=out)]
  transfers between devices with their start and end apart: 82 -> 89, of which waited for: 34 -> 33; matrix products, arithmetic and copies ran while one was open for 17% -> 20% of each run, Pallas kernels for 26% -> 29%
where the time goes in v4:
time: 688 us; the launch traced here: 682 us
  Pallas kernels  201 us (29%)
  waiting for transfers between devices  189 us (27%)
  starting transfers between devices  98 us (14%)
  other arithmetic  90.1 us (13%)
  local copies, waits for them, and re-layouts  48.3 us (7%)
  matrix products  38.8 us (6%)
  between operations  16.6 us (2%)
    ppermute x31, waiting for transfers between devices, shift(): lax.ppermute(value, 'context', [(i, (i + r) % planes) for i in range(plan...  123 us
    pallas_call x4, Pallas kernels, expert_quarter(): pl.pallas_call(expert_kernel, grid=(hidden // tile,), in_specs=[whole(tok...  67.5 us
    ppermute x55, waiting for transfers between devices, swap(): lax.ppermute(value, axis, [(i, i ^ bit) for i in range(lax.axis_size(axis...  66.2 us
    convert_element_type x25, other arithmetic, plus(): return sum((v.astype(F32) for v in values)).astype(values[0].dtype)  56.7 us
    ppermute x55, starting transfers between devices, swap(): lax.ppermute(value, axis, [(i, i ^ bit) for i in range(lax.axis_size(axis...  54.3 us
    pallas_call x3, Pallas kernels, row_grads(): pl.pallas_call(functools.partial(row_grads_kernel, cuts), grid_spec=pltpu...  39.3 us
    dot_general x20, matrix products, dot(): lax.dot_general(left, right, (dims, ((), ())), preferred_element_type=out)  38.8 us
    ppermute x31, starting transfers between devices, shift(): lax.ppermute(value, 'context', [(i, (i + r) % planes) for i in range(plan...  34 us
  transfers between devices with their start and end apart: 89, of which 33 were waited for; matrix products, arithmetic and copies ran while one was open for 20% of the time, Pallas kernels for 29%

profile of v4, /device:TPU:0, one launch (start us, length us, event | category | flops | bytes accessed | tf_op | source)
XLA Modules:
  0.0 682.5 jit_solution(8833026109740388249)
XLA Ops:
  14.8 8.6 %collective-permute-done = bf16[192,1024]{1,0:T(8,128)(2,1)S(1)} collective-permute-done((bf16[192,1024]{1,0:T(8,128)(2,1)S(1)}, bf16[192,1024]{1,0:T(8,128)(2,1)S(1)}, u32[]{:S(2)}, u32[]{:S(2)}) %collective-permute-start) | collective-permute-done | bytes 393248 | tf_op jit(solution)/shard_map/ppermute | solution.py:716
  32.5 6.1 all-to-all-start
  51.0 16.5 %collective-permute-done.4 = bf16[4,1024]{1,0:T(4,128)(2,1)S(1)} collective-permute-done((bf16[4,1024]{1,0:T(4,128)(2,1)S(1)}, bf16[4,1024]{1,0:T(4,128)(2,1)S(1)}, u32[]{:S(2)}, u32[]{:S(2)}) %collective-permute-start.4) | collective-permute-done | bytes 8224 | tf_op jit(solution)/shard_map/ppermute | solution.py:716
  80.7 17.3 %collective-permute-done.7 = bf16[64,2048]{1,0:T(8,128)(2,1)S(1)} collective-permute-done((bf16[64,2048]{1,0:T(8,128)(2,1)S(1)}, bf16[64,2048]{1,0:T(8,128)(2,1)S(1)}, u32[]{:S(2)}, u32[]{:S(2)}) %collective-permute-start.7) | collective-permute-done | bytes 262176 | tf_op jit(solution)/shard_map/ppermute | solution.py:716
  101.9 4.8 attend.1
  110.2 5.6 collective-permute-done.9
  123.3 16.1 %collective-permute-done.10 = bf16[192,2048]{1,0:T(8,128)(2,1)S(1)} collective-permute-done((bf16[192,2048]{1,0:T(8,128)(2,1)S(1)}, bf16[192,2048]{1,0:T(8,128)(2,1)S(1)}, u32[]{:S(2)}, u32[]{:S(2)}) %collective-permute-start.10) | collective-permute-done | bytes 786464 | tf_op jit(solution)/shard_map/ppermute | solution.py:716
  152.0 21.4 %gather_cot.1 = (bf16[1792,2048]{1,0:T(8,128)(2,1)}, f32[1792,1024]{1,0:T(8,128)}) custom-call(s32[16]{0:T(128)S(1)} %stack.98.source_ref, bf16[16,192,2048]{2,1,0:T(8,128)(2,1)} %bitcast.302, bf16[16,192,2048]{2,1,0:T(8,128)(2,1)} %bitcast.303, bf16[16,192,2048]{2,1,0:T(8,128)(2,1)} %bitcast.304, bf16[16,192,2048]{2,1,0:T(8,128)(2,1)} %bitcast.305, ...), custom_call_target="tpu_custom_call" | custom-call | tf_op jit(solution)/shard_map/gather_cot/pallas_call | solution.py:466
  176.6 16.6 %collective-permute-done.19.refs_2_ = bf16[192,2048]{1,0:T(8,128)(2,1)S(1)} collective-permute-done((bf16[192,2048]{1,0:T(8,128)(2,1)S(1)}, bf16[192,2048]{1,0:T(8,128)(2,1)S(1)}, u32[]{:S(2)}, u32[]{:S(2)}) %collective-permute-start.19) | collective-permute-done | bytes 786464 | tf_op jit(solution)/shard_map/ppermute | solution.py:622
  195.5 16.9 %expert.4 = (bf16[1792,2048]{1,0:T(8,128)(2,1)}, bf16[1792,1024]{1,0:T(8,128)(2,1)}, bf16[1792,1024]{1,0:T(8,128)(2,1)}, bf16[1792,1024]{1,0:T(8,128)(2,1)}, bf1...) custom-call(bf16[192,2048]{1,0:T(8,128)(2,1)S(1)} %multiply_convert_fusion.refs_0_, ...), custom_call_target="tpu_custom_call" | custom-call | tf_op jit(solution)/shard_map/expert/pallas_call | solution.py:365
  215.0 16.7 %expert.5 = (bf16[1792,2048]{1,0:T(8,128)(2,1)}, bf16[1792,1024]{1,0:T(8,128)(2,1)}, bf16[1792,1024]{1,0:T(8,128)(2,1)}, bf16[1792,1024]{1,0:T(8,128)(2,1)}, bf1...) custom-call(bf16[192,2048]{1,0:T(8,128)(2,1)S(1)} %collective-permut, ...), custom_call_target="tpu_custom_call", output_to_operand_aliasing={{0}: (10, {}), {1}: (11, {}), {2}: (12, {}), {3}: (13, {})} | custom-call | tf_op jit(solution)/shard_map/expert/pallas_call | solution.py:365
  239.6 17.1 %expert.6 = (bf16[1792,2048]{1,0:T(8,128)(2,1)}, bf16[1792,1024]{1,0:T(8,128)(2,1)}, bf16[1792,1024]{1,0:T(8,128)(2,1)}, bf16[1792,1024]{1,0:T(8,128)(2,1)}, bf1...) custom-call(bf16[192,2048]{1,0:T(8,128)(2,1)S(1)} %collective-permut, ...), custom_call_target="tpu_custom_call", output_to_operand_aliasing={{0}: (10, {}), {1}: (11, {}), {2}: (12, {}), {3}: (13, {})} | custom-call | tf_op jit(solution)/shard_map/expert/pallas_call | solution.py:365
  259.3 16.7 %expert.7 = (bf16[1792,2048]{1,0:T(8,128)(2,1)}, bf16[1792,1024]{1,0:T(8,128)(2,1)}, bf16[1792,1024]{1,0:T(8,128)(2,1)}, bf16[1792,1024]{1,0:T(8,128)(2,1)}, bf1...) custom-call(bf16[192,2048]{1,0:T(8,128)(2,1)S(1)} %collective-permut, ...), custom_call_target="tpu_custom_call", output_to_operand_aliasing={{0}: (10, {}), {1}: (11, {}), {2}: (12, {}), {3}: (13, {})} | custom-call | tf_op jit(solution)/shard_map/expert/pallas_call | solution.py:365
  289.7 13.1 %row_grads.3 = (bf16[1,256,2048]{2,1,0:T(8,128)(2,1)}, bf16[1,256,2048]{2,1,0:T(8,128)(2,1)S(1)}, f32[512,2048]{1,0:T(8,128)}) custom-call(s32[1]{0:T(128)} %bitcast.44.me_ref, bf16[1792,1024]{1,0:T(8,128)(2,1)S(1)} %copy-done.2, bf16[1792,2048]{1,0:T(8,128)(2,1)} %get-tuple-element.374.right_ref), custom_call_target="tpu_custom_call" | custom-call | tf_op jit(solution)/shard_map/row_grads/pallas_call | solution.py:519
  316.8 13.1 %row_grads.4 = (bf16[1,128,2048]{2,1,0:T(8,128)(2,1)S(1)}, bf16[1,256,2048]{2,1,0:T(8,128)(2,1)}, bf16[1,128,2048]{2,1,0:T(8,128)(2,1)S(1)}, f32[512,2048]{1,0:T(8,128)}) custom-call(s32[1]{0:T(128)} %bitcast.44.me_ref, bf16[1792,1024]{1,0:T(8,128)(2,1)S(1)} %copy-done.3, bf16[1792,2048]{1,0:T(8,128)(2,1)} %get-tuple-element.374.right_ref), custom_call_target="tpu_custom_call" | custom-call | tf_op jit(solution)/shard_map/row_grads/pallas_call | solution.py:519
  340.0 22.2 %expert_out.1 = (bf16[4,2,192,2048]{3,2,1,0:T(8,128)(2,1)}, bf16[4,2,192,2048]{3,2,1,0:T(8,128)(2,1)}) custom-call(bf16[16,112,192]{2,1,0:T(8,128)(2,1)S(1)} %fusion.pick_ref.refs_4_, bf16[1792,1024]{1,0:T(8,128)(2,1)S(1)} %copy-done, bf16[1024,2048]{1,0:T(8,128)(2,1)} %bitcast.290), custom_call_target="tpu_custom_call" | custom-call | tf_op jit(solution)/shard_map/expert_out/pallas_call | solution.py:430
  362.2 7.1 %collective-permute-done.41 = bf16[128,2048]{1,0:T(8,128)(2,1)S(1)} collective-permute-done((bf16[128,2048]{1,0:T(8,128)(2,1)}, bf16[128,2048]{1,0:T(8,128)(2,1)S(1)}, u32[]{:S(2)}, u32[]{:S(2)}) %collective-permute-start.41) | collective-permute-done | bytes 524320 | tf_op jit(solution)/shard_map/ppermute | solution.py:716
  380.8 5.6 norm_back.1
  393.0 13.1 %row_grads.5 = (bf16[1,64,2048]{2,1,0:T(8,128)(2,1)S(1)}, bf16[1,256,2048]{2,1,0:T(8,128)(2,1)}, bf16[1,192,2048]{2,1,0:T(8,128)(2,1)S(1)}, f32[512,2048]{1,0:T(8,128)}) custom-call(s32[1]{0:T(128)} %bitcast.44.me_ref, bf16[1792,1024]{1,0:T(8,128)(2,1)S(1)} %copy-done.1, bf16[1792,2048]{1,0:T(8,128)(2,1)} %get-tuple-element.399.right_ref), custom_call_target="tpu_custom_call" | custom-call | tf_op jit(solution)/shard_map/row_grads/pallas_call | solution.py:519
  432.9 11.5 %attend_back.1 = (f32[192,2048]{1,0:T(8,128)}, f32[192,2048]{1,0:T(8,128)}, f32[192,2048]{1,0:T(8,128)}, bf16[128,2048]{1,0:T(8,128)(2,1)S(1)}, bf16[128,2048]{1,0:T(8,128)(2,1)S(1)}) custom-call(s32[2]{0:T(128)S(1)} %pad_add_fusion.1.meta_ref, bf16[192,2048]{1,0:T(8,128)(2,1)S(1)} %copy-done.10, bf16[256,2048]{1,0:T(8,128)(2,1)S(1)} %copy-done.6, ...), custom_call_target="tpu_custom_call" | custom-call | tf_op jit(solution)/shard_map/attend_back/pallas_call | solution.py:280
  453.9 4.8 fusion.8
  469.4 13.2 %collective-permute-done.54.refs_0_ = bf16[64,2048]{1,0:T(8,128)(2,1)S(1)} collective-permute-done((bf16[64,2048]{1,0:T(8,128)(2,1)S(1)}, bf16[64,2048]{1,0:T(8,128)(2,1)S(1)}, u32[]{:S(2)}, u32[]{:S(2)}) %collective-permute-start.54) | collective-permute-done | bytes 262176 | tf_op jit(solution)/shard_map/ppermute | solution.py:716
  509.5 4.9 collective-permute-done.59
  524.1 4.5 weight_grads.6
  528.7 6.0 weight_grads.5
  545.7 4.6 weight_grads.7
  571.9 8.4 %collective-permute-done.71 = bf16[64,2048]{1,0:T(8,128)(2,1)S(1)} collective-permute-done((bf16[64,2048]{1,0:T(8,128)(2,1)S(1)}, bf16[64,2048]{1,0:T(8,128)(2,1)S(1)}, u32[]{:S(2)}, u32[]{:S(2)}) %collective-permute-start.71) | collective-permute-done | bytes 262176 | tf_op jit(solution)/shard_map/ppermute | solution.py:716
  581.3 6.8 collective-permute-done.66
  610.7 4.6 collective-permute-done.73
  627.1 9.3 %collective-permute-done.77 = f32[4,256,20]{1,0,2:T(4,128)S(1)} collective-permute-done((f32[4,256,20]{1,0,2:T(4,128)S(1)}, f32[4,256,20]{1,0,2:T(4,128)S(1)}, u32[]{:S(2)}, u32[]{:S(2)}) %collective-permute-start.77) | collective-permute-done | bytes 81952 | tf_op jit(solution)/shard_map/ppermute | solution.py:716
  646.9 5.7 convert_add_fusion
  663.9 5.6 collective-permute-done.84
  (540 shorter events, 321.1 us)
Async XLA Ops:
  7.2 135.0 %all-gather.2.cloned.1.call-start = ((), (), s32[]{:S(2)}) async-start(), calls=%async_computation.2 | async-start | bytes 13369344 | tf_op jit(solution)/shard_map/all_gather | solution.py:768
  29.8 42.1 %collective-permute-start.2 = (bf16[192,2048]{1,0:T(8,128)(2,1)}, bf16[192,2048]{1,0:T(8,128)(2,1)S(1)}, u32[]{:S(2)}, u32[]{:S(2)}) collective-permute-start(bf16[192,2048]{1,0:T(8,128)(2,1)} %convolution_convert_fusion.3), channel_id=1, source_target_pairs={{0,4},{4,0},{1,5},{5,1},{2,6},{6,2},{3,7},{7,3},{8,12},{12,8},{9,1... | collective-permute-start | bytes 2359304 | tf_op jit(solution)/shard_map/ppermute | solution.py:716
  30.2 41.8 %collective-permute-start.3 = (bf16[192,2048]{1,0:T(8,128)(2,1)}, bf16[192,2048]{1,0:T(8,128)(2,1)}, u32[]{:S(2)}, u32[]{:S(2)}) collective-permute-start(bf16[192,2048]{1,0:T(8,128)(2,1)} %convolution_convert_fusion.2), channel_id=1, source_target_pairs={{0,4},{4,0},{1,5},{5,1},{2,6},{6,2},{3,7},{7,3},{8,12},{12,8},{9,1... | collective-permute-start | bytes 2359304 | tf_op jit(solution)/shard_map/ppermute | solution.py:716
  32.5 35.1 %all-to-all-start = ((f32[16,1,192]{2,1,0:T(1,128)}), f32[16,1,192]{2,1,0:T(1,128)S(1)}, u32[]{:S(2)}, u32[]{:S(2)}) async-start(f32[16,1,192]{2,1,0:T(1,128)} %all_to_all.16), calls=%async_computation | async-start | bytes 32768 | tf_op jit(solution)/shard_map/all_to_all | solution.py:800
  38.6 29.0 %collective-permute-start.4 = (bf16[4,1024]{1,0:T(4,128)(2,1)S(1)}, bf16[4,1024]{1,0:T(4,128)(2,1)S(1)}, u32[]{:S(2)}, u32[]{:S(2)}) collective-permute-start(bf16[4,1024]{1,0:T(4,128)(2,1)S(1)} %pad_maximum_fusion.9), channel_id=1, source_target_pairs={{0,4},{4,0},{1,5},{5,1},{2,6},{6,2},{3,7},{7,3},{8,12},{12,8},{9,1... | collective-permute-start | bytes 24584 | tf_op jit(solution)/shard_map/ppermute | solution.py:716
  40.0 31.0 %collective-permute-start.5 = (bf16[1024,16]{1,0:T(8,128)(2,1)}, bf16[1024,16]{1,0:T(8,128)(2,1)}, u32[]{:S(2)}, u32[]{:S(2)}) collective-permute-start(bf16[1024,16]{1,0:T(8,128)(2,1)} %copy.157), channel_id=1, source_target_pairs={{0,4},{4,0},{1,5},{5,1},{2,6},{6,2},{3,7},{7,3},{8,12},{12,8},{9,1... | collective-permute-start | bytes 98312 | tf_op jit(solution)/shard_map/ppermute | solution.py:716
  72.0 28.8 %collective-permute-start.6 = (bf16[192,2048]{1,0:T(8,128)(2,1)}, bf16[192,2048]{1,0:T(8,128)(2,1)S(1)}, u32[]{:S(2)}, u32[]{:S(2)}) collective-permute-start(bf16[192,2048]{1,0:T(8,128)(2,1)} %convolution_convert_fusion.1), channel_id=1, source_target_pairs={{0,4},{4,0},{1,5},{5,1},{2,6},{6,2},{3,7},{7,3},{8,12},{12,8},{9,1... | collective-permute-start | bytes 2359304 | tf_op jit(solution)/shard_map/ppermute | solution.py:716
  123.0 25.1 %collective-permute-start.16 = (bf16[192,1024]{1,0:T(8,128)(2,1)}, bf16[192,1024]{1,0:T(8,128)(2,1)}, u32[]{:S(2)}, u32[]{:S(2)}) collective-permute-start(bf16[192,1024]{1,0:T(8,128)(2,1)} %pad_maximum_fusion.5), channel_id=1, source_target_pairs={{0,4},{4,0},{1,5},{5,1},{2,6},{6,2},{3,7},{7,3},{8,12},{12,8},{9,1... | collective-permute-start | bytes 1179656 | tf_op jit(solution)/shard_map/ppermute | solution.py:716
  142.2 31.3 %collective-permute-start.11 = (bf16[192,2048]{1,0:T(8,128)(2,1)S(1)}, bf16[192,2048]{1,0:T(8,128)(2,1)S(1)}, u32[]{:S(2)}, u32[]{:S(2)}) collective-permute-start(bf16[192,2048]{1,0:T(8,128)(2,1)S(1)} %multiply_convert_fusion.refs_0_), channel_id=1, source_target_pairs={{0,8},{8,0},{16,24},{24,16},{1,9},{9,1},{17,25},{25,17},{2,10},{10... | collective-permute-start | bytes 2359304 | tf_op jit(solution)/shard_map/ppermute | solution.py:622
  143.3 30.1 %collective-permute-start.12 = (bf16[192,2048]{1,0:T(8,128)(2,1)S(1)}, bf16[192,2048]{1,0:T(8,128)(2,1)S(1)}, u32[]{:S(2)}, u32[]{:S(2)}) collective-permute-start(bf16[192,2048]{1,0:T(8,128)(2,1)S(1)} %multiply_convert_fusion.refs_0_), channel_id=1, source_target_pairs={{0,16},{8,24},{16,0},{24,8},{1,17},{9,25},{17,1},{25,9},{2,18},{10... | collective-permute-start | bytes 2359304 | tf_op jit(solution)/shard_map/ppermute | solution.py:622
  145.6 27.9 %collective-permute-start.13 = (bf16[192,2048]{1,0:T(8,128)(2,1)S(1)}, bf16[192,2048]{1,0:T(8,128)(2,1)S(1)}, u32[]{:S(2)}, u32[]{:S(2)}) collective-permute-start(bf16[192,2048]{1,0:T(8,128)(2,1)S(1)} %multiply_convert_fusion.refs_0_), channel_id=1, source_target_pairs={{0,2},{1,3},{2,0},{3,1},{4,6},{5,7},{6,4},{7,5},{8,10},{9,11},{10,... | collective-permute-start | bytes 2359304 | tf_op jit(solution)/shard_map/ppermute | solution.py:622
  147.1 26.4 %collective-permute-start.14 = (bf16[192,2048]{1,0:T(8,128)(2,1)S(1)}, bf16[192,2048]{1,0:T(8,128)(2,1)S(1)}, u32[]{:S(2)}, u32[]{:S(2)}) collective-permute-start(bf16[192,2048]{1,0:T(8,128)(2,1)S(1)} %multiply_convert_fusion.refs_0_), channel_id=1, source_target_pairs={{0,1},{1,0},{2,3},{3,2},{4,5},{5,4},{6,7},{7,6},{8,9},{9,8},{10,11... | collective-permute-start | bytes 2359304 | tf_op jit(solution)/shard_map/ppermute | solution.py:622
  148.1 25.3 %collective-permute-start.15 = (bf16[192,1024]{1,0:T(8,128)(2,1)S(1)}, bf16[192,1024]{1,0:T(8,128)(2,1)S(1)}, u32[]{:S(2)}, u32[]{:S(2)}) collective-permute-start(bf16[192,1024]{1,0:T(8,128)(2,1)S(1)} %pad_maximum_fusion.4), channel_id=1, source_target_pairs={{0,4},{4,0},{1,5},{5,1},{2,6},{6,2},{3,7},{7,3},{8,12},{12,8},{9,1... | collective-permute-start | bytes 1179656 | tf_op jit(solution)/shard_map/ppermute | solution.py:716
  175.1 37.3 %collective-permute-start.17 = (bf16[192,2048]{1,0:T(8,128)(2,1)S(1)}, bf16[192,2048]{1,0:T(8,128)(2,1)S(1)}, u32[]{:S(2)}, u32[]{:S(2)}) collective-permute-start(bf16[192,2048]{1,0:T(8,128)(2,1)S(1)} %collective-permute-done.12.refs_0_), channel_id=1, source_target_pairs={{0,2},{1,3},{2,0},{3,1},{4,6},{5,7},{6,4},{7,5},{8,10},{9,11},{10,... | collective-permute-start | bytes 2359304 | tf_op jit(solution)/shard_map/ppermute | solution.py:622
  195.0 36.8 %collective-permute-start.25 = (bf16[192,2048]{1,0:T(8,128)(2,1)S(1)}, bf16[192,2048]{1,0:T(8,128)(2,1)S(1)}, u32[]{:S(2)}, u32[]{:S(2)}) collective-permute-start(bf16[192,2048]{1,0:T(8,128)(2,1)S(1)} %collective-permute-done.19.refs_2_), channel_id=1, source_target_pairs={{0,2},{1,3},{2,0},{3,1},{4,6},{5,7},{6,4},{7,5},{8,10},{9,11},{10,... | collective-permute-start | bytes 2359304 | tf_op jit(solution)/shard_map/ppermute | solution.py:622
  277.8 27.4 %collective-permute-start.35 = (bf16[2,192,2048]{2,1,0:T(8,128)(2,1)}, bf16[2,192,2048]{2,1,0:T(8,128)(2,1)}, u32[]{:S(2)}, u32[]{:S(2)}) collective-permute-start(bf16[2,192,2048]{2,1,0:T(8,128)(2,1)} %get-tuple-element.357), channel_id=1, source_target_pairs={{0,1},{1,0},{2,3},{3,2},{4,5},{5,4},{6,7},{7,6},{8,9},{9,8},{10,11... | collective-permute-start | bytes 4718600 | tf_op jit(solution)/shard_map/ppermute | solution.py:622
  305.1 27.1 %collective-permute-start.38 = (bf16[256,2048]{1,0:T(8,128)(2,1)}, bf16[256,2048]{1,0:T(8,128)(2,1)}, u32[]{:S(2)}, u32[]{:S(2)}) collective-permute-start(bf16[256,2048]{1,0:T(8,128)(2,1)} %bitcast.51), channel_id=1, source_target_pairs={{0,4},{4,0},{1,5},{5,1},{2,6},{6,2},{3,7},{7,3},{8,12},{12,8},{9,1... | collective-permute-start | bytes 3145736 | tf_op jit(solution)/shard_map/ppermute | solution.py:716
  332.3 42.0 %collective-permute-start.40 = (bf16[256,2048]{1,0:T(8,128)(2,1)}, bf16[256,2048]{1,0:T(8,128)(2,1)S(1)}, u32[]{:S(2)}, u32[]{:S(2)}) collective-permute-start(bf16[256,2048]{1,0:T(8,128)(2,1)} %bitcast.297), channel_id=1, source_target_pairs={{0,4},{4,0},{1,5},{5,1},{2,6},{6,2},{3,7},{7,3},{8,12},{12,8},{9,1... | collective-permute-start | bytes 3145736 | tf_op jit(solution)/shard_map/ppermute | solution.py:716
  336.1 37.3 %collective-permute-start.39 = (bf16[192,2048]{1,0:T(8,128)(2,1)S(1)}, bf16[192,2048]{1,0:T(8,128)(2,1)S(1)}, u32[]{:S(2)}, u32[]{:S(2)}) collective-permute-start(bf16[192,2048]{1,0:T(8,128)(2,1)S(1)} %fusion.18), channel_id=1, source_target_pairs={{0,16},{8,24},{16,0},{24,8},{1,17},{9,25},{17,1},{25,9},{2,18},{10... | collective-permute-start | bytes 2359304 | tf_op jit(solution)/shard_map/ppermute | solution.py:622
  339.0 30.3 %collective-permute-start.41 = (bf16[128,2048]{1,0:T(8,128)(2,1)}, bf16[128,2048]{1,0:T(8,128)(2,1)S(1)}, u32[]{:S(2)}, u32[]{:S(2)}) collective-permute-start(bf16[128,2048]{1,0:T(8,128)(2,1)} %bitcast.300), channel_id=1, source_target_pairs={{0,4},{4,0},{1,5},{5,1},{2,6},{6,2},{3,7},{7,3},{8,12},{12,8},{9,1... | collective-permute-start | bytes 1572872 | tf_op jit(solution)/shard_map/ppermute | solution.py:716
  392.6 34.5 %collective-permute-start.45 = (bf16[192,2048]{1,0:T(8,128)(2,1)}, bf16[192,2048]{1,0:T(8,128)(2,1)}, u32[]{:S(2)}, u32[]{:S(2)}) collective-permute-start(bf16[192,2048]{1,0:T(8,128)(2,1)} %get-tuple-element.531), channel_id=1, source_target_pairs={{0,2},{1,3},{2,0},{3,1},{4,6},{5,7},{6,4},{7,5},{8,10},{9,11},{10,... | collective-permute-start | bytes 2359304 | tf_op jit(solution)/shard_map/ppermute | solution.py:622
  427.1 25.1 %collective-permute-start.49 = (bf16[256,2048]{1,0:T(8,128)(2,1)}, bf16[256,2048]{1,0:T(8,128)(2,1)}, u32[]{:S(2)}, u32[]{:S(2)}) collective-permute-start(bf16[256,2048]{1,0:T(8,128)(2,1)} %bitcast.61), channel_id=1, source_target_pairs={{0,4},{4,0},{1,5},{5,1},{2,6},{6,2},{3,7},{7,3},{8,12},{12,8},{9,1... | collective-permute-start | bytes 3145736 | tf_op jit(solution)/shard_map/ppermute | solution.py:716
  452.2 30.4 %collective-permute-start.51 = (bf16[4,2,64,2048]{3,2,1,0:T(8,128)(2,1)}, bf16[4,2,64,2048]{3,2,1,0:T(8,128)(2,1)}, u32[]{:S(2)}, u32[]{:S(2)}) collective-permute-start(bf16[4,2,64,2048]{3,2,1,0:T(8,128)(2,1)} %get-tuple-element.427), channel_id=1, source_target_pairs={{0,1},{1,0},{2,3},{3,2},{4,5},{5,4},{6,7},{7,6},{8,9},{9,8},{10,11... | collective-permute-start | bytes 6291464 | tf_op jit(solution)/shard_map/ppermute | solution.py:622
  452.2 30.4 %collective-permute-start.50 = (bf16[192,2048]{1,0:T(8,128)(2,1)}, bf16[192,2048]{1,0:T(8,128)(2,1)}, u32[]{:S(2)}, u32[]{:S(2)}) collective-permute-start(bf16[192,2048]{1,0:T(8,128)(2,1)} %get-tuple-element.426), channel_id=1, source_target_pairs={{0,2},{1,3},{2,0},{3,1},{4,6},{5,7},{6,4},{7,5},{8,10},{9,11},{10,... | collective-permute-start | bytes 2359304 | tf_op jit(solution)/shard_map/ppermute | solution.py:622
  458.7 23.9 %collective-permute-start.52 = (bf16[192,2048]{1,0:T(8,128)(2,1)}, bf16[192,2048]{1,0:T(8,128)(2,1)}, u32[]{:S(2)}, u32[]{:S(2)}) collective-permute-start(bf16[192,2048]{1,0:T(8,128)(2,1)} %get-tuple-element.527), channel_id=1, source_target_pairs={{0,8},{8,0},{16,24},{24,16},{1,9},{9,1},{17,25},{25,17},{2,10},{10... | collective-permute-start | bytes 2359304 | tf_op jit(solution)/shard_map/ppermute | solution.py:622
  487.2 27.3 %collective-permute-start.57 = (bf16[4,1,64,2048]{3,2,1,0:T(8,128)(2,1)}, bf16[4,1,64,2048]{3,2,1,0:T(8,128)(2,1)}, u32[]{:S(2)}, u32[]{:S(2)}) collective-permute-start(bf16[4,1,64,2048]{3,2,1,0:T(8,128)(2,1)} %get-tuple-element.540), channel_id=1, source_target_pairs={{0,2},{1,3},{2,0},{3,1},{4,6},{5,7},{6,4},{7,5},{8,10},{9,11},{10,... | collective-permute-start | bytes 3145736 | tf_op jit(solution)/shard_map/ppermute | solution.py:622
  487.9 26.5 %collective-permute-start.58 = (bf16[192,2048]{1,0:T(8,128)(2,1)S(1)}, bf16[192,2048]{1,0:T(8,128)(2,1)}, u32[]{:S(2)}, u32[]{:S(2)}) collective-permute-start(bf16[192,2048]{1,0:T(8,128)(2,1)S(1)} %value_rows.1.refs_0_), channel_id=1, source_target_pairs={{0,4},{4,0},{1,5},{5,1},{2,6},{6,2},{3,7},{7,3},{8,12},{12,8},{9,1... | collective-permute-start | bytes 2359304 | tf_op jit(solution)/shard_map/ppermute | solution.py:716
  552.0 29.4 %collective-permute-start.70 = (bf16[128,2048]{1,0:T(8,128)(2,1)S(1)}, bf16[128,2048]{1,0:T(8,128)(2,1)S(1)}, u32[]{:S(2)}, u32[]{:S(2)}) collective-permute-start(bf16[128,2048]{1,0:T(8,128)(2,1)S(1)} %bitcast.299), channel_id=1, source_target_pairs={{0,4},{4,0},{1,5},{5,1},{2,6},{6,2},{3,7},{7,3},{8,12},{12,8},{9,1... | collective-permute-start | bytes 1572872 | tf_op jit(solution)/shard_map/ppermute | solution.py:716
  554.8 33.4 %collective-permute-start.68 = (bf16[4,2,64,2048]{3,2,1,0:T(8,128)(2,1)S(1)}, bf16[4,2,64,2048]{3,2,1,0:T(8,128)(2,1)S(1)}, u32[]{:S(2)}, u32[]{:S(2)}) collective-permute-start(bf16[4,2,64,2048]{3,2,1,0:T(8,128)(2,1)S(1)} %copy-done.106), channel_id=1, source_target_pairs={{0,1},{1,0},{2,3},{3,2},{4,5},{5,4},{6,7},{7,6},{8,9},{9,8},{10,11... | collective-permute-start | bytes 6291464 | tf_op jit(solution)/shard_map/ppermute | solution.py:622
  562.0 26.2 %collective-permute-start.66 = (bf16[4,1,64,2048]{3,2,1,0:T(8,128)(2,1)S(1)}, bf16[4,1,64,2048]{3,2,1,0:T(8,128)(2,1)S(1)}, u32[]{:S(2)}, u32[]{:S(2)}) collective-permute-start(bf16[4,1,64,2048]{3,2,1,0:T(8,128)(2,1)S(1)} %get-tuple-element.538), channel_id=1, source_target_pairs={{0,2},{1,3},{2,0},{3,1},{4,6},{5,7},{6,4},{7,5},{8,10},{9,11},{10,... | collective-permute-start | bytes 3145736 | tf_op jit(solution)/shard_map/ppermute | solution.py:622
  580.3 30.4 %collective-permute-start.65 = (bf16[4,1,64,2048]{3,2,1,0:T(8,128)(2,1)}, bf16[4,1,64,2048]{3,2,1,0:T(8,128)(2,1)}, u32[]{:S(2)}, u32[]{:S(2)}) collective-permute-start(bf16[4,1,64,2048]{3,2,1,0:T(8,128)(2,1)} %get-tuple-element.536), channel_id=1, source_target_pairs={{0,2},{1,3},{2,0},{3,1},{4,6},{5,7},{6,4},{7,5},{8,10},{9,11},{10,... | collective-permute-start | bytes 3145736 | tf_op jit(solution)/shard_map/ppermute | solution.py:622
  596.3 40.2 %collective-permute-start.74 = (bf16[4,1,64,2048]{3,2,1,0:T(8,128)(2,1)}, bf16[4,1,64,2048]{3,2,1,0:T(8,128)(2,1)}, u32[]{:S(2)}, u32[]{:S(2)}) collective-permute-start(bf16[4,1,64,2048]{3,2,1,0:T(8,128)(2,1)} %get-tuple-element.534), channel_id=1, source_target_pairs={{0,2},{1,3},{2,0},{3,1},{4,6},{5,7},{6,4},{7,5},{8,10},{9,11},{10,... | collective-permute-start | bytes 3145736 | tf_op jit(solution)/shard_map/ppermute | solution.py:622
  (164 other events, 1693.1 us)
Sparse Core Ops, SparseCore 0:
  10.3 103.7 all-gather.1

commit v5 on v4

--- a/solution.py
+++ b/solution.py
@@ -876,7 +876,7 @@
     def across(v):
         return swap(v, "dp", 2)
 
-    b0, all_cot, normed_low = fence(normed2_low, all_cot, normed_low)
+    b0, all_cot, normed_low, router_probs = fence(normed2_low, all_cot, normed_low, router_probs)
     b1, b2, x0, c0 = z1(b0), z2(b0), across(b0), core(b0)
     normed_sent = [shift(out_part(normed_low, r), r) for r in others]
     attended_sent = [shift(out_part(attended, r), r) for r in others]
@@ -1024,7 +1024,7 @@
     half = tokens // 2
     query_got_a = [shift(d_query_low[:half], r) for r in others]
     out_far = add_blocks((out_keep, 1, 0), (out_near, 1, 0), out_got30, out_second)
-    out_first = z1(add_blocks((out_keep, 0, 1), (out_near, 0, 1), out_got21))
+    out_first = add_blocks((out_keep, 0, 1), (out_near, 0, 1), out_got21)
     out_got20, output_got, out_far, out_first, d_query_low, gate_own, *rest = fence(
         out_got20, output_got, out_far, out_first, d_query_low, gate_own,
         *value_prompt, *key_prompt, *query_got_a,
@@ -1043,15 +1043,18 @@
             own = add_rows(own, [p[k] for p in parts])
         return own
 
-    d_value_low, *key_prompt = fence(d_value_low, *key_prompt)
+    d_value_low, output_rows.parts, *key_prompt = fence(
+        d_value_low, output_rows.parts, *key_prompt
+    )
     got = spread(d_value_low) + [shift(d_query_low[half:], r) for r in others]
-    out_far_a, output_got = z2(out_far[:half]), output_rows.start()
+    out_far_a, out_first, output_got = z2(out_far[:half]), z1(out_first), output_rows.start()
+    d_normed_own = dot(d_value_low, w_value, NT) + dot(d_query_low, w_query, NT)
     d_key_low, key_gain_grad = qk_post_back(
         d_keys, key_raw, gain_key, cosine, sine, key_prompt
     )
     gate_grad = total(gate_own, gate_a, gate_b)
-    out_far_a, out_far_b, output_got, d_key_low, gate_grad, *rest = fence(
-        out_far_a, out_far[half:], output_got, d_key_low, gate_grad, *got
+    out_far_a, out_far_b, out_first, output_got, d_key_low, gate_grad, d_normed_own, *rest = fence(
+        out_far_a, out_far[half:], out_first, output_got, d_key_low, gate_grad, d_normed_own, *got
     )
     d_values = rest[: planes - 1]
     d_query_got = [
@@ -1072,14 +1075,6 @@
     d_key_got, partial = rest[: planes - 1], rest[planes - 1 :]
     output_rows.finish(output_got)
     value_rows, query_rows = RowScatter(*value_pair), RowScatter(*query_pair)
-    out_rows = (
-        mixed_rows
-        + plus(out_keep[0, 0].astype(F32), out_near[0, 0])
-        + out_got20.astype(F32)
-        + out_first.astype(F32)
-        + jnp.concatenate([out_far_a, out_far_b], axis=0).astype(F32)
-    )
-
     value_got, query_got = value_rows.start(), query_rows.start()
     key_pair = weight_grads(normed_out, [d_key_low, *d_key_got])
     blocks_low = [
@@ -1095,9 +1090,7 @@
     d_normed_got = [shift(v, planes - r) for r, v in zip(others, blocks_low)]
     value_got, output_got, key_got = value_rows.start(), output_rows.start(), key_rows.start()
     up_c, down_a = send_rows(up_2), send_rows(down_0)
-    d_normed_own = (
-        dot(d_value_low, w_value, NT) + dot(d_query_low, w_query, NT) + dot(d_key_low, w_key, NT)
-    )
+    d_normed_own = d_normed_own + dot(d_key_low, w_key, NT)
     value_got, output_got, key_got, d_normed_own, down_1, *rest = fence(
         value_got, output_got, key_got, d_normed_own, down_1, *d_normed_got, *up_c, *down_a
     )
@@ -1123,11 +1116,19 @@
         ],
         axis=1,
     )
-    query_got, value_got, d_x, small_grads, down_2, *down_b = fence(
-        query_got, value_got, d_x, small_grads, down_2, *down_b
+    query_got, value_got, d_x, small_grads, down_2, out_first, *down_b = fence(
+        query_got, value_got, d_x, small_grads, down_2, out_first, *down_b
     )
     query_rows.finish(query_got)
     value_rows.finish(value_got)
+    out_rows = (
+        mixed_rows
+        + plus(out_keep[0, 0].astype(F32), out_near[0, 0])
+        + out_got20.astype(F32)
+        + out_first.astype(F32)
+        + jnp.concatenate([out_far_a, out_far_b], axis=0).astype(F32)
+    )
+
 
     def laid(own, *parts):
         for k in range(planes - 1):

time: 688 us -> 687 us (level)
  waiting for transfers between devices: 189 us -> 205 us
    ppermute x55, waiting for transfers between devices: 66.2 us -> 80.7 us  [swap(): lax.ppermute(value, axis, [(i, i ^ bit) for i in range(lax.axis_size(axis...]
    unnamed x218 -> x236, local copies, waits for them, and re-layouts: 26.7 us -> 22.2 us
  transfers between devices with their start and end apart: 89 -> 89, of which waited for: 33 -> 37; matrix products, arithmetic and copies ran while one was open for 20% -> 19% of each run, Pallas kernels for 29% -> 29%
where the time goes in v5:
time: 687 us; the launch traced here: 683 us
  waiting for transfers between devices  205 us (30%)
  Pallas kernels  200 us (29%)
  starting transfers between devices  92.5 us (13%)
  other arithmetic  89.9 us (13%)
  local copies, waits for them, and re-layouts  41.5 us (6%)
  matrix products  37.7 us (5%)
  between operations  16.7 us (2%)
    ppermute x31, waiting for transfers between devices, shift(): lax.ppermute(value, 'context', [(i, (i + r) % planes) for i in range(plan...  124 us
    ppermute x55, waiting for transfers between devices, swap(): lax.ppermute(value, axis, [(i, i ^ bit) for i in range(lax.axis_size(axis...  80.7 us
    pallas_call x4, Pallas kernels, expert_quarter(): pl.pallas_call(expert_kernel, grid=(hidden // tile,), in_specs=[whole(tok...  67.1 us
    convert_element_type x25, other arithmetic, plus(): return sum((v.astype(F32) for v in values)).astype(values[0].dtype)  56.6 us
    ppermute x55, starting transfers between devices, swap(): lax.ppermute(value, axis, [(i, i ^ bit) for i in range(lax.axis_size(axis...  49.4 us
    pallas_call x3, Pallas kernels, row_grads(): pl.pallas_call(functools.partial(row_grads_kernel, cuts), grid_spec=pltpu...  39.4 us
    dot_general x20, matrix products, dot(): lax.dot_general(left, right, (dims, ((), ())), preferred_element_type=out)  37.7 us
    ppermute x31, starting transfers between devices, shift(): lax.ppermute(value, 'context', [(i, (i + r) % planes) for i in range(plan...  33 us
  transfers between devices with their start and end apart: 89, of which 37 were waited for; matrix products, arithmetic and copies ran while one was open for 19% of the time, Pallas kernels for 29%

profile of v5, /device:TPU:0, one launch (start us, length us, event | category | flops | bytes accessed | tf_op | source)
XLA Modules:
  0.0 682.7 jit_solution(7984591854348226148)
XLA Ops:
  14.8 8.6 %collective-permute-done = bf16[192,1024]{1,0:T(8,128)(2,1)S(1)} collective-permute-done((bf16[192,1024]{1,0:T(8,128)(2,1)S(1)}, bf16[192,1024]{1,0:T(8,128)(2,1)S(1)}, u32[]{:S(2)}, u32[]{:S(2)}) %collective-permute-start) | collective-permute-done | bytes 393248 | tf_op jit(solution)/shard_map/ppermute | solution.py:716
  32.5 6.2 all-to-all-start
  51.2 16.4 %collective-permute-done.4 = bf16[4,1024]{1,0:T(4,128)(2,1)S(1)} collective-permute-done((bf16[4,1024]{1,0:T(4,128)(2,1)S(1)}, bf16[4,1024]{1,0:T(4,128)(2,1)S(1)}, u32[]{:S(2)}, u32[]{:S(2)}) %collective-permute-start.4) | collective-permute-done | bytes 8224 | tf_op jit(solution)/shard_map/ppermute | solution.py:716
  80.1 17.8 %collective-permute-done.7 = bf16[64,2048]{1,0:T(8,128)(2,1)S(1)} collective-permute-done((bf16[64,2048]{1,0:T(8,128)(2,1)S(1)}, bf16[64,2048]{1,0:T(8,128)(2,1)S(1)}, u32[]{:S(2)}, u32[]{:S(2)}) %collective-permute-start.7) | collective-permute-done | bytes 262176 | tf_op jit(solution)/shard_map/ppermute | solution.py:716
  101.9 4.8 attend.1
  109.7 6.1 collective-permute-done.9
  123.4 16.1 %collective-permute-done.10 = bf16[192,2048]{1,0:T(8,128)(2,1)S(1)} collective-permute-done((bf16[192,2048]{1,0:T(8,128)(2,1)S(1)}, bf16[192,2048]{1,0:T(8,128)(2,1)S(1)}, u32[]{:S(2)}, u32[]{:S(2)}) %collective-permute-start.10) | collective-permute-done | bytes 786464 | tf_op jit(solution)/shard_map/ppermute | solution.py:716
  152.8 22.0 %gather_cot.1 = (bf16[1792,2048]{1,0:T(8,128)(2,1)}, f32[1792,1024]{1,0:T(8,128)}) custom-call(s32[16]{0:T(128)S(1)} %stack.98.source_ref, bf16[16,192,2048]{2,1,0:T(8,128)(2,1)} %bitcast.302, bf16[16,192,2048]{2,1,0:T(8,128)(2,1)} %bitcast.303, bf16[16,192,2048]{2,1,0:T(8,128)(2,1)} %bitcast.304, bf16[16,192,2048]{2,1,0:T(8,128)(2,1)} %bitcast.305, ...), custom_call_target="tpu_custom_call" | custom-call | tf_op jit(solution)/shard_map/gather_cot/pallas_call | solution.py:466
  178.0 16.6 %collective-permute-done.19.refs_2_ = bf16[192,2048]{1,0:T(8,128)(2,1)S(1)} collective-permute-done((bf16[192,2048]{1,0:T(8,128)(2,1)S(1)}, bf16[192,2048]{1,0:T(8,128)(2,1)S(1)}, u32[]{:S(2)}, u32[]{:S(2)}) %collective-permute-start.19) | collective-permute-done | bytes 786464 | tf_op jit(solution)/shard_map/ppermute | solution.py:622
  196.9 16.7 %expert.4 = (bf16[1792,2048]{1,0:T(8,128)(2,1)}, bf16[1792,1024]{1,0:T(8,128)(2,1)}, bf16[1792,1024]{1,0:T(8,128)(2,1)}, bf16[1792,1024]{1,0:T(8,128)(2,1)}, bf1...) custom-call(bf16[192,2048]{1,0:T(8,128)(2,1)S(1)} %multiply_convert_fusion.refs_0_, ...), custom_call_target="tpu_custom_call" | custom-call | tf_op jit(solution)/shard_map/expert/pallas_call | solution.py:365
  216.3 16.7 %expert.5 = (bf16[1792,2048]{1,0:T(8,128)(2,1)}, bf16[1792,1024]{1,0:T(8,128)(2,1)}, bf16[1792,1024]{1,0:T(8,128)(2,1)}, bf16[1792,1024]{1,0:T(8,128)(2,1)}, bf1...) custom-call(bf16[192,2048]{1,0:T(8,128)(2,1)S(1)} %collective-permut, ...), custom_call_target="tpu_custom_call", output_to_operand_aliasing={{0}: (10, {}), {1}: (11, {}), {2}: (12, {}), {3}: (13, {})} | custom-call | tf_op jit(solution)/shard_map/expert/pallas_call | solution.py:365
  240.8 16.9 %expert.6 = (bf16[1792,2048]{1,0:T(8,128)(2,1)}, bf16[1792,1024]{1,0:T(8,128)(2,1)}, bf16[1792,1024]{1,0:T(8,128)(2,1)}, bf16[1792,1024]{1,0:T(8,128)(2,1)}, bf1...) custom-call(bf16[192,2048]{1,0:T(8,128)(2,1)S(1)} %collective-permut, ...), custom_call_target="tpu_custom_call", output_to_operand_aliasing={{0}: (10, {}), {1}: (11, {}), {2}: (12, {}), {3}: (13, {})} | custom-call | tf_op jit(solution)/shard_map/expert/pallas_call | solution.py:365
  260.5 16.7 %expert.7 = (bf16[1792,2048]{1,0:T(8,128)(2,1)}, bf16[1792,1024]{1,0:T(8,128)(2,1)}, bf16[1792,1024]{1,0:T(8,128)(2,1)}, bf16[1792,1024]{1,0:T(8,128)(2,1)}, bf1...) custom-call(bf16[192,2048]{1,0:T(8,128)(2,1)S(1)} %collective-permut, ...), custom_call_target="tpu_custom_call", output_to_operand_aliasing={{0}: (10, {}), {1}: (11, {}), {2}: (12, {}), {3}: (13, {})} | custom-call | tf_op jit(solution)/shard_map/expert/pallas_call | solution.py:365
  290.9 13.1 %row_grads.3 = (bf16[1,256,2048]{2,1,0:T(8,128)(2,1)}, bf16[1,256,2048]{2,1,0:T(8,128)(2,1)S(1)}, f32[512,2048]{1,0:T(8,128)}) custom-call(s32[1]{0:T(128)} %bitcast.44.me_ref, bf16[1792,1024]{1,0:T(8,128)(2,1)S(1)} %copy-done.1, bf16[1792,2048]{1,0:T(8,128)(2,1)} %get-tuple-element.380.right_ref), custom_call_target="tpu_custom_call" | custom-call | tf_op jit(solution)/shard_map/row_grads/pallas_call | solution.py:519
  318.3 13.1 %row_grads.4 = (bf16[1,128,2048]{2,1,0:T(8,128)(2,1)S(1)}, bf16[1,256,2048]{2,1,0:T(8,128)(2,1)}, bf16[1,128,2048]{2,1,0:T(8,128)(2,1)S(1)}, f32[512,2048]{1,0:T(8,128)}) custom-call(s32[1]{0:T(128)} %bitcast.44.me_ref, bf16[1792,1024]{1,0:T(8,128)(2,1)S(1)} %copy-done.2, bf16[1792,2048]{1,0:T(8,128)(2,1)} %get-tuple-element.380.right_ref), custom_call_target="tpu_custom_call" | custom-call | tf_op jit(solution)/shard_map/row_grads/pallas_call | solution.py:519
  341.6 22.2 %expert_out.1 = (bf16[4,2,192,2048]{3,2,1,0:T(8,128)(2,1)}, bf16[4,2,192,2048]{3,2,1,0:T(8,128)(2,1)}) custom-call(bf16[16,112,192]{2,1,0:T(8,128)(2,1)S(1)} %fusion.pick_ref.refs_4_, bf16[1792,1024]{1,0:T(8,128)(2,1)S(1)} %copy-done, bf16[1024,2048]{1,0:T(8,128)(2,1)} %bitcast.290), custom_call_target="tpu_custom_call" | custom-call | tf_op jit(solution)/shard_map/expert_out/pallas_call | solution.py:430
  363.7 7.0 %collective-permute-done.41 = bf16[128,2048]{1,0:T(8,128)(2,1)S(1)} collective-permute-done((bf16[128,2048]{1,0:T(8,128)(2,1)}, bf16[128,2048]{1,0:T(8,128)(2,1)S(1)}, u32[]{:S(2)}, u32[]{:S(2)}) %collective-permute-start.41) | collective-permute-done | bytes 524320 | tf_op jit(solution)/shard_map/ppermute | solution.py:716
  375.9 4.9 norm_back.1
  380.9 5.5 collective-permute-done.42
  391.9 13.3 %row_grads.5 = (bf16[1,64,2048]{2,1,0:T(8,128)(2,1)S(1)}, bf16[1,256,2048]{2,1,0:T(8,128)(2,1)}, bf16[1,192,2048]{2,1,0:T(8,128)(2,1)S(1)}, f32[512,2048]{1,0:T(8,128)}) custom-call(s32[1]{0:T(128)} %bitcast.44.me_ref, bf16[1792,1024]{1,0:T(8,128)(2,1)S(1)} %copy-done, bf16[1792,2048]{1,0:T(8,128)(2,1)} %get-tuple-element.406.right_ref), custom_call_target="tpu_custom_call" | custom-call | tf_op jit(solution)/shard_map/row_grads/pallas_call | solution.py:519
  431.3 11.4 %attend_back.1 = (f32[192,2048]{1,0:T(8,128)}, f32[192,2048]{1,0:T(8,128)}, f32[192,2048]{1,0:T(8,128)}, bf16[128,2048]{1,0:T(8,128)(2,1)S(1)}, bf16[128,2048]{1,0:T(8,128)(2,1)S(1)}) custom-call(s32[2]{0:T(128)S(1)} %pad_add_fusion.1.meta_ref, bf16[192,2048]{1,0:T(8,128)(2,1)S(1)} %copy-done.9, bf16[256,2048]{1,0:T(8,128)(2,1)S(1)} %copy-done.5, ...), custom_call_target="tpu_custom_call" | custom-call | tf_op jit(solution)/shard_map/attend_back/pallas_call | solution.py:280
  460.5 4.6 fusion.8
  468.0 7.7 %collective-permute-done.54 = bf16[96,2048]{1,0:T(8,128)(2,1)S(1)} collective-permute-done((bf16[96,2048]{1,0:T(8,128)(2,1)S(1)}, bf16[96,2048]{1,0:T(8,128)(2,1)S(1)}, u32[]{:S(2)}, u32[]{:S(2)}) %collective-permute-start.54) | collective-permute-done | bytes 393248 | tf_op jit(solution)/shard_map/ppermute | solution.py:716
  501.4 10.8 %collective-permute-done.59 = bf16[96,2048]{1,0:T(8,128)(2,1)} collective-permute-done((bf16[96,2048]{1,0:T(8,128)(2,1)}, bf16[96,2048]{1,0:T(8,128)(2,1)}, u32[]{:S(2)}, u32[]{:S(2)}) %collective-permute-start.59) | collective-permute-done | bytes 393248 | tf_op jit(solution)/shard_map/ppermute | solution.py:716
  518.5 4.6 weight_grads.6
  524.4 4.8 weight_grads.5
  556.6 9.5 %collective-permute-done.67 = bf16[1,1,64,2048]{3,2,1,0:T(8,128)(2,1)S(1)} collective-permute-done((bf16[1,1,64,2048]{3,2,1,0:T(8,128)(2,1)S(1)}, bf16[1,1,64,2048]{3,2,1,0:T(8,128)(2,1)S(1)}, u32[]{:S(2)}, u32[]{:S(2)}) %collective-permute-start.67) | collective-permute-done | bytes 262176 | tf_op jit(solution)/shard_map/ppermute | solution.py:622
  570.8 9.9 %collective-permute-done.71 = bf16[64,2048]{1,0:T(8,128)(2,1)S(1)} collective-permute-done((bf16[64,2048]{1,0:T(8,128)(2,1)S(1)}, bf16[64,2048]{1,0:T(8,128)(2,1)S(1)}, u32[]{:S(2)}, u32[]{:S(2)}) %collective-permute-start.71) | collective-permute-done | bytes 262176 | tf_op jit(solution)/shard_map/ppermute | solution.py:716
  599.7 7.3 %collective-permute-done.65 = bf16[4,1,64,2048]{3,2,1,0:T(8,128)(2,1)} collective-permute-done((bf16[4,1,64,2048]{3,2,1,0:T(8,128)(2,1)}, bf16[4,1,64,2048]{3,2,1,0:T(8,128)(2,1)}, u32[]{:S(2)}, u32[]{:S(2)}) %collective-permute-start.65) | collective-permute-done | bytes 1048608 | tf_op jit(solution)/shard_map/ppermute | solution.py:622
  625.0 10.8 %collective-permute-done.77 = f32[4,256,20]{1,0,2:T(4,128)S(1)} collective-permute-done((f32[4,256,20]{1,0,2:T(4,128)S(1)}, f32[4,256,20]{1,0,2:T(4,128)S(1)}, u32[]{:S(2)}, u32[]{:S(2)}) %collective-permute-start.77) | collective-permute-done | bytes 81952 | tf_op jit(solution)/shard_map/ppermute | solution.py:716
  643.8 5.7 convert_add_fusion
  663.9 9.9 %collective-permute-done.85 = bf16[1,1,64,2048]{3,2,1,0:T(8,128)(2,1)S(1)} collective-permute-done((bf16[1,1,64,2048]{3,2,1,0:T(8,128)(2,1)S(1)}, bf16[1,1,64,2048]{3,2,1,0:T(8,128)(2,1)S(1)}, u32[]{:S(2)}, u32[]{:S(2)}) %collective-permute-start.85) | collective-permute-done | bytes 262176 | tf_op jit(solution)/shard_map/ppermute | solution.py:622
  (559 shorter events, 308.1 us)
Async XLA Ops:
  7.2 135.8 %all-gather.2.cloned.1.call-start = ((), (), s32[]{:S(2)}) async-start(), calls=%async_computation.2 | async-start | bytes 13369344 | tf_op jit(solution)/shard_map/all_gather | solution.py:768
  29.9 42.1 %collective-permute-start.2 = (bf16[192,2048]{1,0:T(8,128)(2,1)}, bf16[192,2048]{1,0:T(8,128)(2,1)S(1)}, u32[]{:S(2)}, u32[]{:S(2)}) collective-permute-start(bf16[192,2048]{1,0:T(8,128)(2,1)} %convolution_convert_fusion.3), channel_id=1, source_target_pairs={{0,4},{4,0},{1,5},{5,1},{2,6},{6,2},{3,7},{7,3},{8,12},{12,8},{9,1... | collective-permute-start | bytes 2359304 | tf_op jit(solution)/shard_map/ppermute | solution.py:716
  30.2 41.8 %collective-permute-start.3 = (bf16[192,2048]{1,0:T(8,128)(2,1)}, bf16[192,2048]{1,0:T(8,128)(2,1)}, u32[]{:S(2)}, u32[]{:S(2)}) collective-permute-start(bf16[192,2048]{1,0:T(8,128)(2,1)} %convolution_convert_fusion.2), channel_id=1, source_target_pairs={{0,4},{4,0},{1,5},{5,1},{2,6},{6,2},{3,7},{7,3},{8,12},{12,8},{9,1... | collective-permute-start | bytes 2359304 | tf_op jit(solution)/shard_map/ppermute | solution.py:716
  32.5 35.1 %all-to-all-start = ((f32[16,1,192]{2,1,0:T(1,128)}), f32[16,1,192]{2,1,0:T(1,128)S(1)}, u32[]{:S(2)}, u32[]{:S(2)}) async-start(f32[16,1,192]{2,1,0:T(1,128)} %all_to_all.16), calls=%async_computation | async-start | bytes 32768 | tf_op jit(solution)/shard_map/all_to_all | solution.py:800
  38.7 28.9 %collective-permute-start.4 = (bf16[4,1024]{1,0:T(4,128)(2,1)S(1)}, bf16[4,1024]{1,0:T(4,128)(2,1)S(1)}, u32[]{:S(2)}, u32[]{:S(2)}) collective-permute-start(bf16[4,1024]{1,0:T(4,128)(2,1)S(1)} %pad_maximum_fusion.9), channel_id=1, source_target_pairs={{0,4},{4,0},{1,5},{5,1},{2,6},{6,2},{3,7},{7,3},{8,12},{12,8},{9,1... | collective-permute-start | bytes 24584 | tf_op jit(solution)/shard_map/ppermute | solution.py:716
  40.2 30.8 %collective-permute-start.5 = (bf16[1024,16]{1,0:T(8,128)(2,1)}, bf16[1024,16]{1,0:T(8,128)(2,1)}, u32[]{:S(2)}, u32[]{:S(2)}) collective-permute-start(bf16[1024,16]{1,0:T(8,128)(2,1)} %copy.134), channel_id=1, source_target_pairs={{0,4},{4,0},{1,5},{5,1},{2,6},{6,2},{3,7},{7,3},{8,12},{12,8},{9,1... | collective-permute-start | bytes 98312 | tf_op jit(solution)/shard_map/ppermute | solution.py:716
  72.0 28.8 %collective-permute-start.6 = (bf16[192,2048]{1,0:T(8,128)(2,1)}, bf16[192,2048]{1,0:T(8,128)(2,1)S(1)}, u32[]{:S(2)}, u32[]{:S(2)}) collective-permute-start(bf16[192,2048]{1,0:T(8,128)(2,1)} %convolution_convert_fusion.1), channel_id=1, source_target_pairs={{0,4},{4,0},{1,5},{5,1},{2,6},{6,2},{3,7},{7,3},{8,12},{12,8},{9,1... | collective-permute-start | bytes 2359304 | tf_op jit(solution)/shard_map/ppermute | solution.py:716
  123.1 25.7 %collective-permute-start.16 = (bf16[192,1024]{1,0:T(8,128)(2,1)}, bf16[192,1024]{1,0:T(8,128)(2,1)}, u32[]{:S(2)}, u32[]{:S(2)}) collective-permute-start(bf16[192,1024]{1,0:T(8,128)(2,1)} %pad_maximum_fusion.5), channel_id=1, source_target_pairs={{0,4},{4,0},{1,5},{5,1},{2,6},{6,2},{3,7},{7,3},{8,12},{12,8},{9,1... | collective-permute-start | bytes 1179656 | tf_op jit(solution)/shard_map/ppermute | solution.py:716
  143.0 31.8 %collective-permute-start.11 = (bf16[192,2048]{1,0:T(8,128)(2,1)S(1)}, bf16[192,2048]{1,0:T(8,128)(2,1)S(1)}, u32[]{:S(2)}, u32[]{:S(2)}) collective-permute-start(bf16[192,2048]{1,0:T(8,128)(2,1)S(1)} %multiply_convert_fusion.refs_0_), channel_id=1, source_target_pairs={{0,8},{8,0},{16,24},{24,16},{1,9},{9,1},{17,25},{25,17},{2,10},{10... | collective-permute-start | bytes 2359304 | tf_op jit(solution)/shard_map/ppermute | solution.py:622
  144.1 30.8 %collective-permute-start.12 = (bf16[192,2048]{1,0:T(8,128)(2,1)S(1)}, bf16[192,2048]{1,0:T(8,128)(2,1)S(1)}, u32[]{:S(2)}, u32[]{:S(2)}) collective-permute-start(bf16[192,2048]{1,0:T(8,128)(2,1)S(1)} %multiply_convert_fusion.refs_0_), channel_id=1, source_target_pairs={{0,16},{8,24},{16,0},{24,8},{1,17},{9,25},{17,1},{25,9},{2,18},{10... | collective-permute-start | bytes 2359304 | tf_op jit(solution)/shard_map/ppermute | solution.py:622
  146.4 28.5 %collective-permute-start.13 = (bf16[192,2048]{1,0:T(8,128)(2,1)S(1)}, bf16[192,2048]{1,0:T(8,128)(2,1)S(1)}, u32[]{:S(2)}, u32[]{:S(2)}) collective-permute-start(bf16[192,2048]{1,0:T(8,128)(2,1)S(1)} %multiply_convert_fusion.refs_0_), channel_id=1, source_target_pairs={{0,2},{1,3},{2,0},{3,1},{4,6},{5,7},{6,4},{7,5},{8,10},{9,11},{10,... | collective-permute-start | bytes 2359304 | tf_op jit(solution)/shard_map/ppermute | solution.py:622
  147.8 27.0 %collective-permute-start.14 = (bf16[192,2048]{1,0:T(8,128)(2,1)S(1)}, bf16[192,2048]{1,0:T(8,128)(2,1)S(1)}, u32[]{:S(2)}, u32[]{:S(2)}) collective-permute-start(bf16[192,2048]{1,0:T(8,128)(2,1)S(1)} %multiply_convert_fusion.refs_0_), channel_id=1, source_target_pairs={{0,1},{1,0},{2,3},{3,2},{4,5},{5,4},{6,7},{7,6},{8,9},{9,8},{10,11... | collective-permute-start | bytes 2359304 | tf_op jit(solution)/shard_map/ppermute | solution.py:622
  148.8 26.0 %collective-permute-start.15 = (bf16[192,1024]{1,0:T(8,128)(2,1)S(1)}, bf16[192,1024]{1,0:T(8,128)(2,1)S(1)}, u32[]{:S(2)}, u32[]{:S(2)}) collective-permute-start(bf16[192,1024]{1,0:T(8,128)(2,1)S(1)} %pad_maximum_fusion.4), channel_id=1, source_target_pairs={{0,4},{4,0},{1,5},{5,1},{2,6},{6,2},{3,7},{7,3},{8,12},{12,8},{9,1... | collective-permute-start | bytes 1179656 | tf_op jit(solution)/shard_map/ppermute | solution.py:716
  176.5 37.2 %collective-permute-start.17 = (bf16[192,2048]{1,0:T(8,128)(2,1)S(1)}, bf16[192,2048]{1,0:T(8,128)(2,1)S(1)}, u32[]{:S(2)}, u32[]{:S(2)}) collective-permute-start(bf16[192,2048]{1,0:T(8,128)(2,1)S(1)} %collective-permute-done.12.refs_0_), channel_id=1, source_target_pairs={{0,2},{1,3},{2,0},{3,1},{4,6},{5,7},{6,4},{7,5},{8,10},{9,11},{10,... | collective-permute-start | bytes 2359304 | tf_op jit(solution)/shard_map/ppermute | solution.py:622
  196.4 36.7 %collective-permute-start.25 = (bf16[192,2048]{1,0:T(8,128)(2,1)S(1)}, bf16[192,2048]{1,0:T(8,128)(2,1)S(1)}, u32[]{:S(2)}, u32[]{:S(2)}) collective-permute-start(bf16[192,2048]{1,0:T(8,128)(2,1)S(1)} %collective-permute-done.19.refs_2_), channel_id=1, source_target_pairs={{0,2},{1,3},{2,0},{3,1},{4,6},{5,7},{6,4},{7,5},{8,10},{9,11},{10,... | collective-permute-start | bytes 2359304 | tf_op jit(solution)/shard_map/ppermute | solution.py:622
  279.0 27.4 %collective-permute-start.35 = (bf16[2,192,2048]{2,1,0:T(8,128)(2,1)}, bf16[2,192,2048]{2,1,0:T(8,128)(2,1)}, u32[]{:S(2)}, u32[]{:S(2)}) collective-permute-start(bf16[2,192,2048]{2,1,0:T(8,128)(2,1)} %get-tuple-element.363), channel_id=1, source_target_pairs={{0,1},{1,0},{2,3},{3,2},{4,5},{5,4},{6,7},{7,6},{8,9},{9,8},{10,11... | collective-permute-start | bytes 4718600 | tf_op jit(solution)/shard_map/ppermute | solution.py:622
  306.4 27.3 %collective-permute-start.38 = (bf16[256,2048]{1,0:T(8,128)(2,1)}, bf16[256,2048]{1,0:T(8,128)(2,1)}, u32[]{:S(2)}, u32[]{:S(2)}) collective-permute-start(bf16[256,2048]{1,0:T(8,128)(2,1)} %bitcast.51), channel_id=1, source_target_pairs={{0,4},{4,0},{1,5},{5,1},{2,6},{6,2},{3,7},{7,3},{8,12},{12,8},{9,1... | collective-permute-start | bytes 3145736 | tf_op jit(solution)/shard_map/ppermute | solution.py:716
  333.7 41.2 %collective-permute-start.40 = (bf16[256,2048]{1,0:T(8,128)(2,1)}, bf16[256,2048]{1,0:T(8,128)(2,1)S(1)}, u32[]{:S(2)}, u32[]{:S(2)}) collective-permute-start(bf16[256,2048]{1,0:T(8,128)(2,1)} %bitcast.297), channel_id=1, source_target_pairs={{0,4},{4,0},{1,5},{5,1},{2,6},{6,2},{3,7},{7,3},{8,12},{12,8},{9,1... | collective-permute-start | bytes 3145736 | tf_op jit(solution)/shard_map/ppermute | solution.py:716
  337.6 37.3 %collective-permute-start.39 = (bf16[192,2048]{1,0:T(8,128)(2,1)S(1)}, bf16[192,2048]{1,0:T(8,128)(2,1)S(1)}, u32[]{:S(2)}, u32[]{:S(2)}) collective-permute-start(bf16[192,2048]{1,0:T(8,128)(2,1)S(1)} %fusion.18), channel_id=1, source_target_pairs={{0,16},{8,24},{16,0},{24,8},{1,17},{9,25},{17,1},{25,9},{2,18},{10... | collective-permute-start | bytes 2359304 | tf_op jit(solution)/shard_map/ppermute | solution.py:622
  340.5 30.2 %collective-permute-start.41 = (bf16[128,2048]{1,0:T(8,128)(2,1)}, bf16[128,2048]{1,0:T(8,128)(2,1)S(1)}, u32[]{:S(2)}, u32[]{:S(2)}) collective-permute-start(bf16[128,2048]{1,0:T(8,128)(2,1)} %bitcast.300), channel_id=1, source_target_pairs={{0,4},{4,0},{1,5},{5,1},{2,6},{6,2},{3,7},{7,3},{8,12},{12,8},{9,1... | collective-permute-start | bytes 1572872 | tf_op jit(solution)/shard_map/ppermute | solution.py:716
  391.5 34.0 %collective-permute-start.45 = (bf16[192,2048]{1,0:T(8,128)(2,1)S(1)}, bf16[192,2048]{1,0:T(8,128)(2,1)}, u32[]{:S(2)}, u32[]{:S(2)}) collective-permute-start(bf16[192,2048]{1,0:T(8,128)(2,1)S(1)} %get-tuple-element.543), channel_id=1, source_target_pairs={{0,2},{1,3},{2,0},{3,1},{4,6},{5,7},{6,4},{7,5},{8,10},{9,11},{10,... | collective-permute-start | bytes 2359304 | tf_op jit(solution)/shard_map/ppermute | solution.py:622
  450.2 25.5 %collective-permute-start.51 = (bf16[4,2,64,2048]{3,2,1,0:T(8,128)(2,1)}, bf16[4,2,64,2048]{3,2,1,0:T(8,128)(2,1)}, u32[]{:S(2)}, u32[]{:S(2)}) collective-permute-start(bf16[4,2,64,2048]{3,2,1,0:T(8,128)(2,1)} %get-tuple-element.434), channel_id=1, source_target_pairs={{0,1},{1,0},{2,3},{3,2},{4,5},{5,4},{6,7},{7,6},{8,9},{9,8},{10,11... | collective-permute-start | bytes 6291464 | tf_op jit(solution)/shard_map/ppermute | solution.py:622
  480.2 32.0 %collective-permute-start.57 = (bf16[4,1,64,2048]{3,2,1,0:T(8,128)(2,1)}, bf16[4,1,64,2048]{3,2,1,0:T(8,128)(2,1)}, u32[]{:S(2)}, u32[]{:S(2)}) collective-permute-start(bf16[4,1,64,2048]{3,2,1,0:T(8,128)(2,1)} %get-tuple-element.552), channel_id=1, source_target_pairs={{0,2},{1,3},{2,0},{3,1},{4,6},{5,7},{6,4},{7,5},{8,10},{9,11},{10,... | collective-permute-start | bytes 3145736 | tf_op jit(solution)/shard_map/ppermute | solution.py:622
  483.5 28.7 %collective-permute-start.56 = (bf16[192,2048]{1,0:T(8,128)(2,1)}, bf16[192,2048]{1,0:T(8,128)(2,1)}, u32[]{:S(2)}, u32[]{:S(2)}) collective-permute-start(bf16[192,2048]{1,0:T(8,128)(2,1)} %get-tuple-element.453), channel_id=1, source_target_pairs={{0,8},{8,0},{16,24},{24,16},{1,9},{9,1},{17,25},{25,17},{2,10},{10... | collective-permute-start | bytes 2359304 | tf_op jit(solution)/shard_map/ppermute | solution.py:622
  485.7 26.5 %collective-permute-start.58 = (bf16[192,2048]{1,0:T(8,128)(2,1)S(1)}, bf16[192,2048]{1,0:T(8,128)(2,1)S(1)}, u32[]{:S(2)}, u32[]{:S(2)}) collective-permute-start(bf16[192,2048]{1,0:T(8,128)(2,1)S(1)} %value_rows.1.refs_0_), channel_id=1, source_target_pairs={{0,4},{4,0},{1,5},{5,1},{2,6},{6,2},{3,7},{7,3},{8,12},{12,8},{9,1... | collective-permute-start | bytes 2359304 | tf_op jit(solution)/shard_map/ppermute | solution.py:716
  544.7 36.5 %collective-permute-start.68 = (bf16[4,2,64,2048]{3,2,1,0:T(8,128)(2,1)}, bf16[4,2,64,2048]{3,2,1,0:T(8,128)(2,1)}, u32[]{:S(2)}, u32[]{:S(2)}) collective-permute-start(bf16[4,2,64,2048]{3,2,1,0:T(8,128)(2,1)} %get-tuple-element.487), channel_id=1, source_target_pairs={{0,1},{1,0},{2,3},{3,2},{4,5},{5,4},{6,7},{7,6},{8,9},{9,8},{10,11... | collective-permute-start | bytes 6291464 | tf_op jit(solution)/shard_map/ppermute | solution.py:622
  548.4 32.8 %collective-permute-start.66 = (bf16[4,1,64,2048]{3,2,1,0:T(8,128)(2,1)S(1)}, bf16[4,1,64,2048]{3,2,1,0:T(8,128)(2,1)S(1)}, u32[]{:S(2)}, u32[]{:S(2)}) collective-permute-start(bf16[4,1,64,2048]{3,2,1,0:T(8,128)(2,1)S(1)} %get-tuple-element.550), channel_id=1, source_target_pairs={{0,2},{1,3},{2,0},{3,1},{4,6},{5,7},{6,4},{7,5},{8,10},{9,11},{10,... | collective-permute-start | bytes 3145736 | tf_op jit(solution)/shard_map/ppermute | solution.py:622
  552.9 28.3 %collective-permute-start.70 = (bf16[128,2048]{1,0:T(8,128)(2,1)S(1)}, bf16[128,2048]{1,0:T(8,128)(2,1)S(1)}, u32[]{:S(2)}, u32[]{:S(2)}) collective-permute-start(bf16[128,2048]{1,0:T(8,128)(2,1)S(1)} %bitcast.299), channel_id=1, source_target_pairs={{0,4},{4,0},{1,5},{5,1},{2,6},{6,2},{3,7},{7,3},{8,12},{12,8},{9,1... | collective-permute-start | bytes 1572872 | tf_op jit(solution)/shard_map/ppermute | solution.py:716
  553.8 27.4 %collective-permute-start.69 = (bf16[192,1024]{1,0:T(8,128)(2,1)S(1)}, bf16[192,1024]{1,0:T(8,128)(2,1)S(1)}, u32[]{:S(2)}, u32[]{:S(2)}) collective-permute-start(bf16[192,1024]{1,0:T(8,128)(2,1)S(1)} %copy-done.99), channel_id=1, source_target_pairs={{0,4},{4,0},{1,5},{5,1},{2,6},{6,2},{3,7},{7,3},{8,12},{12,8},{9,1... | collective-permute-start | bytes 1179656 | tf_op jit(solution)/shard_map/ppermute | solution.py:716
  580.6 26.4 %collective-permute-start.65 = (bf16[4,1,64,2048]{3,2,1,0:T(8,128)(2,1)}, bf16[4,1,64,2048]{3,2,1,0:T(8,128)(2,1)}, u32[]{:S(2)}, u32[]{:S(2)}) collective-permute-start(bf16[4,1,64,2048]{3,2,1,0:T(8,128)(2,1)} %get-tuple-element.548), channel_id=1, source_target_pairs={{0,2},{1,3},{2,0},{3,1},{4,6},{5,7},{6,4},{7,5},{8,10},{9,11},{10,... | collective-permute-start | bytes 3145736 | tf_op jit(solution)/shard_map/ppermute | solution.py:622
  582.1 24.9 %collective-permute-start.72 = (bf16[2,1,64,2048]{3,2,1,0:T(8,128)(2,1)}, bf16[2,1,64,2048]{3,2,1,0:T(8,128)(2,1)}, u32[]{:S(2)}, u32[]{:S(2)}) collective-permute-start(bf16[2,1,64,2048]{3,2,1,0:T(8,128)(2,1)} %fusion.29), channel_id=1, source_target_pairs={{0,8},{8,0},{16,24},{24,16},{1,9},{9,1},{17,25},{25,17},{2,10},{10... | collective-permute-start | bytes 1572872 | tf_op jit(solution)/shard_map/ppermute | solution.py:622
  589.0 46.8 %collective-permute-start.74 = (bf16[4,1,64,2048]{3,2,1,0:T(8,128)(2,1)}, bf16[4,1,64,2048]{3,2,1,0:T(8,128)(2,1)}, u32[]{:S(2)}, u32[]{:S(2)}) collective-permute-start(bf16[4,1,64,2048]{3,2,1,0:T(8,128)(2,1)} %get-tuple-element.546), channel_id=1, source_target_pairs={{0,2},{1,3},{2,0},{3,1},{4,6},{5,7},{6,4},{7,5},{8,10},{9,11},{10,... | collective-permute-start | bytes 3145736 | tf_op jit(solution)/shard_map/ppermute | solution.py:622
  (173 other events, 1970.6 us)
Sparse Core Ops, SparseCore 0:
  10.3 103.7 all-gather.1

commit v6 on v5

--- a/solution.py
+++ b/solution.py
@@ -917,7 +917,8 @@
         return [shift(values[r - 1], r) for r in others]
 
     first_got, near1 = z1(add_blocks((keep0, 1), (near0, 1), got21)), core(send1)
-    got31 = across(add_blocks((keep3, 1), (near3, 1)))
+    pair31, keep3, near3 = fence(add_blocks((keep3, 1), (near3, 1)), keep3, near3)
+    got31 = across(pair31)
     pair30 = add_blocks((keep3, 0), (near3, 0))
     *gate_low, gate_own = row_grads(me, planes, d_gate, slot_in, (1, 1))
     towards = jnp.arange(owners, dtype=jnp.int32)
@@ -961,7 +962,8 @@
         return add_blocks((out_keep, q, i), (out_near, q, i))
 
     sent = [shift(branch_low, r) for r in others]
-    out_got31, out_got30 = across(out_sum(3, 1)), across(out_sum(3, 0))
+    out31, out_keep, out_near = fence(out_sum(3, 1), out_keep, out_near)
+    out_got31, out_got30 = across(out31), across(out_sum(3, 0))
     *down_low, down_own = row_grads(me, planes, act_low, slot_cot, (1, 4, 3))
     out_got31, out_keep, out_near, down_own, down_0, down_1, down_2, branch_low, *sent = fence(
         out_got31, out_keep, out_near, down_own, *down_low, branch_low, *sent

time: 687 us -> 685 us (level)
    convert_element_type x25 -> x27, other arithmetic: 56.6 us -> 59.2 us  [plus(): return sum((v.astype(F32) for v in values)).astype(values[0].dtype)]
    unnamed x236 -> x240, local copies, waits for them, and re-layouts: 22.2 us -> 22.3 us
  transfers between devices with their start and end apart: 89 -> 89, of which waited for: 37 -> 36; matrix products, arithmetic and copies ran while one was open for 19% -> 20% of each run, Pallas kernels for 29% -> 29%
where the time goes in v6:
time: 685 us; the launch traced here: 681 us
  waiting for transfers between devices  202 us (29%)
  Pallas kernels  200 us (29%)
  other arithmetic  92.4 us (13%)
  starting transfers between devices  90.4 us (13%)
  local copies, waits for them, and re-layouts  41.5 us (6%)
  matrix products  37.7 us (6%)
  between operations  16.8 us (2%)
    ppermute x31, waiting for transfers between devices, shift(): lax.ppermute(value, 'context', [(i, (i + r) % planes) for i in range(plan...  124 us
    ppermute x55, waiting for transfers between devices, swap(): lax.ppermute(value, axis, [(i, i ^ bit) for i in range(lax.axis_size(axis...  77.3 us
    pallas_call x4, Pallas kernels, expert_quarter(): pl.pallas_call(expert_kernel, grid=(hidden // tile,), in_specs=[whole(tok...  67.1 us
    convert_element_type x27, other arithmetic, plus(): return sum((v.astype(F32) for v in values)).astype(values[0].dtype)  59.2 us
    ppermute x55, starting transfers between devices, swap(): lax.ppermute(value, axis, [(i, i ^ bit) for i in range(lax.axis_size(axis...  48.4 us
    pallas_call x3, Pallas kernels, row_grads(): pl.pallas_call(functools.partial(row_grads_kernel, cuts), grid_spec=pltpu...  39.8 us
    dot_general x20, matrix products, dot(): lax.dot_general(left, right, (dims, ((), ())), preferred_element_type=out)  37.7 us
    ppermute x31, starting transfers between devices, shift(): lax.ppermute(value, 'context', [(i, (i + r) % planes) for i in range(plan...  32.1 us
  transfers between devices with their start and end apart: 89, of which 36 were waited for; matrix products, arithmetic and copies ran while one was open for 20% of the time, Pallas kernels for 29%

profile of v6, /device:TPU:0, one launch (start us, length us, event | category | flops | bytes accessed | tf_op | source)
XLA Modules:
  0.0 680.7 jit_solution(3208897309928919923)
XLA Ops:
  14.8 8.6 %collective-permute-done = bf16[192,1024]{1,0:T(8,128)(2,1)S(1)} collective-permute-done((bf16[192,1024]{1,0:T(8,128)(2,1)S(1)}, bf16[192,1024]{1,0:T(8,128)(2,1)S(1)}, u32[]{:S(2)}, u32[]{:S(2)}) %collective-permute-start) | collective-permute-done | bytes 393248 | tf_op jit(solution)/shard_map/ppermute | solution.py:716
  32.5 6.2 all-to-all-start
  51.2 16.4 %collective-permute-done.4 = bf16[4,1024]{1,0:T(4,128)(2,1)S(1)} collective-permute-done((bf16[4,1024]{1,0:T(4,128)(2,1)S(1)}, bf16[4,1024]{1,0:T(4,128)(2,1)S(1)}, u32[]{:S(2)}, u32[]{:S(2)}) %collective-permute-start.4) | collective-permute-done | bytes 8224 | tf_op jit(solution)/shard_map/ppermute | solution.py:716
  80.1 17.8 %collective-permute-done.7 = bf16[64,2048]{1,0:T(8,128)(2,1)S(1)} collective-permute-done((bf16[64,2048]{1,0:T(8,128)(2,1)S(1)}, bf16[64,2048]{1,0:T(8,128)(2,1)S(1)}, u32[]{:S(2)}, u32[]{:S(2)}) %collective-permute-start.7) | collective-permute-done | bytes 262176 | tf_op jit(solution)/shard_map/ppermute | solution.py:716
  101.9 4.8 attend.1
  109.7 6.1 collective-permute-done.9
  123.4 16.1 %collective-permute-done.10 = bf16[192,2048]{1,0:T(8,128)(2,1)S(1)} collective-permute-done((bf16[192,2048]{1,0:T(8,128)(2,1)S(1)}, bf16[192,2048]{1,0:T(8,128)(2,1)S(1)}, u32[]{:S(2)}, u32[]{:S(2)}) %collective-permute-start.10) | collective-permute-done | bytes 786464 | tf_op jit(solution)/shard_map/ppermute | solution.py:716
  152.8 22.0 %gather_cot.1 = (bf16[1792,2048]{1,0:T(8,128)(2,1)}, f32[1792,1024]{1,0:T(8,128)}) custom-call(s32[16]{0:T(128)S(1)} %stack.98.source_ref, bf16[16,192,2048]{2,1,0:T(8,128)(2,1)} %bitcast.302, bf16[16,192,2048]{2,1,0:T(8,128)(2,1)} %bitcast.303, bf16[16,192,2048]{2,1,0:T(8,128)(2,1)} %bitcast.304, bf16[16,192,2048]{2,1,0:T(8,128)(2,1)} %bitcast.305, ...), custom_call_target="tpu_custom_call" | custom-call | tf_op jit(solution)/shard_map/gather_cot/pallas_call | solution.py:466
  178.0 16.6 %collective-permute-done.19.refs_2_ = bf16[192,2048]{1,0:T(8,128)(2,1)S(1)} collective-permute-done((bf16[192,2048]{1,0:T(8,128)(2,1)S(1)}, bf16[192,2048]{1,0:T(8,128)(2,1)S(1)}, u32[]{:S(2)}, u32[]{:S(2)}) %collective-permute-start.19) | collective-permute-done | bytes 786464 | tf_op jit(solution)/shard_map/ppermute | solution.py:622
  196.9 16.7 %expert.4 = (bf16[1792,2048]{1,0:T(8,128)(2,1)}, bf16[1792,1024]{1,0:T(8,128)(2,1)}, bf16[1792,1024]{1,0:T(8,128)(2,1)}, bf16[1792,1024]{1,0:T(8,128)(2,1)}, bf1...) custom-call(bf16[192,2048]{1,0:T(8,128)(2,1)S(1)} %multiply_convert_fusion.refs_0_, ...), custom_call_target="tpu_custom_call" | custom-call | tf_op jit(solution)/shard_map/expert/pallas_call | solution.py:365
  216.3 16.7 %expert.5 = (bf16[1792,2048]{1,0:T(8,128)(2,1)}, bf16[1792,1024]{1,0:T(8,128)(2,1)}, bf16[1792,1024]{1,0:T(8,128)(2,1)}, bf16[1792,1024]{1,0:T(8,128)(2,1)}, bf1...) custom-call(bf16[192,2048]{1,0:T(8,128)(2,1)S(1)} %collective-permut, ...), custom_call_target="tpu_custom_call", output_to_operand_aliasing={{0}: (10, {}), {1}: (11, {}), {2}: (12, {}), {3}: (13, {})} | custom-call | tf_op jit(solution)/shard_map/expert/pallas_call | solution.py:365
  240.8 16.9 %expert.6 = (bf16[1792,2048]{1,0:T(8,128)(2,1)}, bf16[1792,1024]{1,0:T(8,128)(2,1)}, bf16[1792,1024]{1,0:T(8,128)(2,1)}, bf16[1792,1024]{1,0:T(8,128)(2,1)}, bf1...) custom-call(bf16[192,2048]{1,0:T(8,128)(2,1)S(1)} %collective-permut, ...), custom_call_target="tpu_custom_call", output_to_operand_aliasing={{0}: (10, {}), {1}: (11, {}), {2}: (12, {}), {3}: (13, {})} | custom-call | tf_op jit(solution)/shard_map/expert/pallas_call | solution.py:365
  260.5 16.8 %expert.7 = (bf16[1792,2048]{1,0:T(8,128)(2,1)}, bf16[1792,1024]{1,0:T(8,128)(2,1)}, bf16[1792,1024]{1,0:T(8,128)(2,1)}, bf16[1792,1024]{1,0:T(8,128)(2,1)}, bf1...) custom-call(bf16[192,2048]{1,0:T(8,128)(2,1)S(1)} %collective-permut, ...), custom_call_target="tpu_custom_call", output_to_operand_aliasing={{0}: (10, {}), {1}: (11, {}), {2}: (12, {}), {3}: (13, {})} | custom-call | tf_op jit(solution)/shard_map/expert/pallas_call | solution.py:365
  289.9 13.5 %row_grads.3 = (bf16[1,256,2048]{2,1,0:T(8,128)(2,1)}, bf16[1,256,2048]{2,1,0:T(8,128)(2,1)S(1)}, f32[512,2048]{1,0:T(8,128)}) custom-call(s32[1]{0:T(128)} %bitcast.44.me_ref, bf16[1792,1024]{1,0:T(8,128)(2,1)S(1)} %copy-done.1, bf16[1792,2048]{1,0:T(8,128)(2,1)} %get-tuple-element.389.right_ref), custom_call_target="tpu_custom_call" | custom-call | tf_op jit(solution)/shard_map/row_grads/pallas_call | solution.py:519
  317.1 13.1 %row_grads.4 = (bf16[1,128,2048]{2,1,0:T(8,128)(2,1)S(1)}, bf16[1,256,2048]{2,1,0:T(8,128)(2,1)}, bf16[1,128,2048]{2,1,0:T(8,128)(2,1)S(1)}, f32[512,2048]{1,0:T(8,128)}) custom-call(s32[1]{0:T(128)} %bitcast.44.me_ref, bf16[1792,1024]{1,0:T(8,128)(2,1)S(1)} %copy-done.2, bf16[1792,2048]{1,0:T(8,128)(2,1)} %get-tuple-element.389.right_ref), custom_call_target="tpu_custom_call" | custom-call | tf_op jit(solution)/shard_map/row_grads/pallas_call | solution.py:519
  340.3 22.2 %expert_out.1 = (bf16[4,2,192,2048]{3,2,1,0:T(8,128)(2,1)}, bf16[4,2,192,2048]{3,2,1,0:T(8,128)(2,1)}) custom-call(bf16[16,112,192]{2,1,0:T(8,128)(2,1)S(1)} %fusion.pick_ref.refs_4_, bf16[1792,1024]{1,0:T(8,128)(2,1)S(1)} %copy-done, bf16[1024,2048]{1,0:T(8,128)(2,1)} %bitcast.290), custom_call_target="tpu_custom_call" | custom-call | tf_op jit(solution)/shard_map/expert_out/pallas_call | solution.py:430
  362.4 7.1 %collective-permute-done.41 = bf16[128,2048]{1,0:T(8,128)(2,1)S(1)} collective-permute-done((bf16[128,2048]{1,0:T(8,128)(2,1)}, bf16[128,2048]{1,0:T(8,128)(2,1)S(1)}, u32[]{:S(2)}, u32[]{:S(2)}) %collective-permute-start.41) | collective-permute-done | bytes 524320 | tf_op jit(solution)/shard_map/ppermute | solution.py:716
  374.8 4.9 norm_back.1
  379.8 5.5 collective-permute-done.42
  391.5 13.3 %row_grads.5 = (bf16[1,64,2048]{2,1,0:T(8,128)(2,1)S(1)}, bf16[1,256,2048]{2,1,0:T(8,128)(2,1)}, bf16[1,192,2048]{2,1,0:T(8,128)(2,1)S(1)}, f32[512,2048]{1,0:T(8,128)}) custom-call(s32[1]{0:T(128)} %bitcast.44.me_ref, bf16[1792,1024]{1,0:T(8,128)(2,1)S(1)} %copy-done, bf16[1792,2048]{1,0:T(8,128)(2,1)} %get-tuple-element.418.right_ref), custom_call_target="tpu_custom_call" | custom-call | tf_op jit(solution)/shard_map/row_grads/pallas_call | solution.py:519
  419.0 4.6 collective-permute-done.45
  429.1 11.4 %attend_back.1 = (f32[192,2048]{1,0:T(8,128)}, f32[192,2048]{1,0:T(8,128)}, f32[192,2048]{1,0:T(8,128)}, bf16[128,2048]{1,0:T(8,128)(2,1)S(1)}, bf16[128,2048]{1,0:T(8,128)(2,1)S(1)}) custom-call(s32[2]{0:T(128)S(1)} %pad_add_fusion.1.meta_ref, bf16[192,2048]{1,0:T(8,128)(2,1)S(1)} %copy-done.9, bf16[256,2048]{1,0:T(8,128)(2,1)S(1)} %copy-done.5, ...), custom_call_target="tpu_custom_call" | custom-call | tf_op jit(solution)/shard_map/attend_back/pallas_call | solution.py:280
  458.4 4.6 fusion.8
  466.0 7.7 %collective-permute-done.54 = bf16[96,2048]{1,0:T(8,128)(2,1)S(1)} collective-permute-done((bf16[96,2048]{1,0:T(8,128)(2,1)S(1)}, bf16[96,2048]{1,0:T(8,128)(2,1)S(1)}, u32[]{:S(2)}, u32[]{:S(2)}) %collective-permute-start.54) | collective-permute-done | bytes 393248 | tf_op jit(solution)/shard_map/ppermute | solution.py:716
  499.4 10.8 %collective-permute-done.59 = bf16[96,2048]{1,0:T(8,128)(2,1)} collective-permute-done((bf16[96,2048]{1,0:T(8,128)(2,1)}, bf16[96,2048]{1,0:T(8,128)(2,1)}, u32[]{:S(2)}, u32[]{:S(2)}) %collective-permute-start.59) | collective-permute-done | bytes 393248 | tf_op jit(solution)/shard_map/ppermute | solution.py:716
  522.3 4.8 weight_grads.5
  554.6 9.5 %collective-permute-done.67 = bf16[1,1,64,2048]{3,2,1,0:T(8,128)(2,1)S(1)} collective-permute-done((bf16[1,1,64,2048]{3,2,1,0:T(8,128)(2,1)S(1)}, bf16[1,1,64,2048]{3,2,1,0:T(8,128)(2,1)S(1)}, u32[]{:S(2)}, u32[]{:S(2)}) %collective-permute-start.67) | collective-permute-done | bytes 262176 | tf_op jit(solution)/shard_map/ppermute | solution.py:622
  568.6 10.0 %collective-permute-done.71 = bf16[64,2048]{1,0:T(8,128)(2,1)S(1)} collective-permute-done((bf16[64,2048]{1,0:T(8,128)(2,1)S(1)}, bf16[64,2048]{1,0:T(8,128)(2,1)S(1)}, u32[]{:S(2)}, u32[]{:S(2)}) %collective-permute-start.71) | collective-permute-done | bytes 262176 | tf_op jit(solution)/shard_map/ppermute | solution.py:716
  597.6 7.4 %collective-permute-done.65 = bf16[4,1,64,2048]{3,2,1,0:T(8,128)(2,1)} collective-permute-done((bf16[4,1,64,2048]{3,2,1,0:T(8,128)(2,1)}, bf16[4,1,64,2048]{3,2,1,0:T(8,128)(2,1)}, u32[]{:S(2)}, u32[]{:S(2)}) %collective-permute-start.65) | collective-permute-done | bytes 1048608 | tf_op jit(solution)/shard_map/ppermute | solution.py:622
  622.9 10.9 %collective-permute-done.77 = f32[4,256,20]{1,0,2:T(4,128)S(1)} collective-permute-done((f32[4,256,20]{1,0,2:T(4,128)S(1)}, f32[4,256,20]{1,0,2:T(4,128)S(1)}, u32[]{:S(2)}, u32[]{:S(2)}) %collective-permute-start.77) | collective-permute-done | bytes 81952 | tf_op jit(solution)/shard_map/ppermute | solution.py:716
  641.8 5.7 convert_add_fusion
  661.9 9.8 %collective-permute-done.85 = bf16[1,1,64,2048]{3,2,1,0:T(8,128)(2,1)S(1)} collective-permute-done((bf16[1,1,64,2048]{3,2,1,0:T(8,128)(2,1)S(1)}, bf16[1,1,64,2048]{3,2,1,0:T(8,128)(2,1)S(1)}, u32[]{:S(2)}, u32[]{:S(2)}) %collective-permute-start.85) | collective-permute-done | bytes 262176 | tf_op jit(solution)/shard_map/ppermute | solution.py:622
  (565 shorter events, 305.4 us)
Async XLA Ops:
  7.2 135.8 %all-gather.2.cloned.1.call-start = ((), (), s32[]{:S(2)}) async-start(), calls=%async_computation.2 | async-start | bytes 13369344 | tf_op jit(solution)/shard_map/all_gather | solution.py:768
  29.9 42.1 %collective-permute-start.2 = (bf16[192,2048]{1,0:T(8,128)(2,1)}, bf16[192,2048]{1,0:T(8,128)(2,1)S(1)}, u32[]{:S(2)}, u32[]{:S(2)}) collective-permute-start(bf16[192,2048]{1,0:T(8,128)(2,1)} %convolution_convert_fusion.3), channel_id=1, source_target_pairs={{0,4},{4,0},{1,5},{5,1},{2,6},{6,2},{3,7},{7,3},{8,12},{12,8},{9,1... | collective-permute-start | bytes 2359304 | tf_op jit(solution)/shard_map/ppermute | solution.py:716
  30.2 41.8 %collective-permute-start.3 = (bf16[192,2048]{1,0:T(8,128)(2,1)}, bf16[192,2048]{1,0:T(8,128)(2,1)}, u32[]{:S(2)}, u32[]{:S(2)}) collective-permute-start(bf16[192,2048]{1,0:T(8,128)(2,1)} %convolution_convert_fusion.2), channel_id=1, source_target_pairs={{0,4},{4,0},{1,5},{5,1},{2,6},{6,2},{3,7},{7,3},{8,12},{12,8},{9,1... | collective-permute-start | bytes 2359304 | tf_op jit(solution)/shard_map/ppermute | solution.py:716
  32.5 35.1 %all-to-all-start = ((f32[16,1,192]{2,1,0:T(1,128)}), f32[16,1,192]{2,1,0:T(1,128)S(1)}, u32[]{:S(2)}, u32[]{:S(2)}) async-start(f32[16,1,192]{2,1,0:T(1,128)} %all_to_all.16), calls=%async_computation | async-start | bytes 32768 | tf_op jit(solution)/shard_map/all_to_all | solution.py:800
  38.7 28.9 %collective-permute-start.4 = (bf16[4,1024]{1,0:T(4,128)(2,1)S(1)}, bf16[4,1024]{1,0:T(4,128)(2,1)S(1)}, u32[]{:S(2)}, u32[]{:S(2)}) collective-permute-start(bf16[4,1024]{1,0:T(4,128)(2,1)S(1)} %pad_maximum_fusion.9), channel_id=1, source_target_pairs={{0,4},{4,0},{1,5},{5,1},{2,6},{6,2},{3,7},{7,3},{8,12},{12,8},{9,1... | collective-permute-start | bytes 24584 | tf_op jit(solution)/shard_map/ppermute | solution.py:716
  40.2 30.8 %collective-permute-start.5 = (bf16[1024,16]{1,0:T(8,128)(2,1)}, bf16[1024,16]{1,0:T(8,128)(2,1)}, u32[]{:S(2)}, u32[]{:S(2)}) collective-permute-start(bf16[1024,16]{1,0:T(8,128)(2,1)} %copy.134), channel_id=1, source_target_pairs={{0,4},{4,0},{1,5},{5,1},{2,6},{6,2},{3,7},{7,3},{8,12},{12,8},{9,1... | collective-permute-start | bytes 98312 | tf_op jit(solution)/shard_map/ppermute | solution.py:716
  72.0 28.8 %collective-permute-start.6 = (bf16[192,2048]{1,0:T(8,128)(2,1)}, bf16[192,2048]{1,0:T(8,128)(2,1)S(1)}, u32[]{:S(2)}, u32[]{:S(2)}) collective-permute-start(bf16[192,2048]{1,0:T(8,128)(2,1)} %convolution_convert_fusion.1), channel_id=1, source_target_pairs={{0,4},{4,0},{1,5},{5,1},{2,6},{6,2},{3,7},{7,3},{8,12},{12,8},{9,1... | collective-permute-start | bytes 2359304 | tf_op jit(solution)/shard_map/ppermute | solution.py:716
  123.1 25.7 %collective-permute-start.16 = (bf16[192,1024]{1,0:T(8,128)(2,1)}, bf16[192,1024]{1,0:T(8,128)(2,1)}, u32[]{:S(2)}, u32[]{:S(2)}) collective-permute-start(bf16[192,1024]{1,0:T(8,128)(2,1)} %pad_maximum_fusion.5), channel_id=1, source_target_pairs={{0,4},{4,0},{1,5},{5,1},{2,6},{6,2},{3,7},{7,3},{8,12},{12,8},{9,1... | collective-permute-start | bytes 1179656 | tf_op jit(solution)/shard_map/ppermute | solution.py:716
  143.0 31.8 %collective-permute-start.11 = (bf16[192,2048]{1,0:T(8,128)(2,1)S(1)}, bf16[192,2048]{1,0:T(8,128)(2,1)S(1)}, u32[]{:S(2)}, u32[]{:S(2)}) collective-permute-start(bf16[192,2048]{1,0:T(8,128)(2,1)S(1)} %multiply_convert_fusion.refs_0_), channel_id=1, source_target_pairs={{0,8},{8,0},{16,24},{24,16},{1,9},{9,1},{17,25},{25,17},{2,10},{10... | collective-permute-start | bytes 2359304 | tf_op jit(solution)/shard_map/ppermute | solution.py:622
  144.1 30.8 %collective-permute-start.12 = (bf16[192,2048]{1,0:T(8,128)(2,1)S(1)}, bf16[192,2048]{1,0:T(8,128)(2,1)S(1)}, u32[]{:S(2)}, u32[]{:S(2)}) collective-permute-start(bf16[192,2048]{1,0:T(8,128)(2,1)S(1)} %multiply_convert_fusion.refs_0_), channel_id=1, source_target_pairs={{0,16},{8,24},{16,0},{24,8},{1,17},{9,25},{17,1},{25,9},{2,18},{10... | collective-permute-start | bytes 2359304 | tf_op jit(solution)/shard_map/ppermute | solution.py:622
  146.4 28.5 %collective-permute-start.13 = (bf16[192,2048]{1,0:T(8,128)(2,1)S(1)}, bf16[192,2048]{1,0:T(8,128)(2,1)S(1)}, u32[]{:S(2)}, u32[]{:S(2)}) collective-permute-start(bf16[192,2048]{1,0:T(8,128)(2,1)S(1)} %multiply_convert_fusion.refs_0_), channel_id=1, source_target_pairs={{0,2},{1,3},{2,0},{3,1},{4,6},{5,7},{6,4},{7,5},{8,10},{9,11},{10,... | collective-permute-start | bytes 2359304 | tf_op jit(solution)/shard_map/ppermute | solution.py:622
  147.8 27.0 %collective-permute-start.14 = (bf16[192,2048]{1,0:T(8,128)(2,1)S(1)}, bf16[192,2048]{1,0:T(8,128)(2,1)S(1)}, u32[]{:S(2)}, u32[]{:S(2)}) collective-permute-start(bf16[192,2048]{1,0:T(8,128)(2,1)S(1)} %multiply_convert_fusion.refs_0_), channel_id=1, source_target_pairs={{0,1},{1,0},{2,3},{3,2},{4,5},{5,4},{6,7},{7,6},{8,9},{9,8},{10,11... | collective-permute-start | bytes 2359304 | tf_op jit(solution)/shard_map/ppermute | solution.py:622
  148.8 26.0 %collective-permute-start.15 = (bf16[192,1024]{1,0:T(8,128)(2,1)S(1)}, bf16[192,1024]{1,0:T(8,128)(2,1)S(1)}, u32[]{:S(2)}, u32[]{:S(2)}) collective-permute-start(bf16[192,1024]{1,0:T(8,128)(2,1)S(1)} %pad_maximum_fusion.4), channel_id=1, source_target_pairs={{0,4},{4,0},{1,5},{5,1},{2,6},{6,2},{3,7},{7,3},{8,12},{12,8},{9,1... | collective-permute-start | bytes 1179656 | tf_op jit(solution)/shard_map/ppermute | solution.py:716
  176.5 37.2 %collective-permute-start.17 = (bf16[192,2048]{1,0:T(8,128)(2,1)S(1)}, bf16[192,2048]{1,0:T(8,128)(2,1)S(1)}, u32[]{:S(2)}, u32[]{:S(2)}) collective-permute-start(bf16[192,2048]{1,0:T(8,128)(2,1)S(1)} %collective-permute-done.12.refs_0_), channel_id=1, source_target_pairs={{0,2},{1,3},{2,0},{3,1},{4,6},{5,7},{6,4},{7,5},{8,10},{9,11},{10,... | collective-permute-start | bytes 2359304 | tf_op jit(solution)/shard_map/ppermute | solution.py:622
  196.4 36.7 %collective-permute-start.25 = (bf16[192,2048]{1,0:T(8,128)(2,1)S(1)}, bf16[192,2048]{1,0:T(8,128)(2,1)S(1)}, u32[]{:S(2)}, u32[]{:S(2)}) collective-permute-start(bf16[192,2048]{1,0:T(8,128)(2,1)S(1)} %collective-permute-done.19.refs_2_), channel_id=1, source_target_pairs={{0,2},{1,3},{2,0},{3,1},{4,6},{5,7},{6,4},{7,5},{8,10},{9,11},{10,... | collective-permute-start | bytes 2359304 | tf_op jit(solution)/shard_map/ppermute | solution.py:622
  279.0 27.2 %collective-permute-start.35 = (bf16[2,192,2048]{2,1,0:T(8,128)(2,1)}, bf16[2,192,2048]{2,1,0:T(8,128)(2,1)}, u32[]{:S(2)}, u32[]{:S(2)}) collective-permute-start(bf16[2,192,2048]{2,1,0:T(8,128)(2,1)} %get-tuple-element.370), channel_id=1, source_target_pairs={{0,1},{1,0},{2,3},{3,2},{4,5},{5,4},{6,7},{7,6},{8,9},{9,8},{10,11... | collective-permute-start | bytes 4718600 | tf_op jit(solution)/shard_map/ppermute | solution.py:622
  306.2 26.3 %collective-permute-start.38 = (bf16[256,2048]{1,0:T(8,128)(2,1)}, bf16[256,2048]{1,0:T(8,128)(2,1)}, u32[]{:S(2)}, u32[]{:S(2)}) collective-permute-start(bf16[256,2048]{1,0:T(8,128)(2,1)} %bitcast.51), channel_id=1, source_target_pairs={{0,4},{4,0},{1,5},{5,1},{2,6},{6,2},{3,7},{7,3},{8,12},{12,8},{9,1... | collective-permute-start | bytes 3145736 | tf_op jit(solution)/shard_map/ppermute | solution.py:716
  332.5 41.3 %collective-permute-start.40 = (bf16[256,2048]{1,0:T(8,128)(2,1)}, bf16[256,2048]{1,0:T(8,128)(2,1)S(1)}, u32[]{:S(2)}, u32[]{:S(2)}) collective-permute-start(bf16[256,2048]{1,0:T(8,128)(2,1)} %bitcast.297), channel_id=1, source_target_pairs={{0,4},{4,0},{1,5},{5,1},{2,6},{6,2},{3,7},{7,3},{8,12},{12,8},{9,1... | collective-permute-start | bytes 3145736 | tf_op jit(solution)/shard_map/ppermute | solution.py:716
  336.4 37.4 %collective-permute-start.39 = (bf16[192,2048]{1,0:T(8,128)(2,1)S(1)}, bf16[192,2048]{1,0:T(8,128)(2,1)S(1)}, u32[]{:S(2)}, u32[]{:S(2)}) collective-permute-start(bf16[192,2048]{1,0:T(8,128)(2,1)S(1)} %fusion.18), channel_id=1, source_target_pairs={{0,16},{8,24},{16,0},{24,8},{1,17},{9,25},{17,1},{25,9},{2,18},{10... | collective-permute-start | bytes 2359304 | tf_op jit(solution)/shard_map/ppermute | solution.py:622
  339.3 30.2 %collective-permute-start.41 = (bf16[128,2048]{1,0:T(8,128)(2,1)}, bf16[128,2048]{1,0:T(8,128)(2,1)S(1)}, u32[]{:S(2)}, u32[]{:S(2)}) collective-permute-start(bf16[128,2048]{1,0:T(8,128)(2,1)} %bitcast.300), channel_id=1, source_target_pairs={{0,4},{4,0},{1,5},{5,1},{2,6},{6,2},{3,7},{7,3},{8,12},{12,8},{9,1... | collective-permute-start | bytes 1572872 | tf_op jit(solution)/shard_map/ppermute | solution.py:716
  391.1 32.5 %collective-permute-start.45 = (bf16[192,2048]{1,0:T(8,128)(2,1)S(1)}, bf16[192,2048]{1,0:T(8,128)(2,1)}, u32[]{:S(2)}, u32[]{:S(2)}) collective-permute-start(bf16[192,2048]{1,0:T(8,128)(2,1)S(1)} %fusion.25), channel_id=1, source_target_pairs={{0,2},{1,3},{2,0},{3,1},{4,6},{5,7},{6,4},{7,5},{8,10},{9,11},{10,... | collective-permute-start | bytes 2359304 | tf_op jit(solution)/shard_map/ppermute | solution.py:622
  448.3 25.5 %collective-permute-start.51 = (bf16[4,2,64,2048]{3,2,1,0:T(8,128)(2,1)}, bf16[4,2,64,2048]{3,2,1,0:T(8,128)(2,1)}, u32[]{:S(2)}, u32[]{:S(2)}) collective-permute-start(bf16[4,2,64,2048]{3,2,1,0:T(8,128)(2,1)} %get-tuple-element.446), channel_id=1, source_target_pairs={{0,1},{1,0},{2,3},{3,2},{4,5},{5,4},{6,7},{7,6},{8,9},{9,8},{10,11... | collective-permute-start | bytes 6291464 | tf_op jit(solution)/shard_map/ppermute | solution.py:622
  478.2 32.0 %collective-permute-start.57 = (bf16[4,1,64,2048]{3,2,1,0:T(8,128)(2,1)}, bf16[4,1,64,2048]{3,2,1,0:T(8,128)(2,1)}, u32[]{:S(2)}, u32[]{:S(2)}) collective-permute-start(bf16[4,1,64,2048]{3,2,1,0:T(8,128)(2,1)} %get-tuple-element.562), channel_id=1, source_target_pairs={{0,2},{1,3},{2,0},{3,1},{4,6},{5,7},{6,4},{7,5},{8,10},{9,11},{10,... | collective-permute-start | bytes 3145736 | tf_op jit(solution)/shard_map/ppermute | solution.py:622
  481.3 28.9 %collective-permute-start.56 = (bf16[192,2048]{1,0:T(8,128)(2,1)}, bf16[192,2048]{1,0:T(8,128)(2,1)}, u32[]{:S(2)}, u32[]{:S(2)}) collective-permute-start(bf16[192,2048]{1,0:T(8,128)(2,1)} %get-tuple-element.465), channel_id=1, source_target_pairs={{0,8},{8,0},{16,24},{24,16},{1,9},{9,1},{17,25},{25,17},{2,10},{10... | collective-permute-start | bytes 2359304 | tf_op jit(solution)/shard_map/ppermute | solution.py:622
  483.6 26.5 %collective-permute-start.58 = (bf16[192,2048]{1,0:T(8,128)(2,1)S(1)}, bf16[192,2048]{1,0:T(8,128)(2,1)S(1)}, u32[]{:S(2)}, u32[]{:S(2)}) collective-permute-start(bf16[192,2048]{1,0:T(8,128)(2,1)S(1)} %value_rows.1.refs_0_), channel_id=1, source_target_pairs={{0,4},{4,0},{1,5},{5,1},{2,6},{6,2},{3,7},{7,3},{8,12},{12,8},{9,1... | collective-permute-start | bytes 2359304 | tf_op jit(solution)/shard_map/ppermute | solution.py:716
  485.2 25.0 %collective-permute-start.59 = (bf16[96,2048]{1,0:T(8,128)(2,1)}, bf16[96,2048]{1,0:T(8,128)(2,1)}, u32[]{:S(2)}, u32[]{:S(2)}) collective-permute-start(bf16[96,2048]{1,0:T(8,128)(2,1)} %slice.240), channel_id=1, source_target_pairs={{0,4},{4,0},{1,5},{5,1},{2,6},{6,2},{3,7},{7,3},{8,12},{12,8},{9,1... | collective-permute-start | bytes 1179656 | tf_op jit(solution)/shard_map/ppermute | solution.py:716
  542.7 36.5 %collective-permute-start.68 = (bf16[4,2,64,2048]{3,2,1,0:T(8,128)(2,1)}, bf16[4,2,64,2048]{3,2,1,0:T(8,128)(2,1)}, u32[]{:S(2)}, u32[]{:S(2)}) collective-permute-start(bf16[4,2,64,2048]{3,2,1,0:T(8,128)(2,1)} %get-tuple-element.499), channel_id=1, source_target_pairs={{0,1},{1,0},{2,3},{3,2},{4,5},{5,4},{6,7},{7,6},{8,9},{9,8},{10,11... | collective-permute-start | bytes 6291464 | tf_op jit(solution)/shard_map/ppermute | solution.py:622
  546.3 32.8 %collective-permute-start.66 = (bf16[4,1,64,2048]{3,2,1,0:T(8,128)(2,1)S(1)}, bf16[4,1,64,2048]{3,2,1,0:T(8,128)(2,1)S(1)}, u32[]{:S(2)}, u32[]{:S(2)}) collective-permute-start(bf16[4,1,64,2048]{3,2,1,0:T(8,128)(2,1)S(1)} %get-tuple-element.560), channel_id=1, source_target_pairs={{0,2},{1,3},{2,0},{3,1},{4,6},{5,7},{6,4},{7,5},{8,10},{9,11},{10,... | collective-permute-start | bytes 3145736 | tf_op jit(solution)/shard_map/ppermute | solution.py:622
  550.8 28.3 %collective-permute-start.70 = (bf16[128,2048]{1,0:T(8,128)(2,1)S(1)}, bf16[128,2048]{1,0:T(8,128)(2,1)S(1)}, u32[]{:S(2)}, u32[]{:S(2)}) collective-permute-start(bf16[128,2048]{1,0:T(8,128)(2,1)S(1)} %bitcast.299), channel_id=1, source_target_pairs={{0,4},{4,0},{1,5},{5,1},{2,6},{6,2},{3,7},{7,3},{8,12},{12,8},{9,1... | collective-permute-start | bytes 1572872 | tf_op jit(solution)/shard_map/ppermute | solution.py:716
  551.6 27.5 %collective-permute-start.69 = (bf16[192,1024]{1,0:T(8,128)(2,1)S(1)}, bf16[192,1024]{1,0:T(8,128)(2,1)S(1)}, u32[]{:S(2)}, u32[]{:S(2)}) collective-permute-start(bf16[192,1024]{1,0:T(8,128)(2,1)S(1)} %copy-done.101), channel_id=1, source_target_pairs={{0,4},{4,0},{1,5},{5,1},{2,6},{6,2},{3,7},{7,3},{8,12},{12,8},{9,1... | collective-permute-start | bytes 1179656 | tf_op jit(solution)/shard_map/ppermute | solution.py:716
  578.6 26.4 %collective-permute-start.65 = (bf16[4,1,64,2048]{3,2,1,0:T(8,128)(2,1)}, bf16[4,1,64,2048]{3,2,1,0:T(8,128)(2,1)}, u32[]{:S(2)}, u32[]{:S(2)}) collective-permute-start(bf16[4,1,64,2048]{3,2,1,0:T(8,128)(2,1)} %get-tuple-element.558), channel_id=1, source_target_pairs={{0,2},{1,3},{2,0},{3,1},{4,6},{5,7},{6,4},{7,5},{8,10},{9,11},{10,... | collective-permute-start | bytes 3145736 | tf_op jit(solution)/shard_map/ppermute | solution.py:622
  586.8 47.1 %collective-permute-start.74 = (bf16[4,1,64,2048]{3,2,1,0:T(8,128)(2,1)}, bf16[4,1,64,2048]{3,2,1,0:T(8,128)(2,1)}, u32[]{:S(2)}, u32[]{:S(2)}) collective-permute-start(bf16[4,1,64,2048]{3,2,1,0:T(8,128)(2,1)} %get-tuple-element.556), channel_id=1, source_target_pairs={{0,2},{1,3},{2,0},{3,1},{4,6},{5,7},{6,4},{7,5},{8,10},{9,11},{10,... | collective-permute-start | bytes 3145736 | tf_op jit(solution)/shard_map/ppermute | solution.py:622
  (175 other events, 1993.2 us)
Sparse Core Ops, SparseCore 0:
  10.3 103.7 all-gather.1
